TPU v7x, 512 devices: a whole 4x8x8 slice. The times are simulated.
512 devices in a mesh: group: 16 (over z, core), dev: 32 (over x, y).
Axes of the slice: x: 4, y: 8, z: 8, core: 2. Of those that a mesh axis runs over, the one named last changes fastest.
Arguments:
- points: float32 [8, 1048576], P(None, ('group', 'dev')), may hold values from -6 to 6
- order: int32 [512, 2048], P(('group', 'dev')), may hold values from 0 to 2047, each once within a row
- rhs: bfloat16 [1048576, 256], P(('group', 'dev')), may hold values from -6 to 6
- leaf_basis: bfloat16 [2048, 512, 128], P(('group', 'dev')), may hold values from -0.25 to 0.25
- local_transfer: float32 [512, 6, 128, 128], P(('group', 'dev')), may hold values from -0.4375 to 0.4375
- local_coupling: float32 [512, 3, 128, 128], P(('group', 'dev')), may hold values from -0.5 to 0.5
- cross_transfer: float32 [8, 512, 128, 128], P(None, ('group', 'dev')), as said below
- cross_coupling: float32 [9, 512, 128, 128], P(None, ('group', 'dev')), as said below
Outputs:
- product: bfloat16 [1048576, 256], P(('group', 'dev'))
Inputs may be any that keep to these rules, and one draw needn't show every extreme that they name: Each row of order holds every number 0 to 2047 once. cross_transfer[l, d] is the same matrix for all devices d of one level-l node. cross_coupling[l, d] is the same matrix for all devices d of one level-l pair.
All inputs are finite; a program needn't handle non-finite values.
Results may differ from a plain program's by a relative error of at most 0.0048.
Values sent between devices are 32-bit elements; how exact they have to be, the bound alone decides.
No kernel may reach another device: no remote copies, remote signals or barrier semaphores. Data moves between devices by JAX's collectives and lax.ppermute only.
A program may use at most 64 MiB of HBM per device.

v0:
```python
import jax
import jax.numpy as jnp
from jax import lax
from jax.sharding import PartitionSpec as P

kernel_rate = 0.125
ridge_shift = 1.0
highest = lax.Precision.HIGHEST


def partner(block, axis, stride):
    count = lax.axis_size(axis)
    route = []
    for low in range(count):
        high = low | 1 << stride
        if high != low and high < count:
            route += [(low, high), (high, low)]
    return lax.ppermute(block, axis, route)


def kernel_block(features):
    squares = jnp.sum(features * features, axis=0)
    inner = jnp.dot(features.T, features, precision=highest, preferred_element_type=jnp.float32)
    distance = squares[:, None] + squares[None, :] - 2.0 * inner
    return jnp.exp(-kernel_rate * distance).astype(jnp.bfloat16)


def lift_nodes(nodes, edges):
    return jnp.einsum("...iab,...iak->...ibk", edges, nodes, precision=highest)


def merge_pairs(lifted):
    return lifted[..., 0::2, :, :] + lifted[..., 1::2, :, :]


def pair_links(nodes, links):
    left_nodes = nodes[..., 0::2, :, :]
    right_nodes = nodes[..., 1::2, :, :]
    to_left = jnp.einsum("...iab,...ibk->...iak", links, right_nodes, precision=highest)
    to_right = jnp.einsum("...iab,...iak->...ibk", links, left_nodes, precision=highest)
    paired = jnp.stack([to_left, to_right], axis=-3)
    return paired.reshape(nodes.shape)


def descend(coupled, edges, parents):
    spread = jnp.repeat(parents, 2, axis=-3)
    return coupled + jnp.einsum("...iab,...ibk->...iak", edges, spread, precision=highest)


def apply_matrix(matrix, vectors):
    return jnp.dot(matrix, vectors, precision=highest, preferred_element_type=jnp.float32)


def apply_transposed(matrix, vectors):
    return jnp.dot(matrix.T, vectors, precision=highest, preferred_element_type=jnp.float32)


def body(
    points, order, rhs, leaf_basis, local_transfer, local_coupling, cross_transfer, cross_coupling
):
    per_device = order.shape[1]
    leaves_dev = leaf_basis.shape[0]
    leaf_size = leaf_basis.shape[1]
    ordering = order[0]
    tree_rhs = jnp.take(rhs, ordering, axis=0).reshape(leaves_dev, leaf_size, rhs.shape[1])
    tree_points = jnp.take(points, ordering, axis=1).reshape(points.shape[0], leaves_dev, leaf_size)
    tree_points = jnp.transpose(tree_points, (1, 0, 2))
    nodes = jnp.einsum("lpr,lpn->lrn", leaf_basis, tree_rhs, preferred_element_type=jnp.float32)[
        None
    ]
    local_coupled = []
    local_edges = []
    edge_start = 0
    link_start = 0
    count = leaves_dev
    while count > 1:
        edges = local_transfer[:, edge_start : edge_start + count]
        links = local_coupling[:, link_start : link_start + count // 2]
        local_coupled.append(pair_links(nodes, links))
        local_edges.append(edges)
        nodes = merge_pairs(lift_nodes(nodes, edges))
        edge_start += count
        link_start += count // 2
        count //= 2
    level_nodes = nodes[0, 0]
    kernel = jax.vmap(kernel_block)(tree_points)
    near = jnp.einsum("lpq,lqn->lpn", kernel, tree_rhs, preferred_element_type=jnp.float32)
    near = near + ridge_shift * tree_rhs.astype(jnp.float32)
    dev_bits = lax.axis_size("dev").bit_length() - 1
    group_bits = lax.axis_size("group").bit_length() - 1
    dev_index = lax.axis_index("dev")
    group_index = lax.axis_index("group")
    cross_coupled = []
    cross_edges = []
    for bit_index in range(dev_bits):
        is_left = dev_index // 2**bit_index % 2 == 0
        edge = cross_transfer[bit_index, 0]
        link = cross_coupling[bit_index, 0]
        lifted = apply_transposed(edge, level_nodes)
        side = jnp.where(is_left, apply_transposed(link, level_nodes), level_nodes)
        got_lift, got_side = partner((lifted, side), "dev", bit_index)
        cross_coupled.append(jnp.where(is_left, apply_matrix(link, got_side), got_side))
        cross_edges.append(edge)
        level_nodes = lifted + got_lift
    for bit_index in range(group_bits - 1):
        level = dev_bits + bit_index
        is_left = group_index // 2**bit_index % 2 == 0
        edge = cross_transfer[level, 0]
        link = cross_coupling[level, 0]
        lifted = apply_transposed(edge, level_nodes)
        side = jnp.where(is_left, apply_transposed(link, level_nodes), level_nodes)
        got_lift, got_side = partner((lifted, side), "group", bit_index)
        cross_coupled.append(jnp.where(is_left, apply_matrix(link, got_side), got_side))
        cross_edges.append(edge)
        level_nodes = lifted + got_lift
    top_bit = group_bits - 1
    top_left = group_index // 2**top_bit % 2 == 0
    top_link = cross_coupling[dev_bits + top_bit, 0]
    top_side = jnp.where(top_left, apply_transposed(top_link, level_nodes), level_nodes)
    got_top = partner(top_side, "group", top_bit)
    falling = jnp.where(top_left, apply_matrix(top_link, got_top), got_top)
    for bit_index in range(group_bits - 2, -1, -1):
        level = dev_bits + bit_index
        falling = cross_coupled[level] + apply_matrix(cross_edges[level], falling)
    for bit_index in range(dev_bits - 1, -1, -1):
        falling = cross_coupled[bit_index] + apply_matrix(cross_edges[bit_index], falling)
    falling = falling[None, None]
    for depth in range(len(local_coupled) - 1, -1, -1):
        falling = descend(local_coupled[depth], local_edges[depth], falling)
    far = jnp.einsum(
        "lpr,lrn->lpn",
        leaf_basis,
        falling[0].astype(jnp.bfloat16),
        preferred_element_type=jnp.float32,
    )
    tree_out = (near + far).astype(jnp.bfloat16).reshape(per_device, rhs.shape[1])
    inverse = (
        jnp.zeros((per_device,), jnp.int32)
        .at[ordering]
        .set(jnp.arange(per_device, dtype=jnp.int32))
    )
    return jnp.take(tree_out, inverse, axis=0)


def solution(mesh):
    placed = (
        P(None, ("group", "dev")),
        P(("group", "dev"), None),
        P(("group", "dev"), None),
        P(("group", "dev"), None, None),
        P(("group", "dev"), None, None, None),
        P(("group", "dev"), None, None, None),
        P(None, ("group", "dev"), None, None),
        P(None, ("group", "dev"), None, None),
    )
    return jax.shard_map(
        body, mesh=mesh, in_specs=placed, out_specs=P(("group", "dev"), None), check_vma=False
    )
```

profile of v0, /device:TPU:1, one launch (start us, length us, event | category | flops | bytes accessed | tf_op | source)
XLA Modules:
  0.0 185.8 jit_solution(13880331588320730974)
XLA Ops:
  1.5 7.5 %gather_fusion.1 = bf16[2048,256]{1,0:T(8,128)(2,1)S(1)} fusion(bf16[2048,256]{1,0:T(8,128)(2,1)S(1)} %copy-done, s32[2048]{0:T(1024)S(1)} %fusion.144), kind=kCustom, calls=%fused_computation.clone | custom fusion | bytes 2105344 | tf_op jit(solution)/shard_map/jit(_take)/gather | solution.py:65
  14.1 4.0 %collective-permute-start.1 = (f32[128,256]{0,1:T(8,128)}, f32[128,256]{0,1:T(8,128)}, u32[]{:S(2)}, u32[]{:S(2)}) collective-permute-start(f32[128,256]{0,1:T(8,128)} %convolution_bitcast_fusion.37), channel_id=1, source_target_pairs={{0,1},{1,0},{2,3},{3,2},{4,5},{5,4},{6,7},{7,6},{8,9},{9,8},{10,11... | collective-permute-start | bytes 393224 | tf_op jit(solution)/shard_map/ppermute | solution.py:18
  18.1 2.0 %fusion.21 = f32[128,256]{0,1:T(8,128)} fusion(pred[]{:T(512)S(6)} %eq.37, f32[9,1,128,128]{3,2,1,0:T(8,128)S(1)} %copy-done.2, f32[1,2,128,256]{2,3,1,0:T(8,128)} %copy-done.6), kind=kOutput, calls=%fused_computation.67 | convolution fusion | flops 50429952 | bytes 720897 | tf_op jit(solution)/shard_map/dot_general | solution.py:55
  20.1 1.9 %collective-permute-start = (f32[128,256]{0,1:T(8,128)}, f32[128,256]{0,1:T(8,128)}, u32[]{:S(2)}, u32[]{:S(2)}) collective-permute-start(f32[128,256]{0,1:T(8,128)} %fusion.21), channel_id=1, source_target_pairs={{0,1},{1,0},{2,3},{3,2},{4,5},{5,4},{6,7},{7,6},{8,9},{9,8},{10,11... | collective-permute-start | bytes 393224 | tf_op jit(solution)/shard_map/ppermute | solution.py:18
  23.3 8.2 %scatter_custom_fusion = s32[2048]{0:T(1024)S(1)} fusion(s32[2048]{0:T(1024)} %bitcast.350, s32[2048]{0:T(1024)} %iota.3, s32[]{:T(128)} %constant.150.clone.1), kind=kCustom, calls=%fused_computation.209 | custom fusion | bytes 8704 | tf_op jit(solution)/shard_map/scatter | solution.py:140
  35.1 9.5 %gather_fusion = f32[2048,8]{1,0:T(8,128)} fusion(f32[8,2048]{0,1:T(8,128)} %copy.13, s32[2048]{0:T(1024)} %broadcast_clamp_fusion), kind=kCustom, calls=%fused_computation.2 | custom fusion | bytes 139264 | tf_op jit(solution)/shard_map/jit(_take)/gather | solution.py:66
  46.5 6.0 %exponential_convert_fusion = bf16[4,512,512]{2,1,0:T(8,128)(2,1)S(1)} fusion(f32[4,512]{1,0:T(4,128)S(1)} %fusion.32, f32[8,4,512]{0,2,1:T(8,128)} %bitcast.346, pred[4,512]{1,0:T(4,128)(4,1)S(1)} %compare_and_fusion.2), kind=kOutput, calls=%fused_computation.4 | convolution fusion | flops 105938944 | bytes 2172928 | tf_op jit(solution)/shard_map/vmap()/dot_general | solution.py:23
  52.4 2.0 %fusion.149 = f32[4,512,256]{2,1,0:T(8,128)} fusion(bf16[4,512,512]{2,1,0:T(8,128)(2,1)S(1)} %exponential_convert_fusion, bf16[4,512,256]{2,1,0:T(8,128)(2,1)S(1)} %bitcast.339), kind=kOutput, calls=%fused_computation.212 | convolution fusion | flops 536870912 | bytes 5242880 | tf_op jit(solution)/shard_map/lpq,lqn->lpn/dot_general | solution.py:87
  56.1 1.9 %convolution_bitcast_fusion.34 = f32[128,256]{0,1:T(8,128)} fusion(f32[8,1,128,128]{3,2,1,0:T(8,128)} %param.16, f32[128,256]{0,1:T(8,128)} %convolution_bitcast_fusion.37, f32[128,256]{0,1:T(8,128)} %collective-permute-done.1), kind=kOutput, calls=%fused_computation.58 | convolution fusion | flops 50364416 | bytes 458752 | tf_op jit(solution)/shard_map/dot_general | solution.py:55
  58.0 4.4 %collective-permute-start.3 = (f32[128,256]{0,1:T(8,128)}, f32[128,256]{0,1:T(8,128)}, u32[]{:S(2)}, u32[]{:S(2)}) collective-permute-start(f32[128,256]{0,1:T(8,128)} %convolution_bitcast_fusion.34), channel_id=1, source_target_pairs={{0,2},{2,0},{1,3},{3,1},{4,6},{6,4},{5,7},{7,5},{8,10},{10,8},{9,1... | collective-permute-start | bytes 393224 | tf_op jit(solution)/shard_map/ppermute | solution.py:18
  63.2 2.0 %copy.15 = f32[1,2,2,128,256]{4,3,2,1,0:T(8,128)} copy(f32[1,2,2,128,256]{3,4,1,2,0:T(8,128)} %pad_maximum_fusion) | data formatting | bytes 1048576 | tf_op jit(solution)/shard_map/stack | solution.py:41
  67.6 10.5 %collective-permute-start.5 = (f32[128,256]{0,1:T(8,128)S(1)}, f32[128,256]{0,1:T(8,128)S(1)}, u32[]{:S(2)}, u32[]{:S(2)}) collective-permute-start(f32[128,256]{0,1:T(8,128)S(1)} %convolution_bitcast_fusion.31), channel_id=1, source_target_pairs={{0,4},{4,0},{1,5},{5,1},{2,6},{6,2},{3,7},{7,3},{8,12},{12,8},{9,1... | collective-permute-start | bytes 393224 | tf_op jit(solution)/shard_map/ppermute | solution.py:18
  79.5 1.9 %collective-permute-start.2 = (f32[128,256]{0,1:T(8,128)S(1)}, f32[128,256]{0,1:T(8,128)S(1)}, u32[]{:S(2)}, u32[]{:S(2)}) collective-permute-start(f32[128,256]{0,1:T(8,128)S(1)} %fusion.19), channel_id=1, source_target_pairs={{0,2},{2,0},{1,3},{3,1},{4,6},{6,4},{5,7},{7,5},{8,10},{10,8},{9,1... | collective-permute-start | bytes 393224 | tf_op jit(solution)/shard_map/ppermute | solution.py:18
  81.7 3.1 %collective-permute-start.7 = (f32[128,256]{0,1:T(8,128)S(1)}, f32[128,256]{0,1:T(8,128)S(1)}, u32[]{:S(2)}, u32[]{:S(2)}) collective-permute-start(f32[128,256]{0,1:T(8,128)S(1)} %convolution_bitcast_fusion.28), channel_id=1, source_target_pairs={{0,8},{8,0},{1,9},{9,1},{2,10},{10,2},{3,11},{11,3},{4,12},{12,4},... | collective-permute-start | bytes 393224 | tf_op jit(solution)/shard_map/ppermute | solution.py:18
  86.2 6.7 %collective-permute-start.4 = (f32[128,256]{0,1:T(8,128)S(1)}, f32[128,256]{0,1:T(8,128)S(1)}, u32[]{:S(2)}, u32[]{:S(2)}) collective-permute-start(f32[128,256]{0,1:T(8,128)S(1)} %fusion.17), channel_id=1, source_target_pairs={{0,4},{4,0},{1,5},{5,1},{2,6},{6,2},{3,7},{7,3},{8,12},{12,8},{9,1... | collective-permute-start | bytes 393224 | tf_op jit(solution)/shard_map/ppermute | solution.py:18
  93.2 4.3 %collective-permute-start.9 = (f32[128,256]{0,1:T(8,128)S(1)}, f32[128,256]{0,1:T(8,128)S(1)}, u32[]{:S(2)}, u32[]{:S(2)}) collective-permute-start(f32[128,256]{0,1:T(8,128)S(1)} %convolution_bitcast_fusion.25), channel_id=1, source_target_pairs={{0,16},{16,0},{1,17},{17,1},{2,18},{18,2},{3,19},{19,3},{4,20},{20... | collective-permute-start | bytes 393224 | tf_op jit(solution)/shard_map/ppermute | solution.py:18
  97.8 1.9 %collective-permute-start.6 = (f32[128,256]{0,1:T(8,128)S(1)}, f32[128,256]{0,1:T(8,128)S(1)}, u32[]{:S(2)}, u32[]{:S(2)}) collective-permute-start(f32[128,256]{0,1:T(8,128)S(1)} %fusion.15), channel_id=1, source_target_pairs={{0,8},{8,0},{1,9},{9,1},{2,10},{10,2},{3,11},{11,3},{4,12},{12,4},... | collective-permute-start | bytes 393224 | tf_op jit(solution)/shard_map/ppermute | solution.py:18
  100.9 6.8 %collective-permute-start.11 = (f32[128,256]{0,1:T(8,128)S(1)}, f32[128,256]{0,1:T(8,128)S(1)}, u32[]{:S(2)}, u32[]{:S(2)}) collective-permute-start(f32[128,256]{0,1:T(8,128)S(1)} %convolution_bitcast_fusion.22), channel_id=1, source_target_pairs={{0,32},{32,0},{64,96},{96,64},{128,160},{160,128},{192,224},{224,1... | collective-permute-start | bytes 393224 | tf_op jit(solution)/shard_map/ppermute | solution.py:18
  108.9 3.2 %collective-permute-start.13 = (f32[128,256]{0,1:T(8,128)S(1)}, f32[128,256]{0,1:T(8,128)S(1)}, u32[]{:S(2)}, u32[]{:S(2)}) collective-permute-start(f32[128,256]{0,1:T(8,128)S(1)} %convolution_bitcast_fusion.19), channel_id=1, source_target_pairs={{0,64},{64,0},{32,96},{96,32},{128,192},{192,128},{160,224},{224,1... | collective-permute-start | bytes 393224 | tf_op jit(solution)/shard_map/ppermute | solution.py:18
  112.4 3.2 %collective-permute-done.13 = f32[128,256]{0,1:T(8,128)S(1)} collective-permute-done((f32[128,256]{0,1:T(8,128)S(1)}, f32[128,256]{0,1:T(8,128)S(1)}, u32[]{:S(2)}, u32[]{:S(2)}) %collective-permute-start.13) | collective-permute-done | bytes 131104 | tf_op jit(solution)/shard_map/ppermute | solution.py:18
  115.8 5.9 %collective-permute-start.15 = (f32[128,256]{0,1:T(8,128)S(1)}, f32[128,256]{0,1:T(8,128)S(1)}, u32[]{:S(2)}, u32[]{:S(2)}) collective-permute-start(f32[128,256]{0,1:T(8,128)S(1)} %convolution_bitcast_fusion.16), channel_id=1, source_target_pairs={{0,128},{128,0},{32,160},{160,32},{64,192},{192,64},{96,224},{224,... | collective-permute-start | bytes 393224 | tf_op jit(solution)/shard_map/ppermute | solution.py:18
  122.0 5.6 %collective-permute-done.15 = f32[128,256]{0,1:T(8,128)S(1)} collective-permute-done((f32[128,256]{0,1:T(8,128)S(1)}, f32[128,256]{0,1:T(8,128)S(1)}, u32[]{:S(2)}, u32[]{:S(2)}) %collective-permute-start.15) | collective-permute-done | bytes 131104 | tf_op jit(solution)/shard_map/ppermute | solution.py:18
  127.9 8.0 %collective-permute-start.16 = (f32[128,256]{0,1:T(8,128)S(1)}, f32[128,256]{0,1:T(8,128)S(1)}, u32[]{:S(2)}, u32[]{:S(2)}) collective-permute-start(f32[128,256]{0,1:T(8,128)S(1)} %fusion.5), channel_id=1, source_target_pairs={{0,256},{256,0},{32,288},{288,32},{64,320},{320,64},{96,352},{352,... | collective-permute-start | bytes 393224 | tf_op jit(solution)/shard_map/ppermute | solution.py:18
  136.2 2.2 %collective-permute-done.16 = f32[128,256]{0,1:T(8,128)S(1)} collective-permute-done((f32[128,256]{0,1:T(8,128)S(1)}, f32[128,256]{0,1:T(8,128)S(1)}, u32[]{:S(2)}, u32[]{:S(2)}) %collective-permute-start.16) | collective-permute-done | bytes 131104 | tf_op jit(solution)/shard_map/ppermute | solution.py:18
  138.3 1.9 %collective-permute-start.14 = (f32[128,256]{0,1:T(8,128)S(1)}, f32[128,256]{0,1:T(8,128)S(1)}, u32[]{:S(2)}, u32[]{:S(2)}) collective-permute-start(f32[128,256]{0,1:T(8,128)S(1)} %fusion.7), channel_id=1, source_target_pairs={{0,128},{128,0},{32,160},{160,32},{64,192},{192,64},{96,224},{224,... | collective-permute-start | bytes 393224 | tf_op jit(solution)/shard_map/ppermute | solution.py:18
  140.8 4.1 %collective-permute-done.14 = f32[128,256]{0,1:T(8,128)S(1)} collective-permute-done((f32[128,256]{0,1:T(8,128)S(1)}, f32[128,256]{0,1:T(8,128)S(1)}, u32[]{:S(2)}, u32[]{:S(2)}) %collective-permute-start.14) | collective-permute-done | bytes 131104 | tf_op jit(solution)/shard_map/ppermute | solution.py:18
  144.9 5.4 %collective-permute-start.12 = (f32[128,256]{0,1:T(8,128)S(1)}, f32[128,256]{0,1:T(8,128)S(1)}, u32[]{:S(2)}, u32[]{:S(2)}) collective-permute-start(f32[128,256]{0,1:T(8,128)S(1)} %fusion.9), channel_id=1, source_target_pairs={{0,64},{64,0},{32,96},{96,32},{128,192},{192,128},{160,224},{224,1... | collective-permute-start | bytes 393224 | tf_op jit(solution)/shard_map/ppermute | solution.py:18
  152.7 6.7 %collective-permute-start.10 = (f32[128,256]{0,1:T(8,128)S(1)}, f32[128,256]{0,1:T(8,128)S(1)}, u32[]{:S(2)}, u32[]{:S(2)}) collective-permute-start(f32[128,256]{0,1:T(8,128)S(1)} %fusion.11), channel_id=1, source_target_pairs={{0,32},{32,0},{64,96},{96,64},{128,160},{160,128},{192,224},{224,1... | collective-permute-start | bytes 393224 | tf_op jit(solution)/shard_map/ppermute | solution.py:18
  160.4 4.3 %collective-permute-start.8 = (f32[128,256]{0,1:T(8,128)S(1)}, f32[128,256]{0,1:T(8,128)S(1)}, u32[]{:S(2)}, u32[]{:S(2)}) collective-permute-start(f32[128,256]{0,1:T(8,128)S(1)} %fusion.13), channel_id=1, source_target_pairs={{0,16},{16,0},{1,17},{17,1},{2,18},{18,2},{3,19},{19,3},{4,20},{20... | collective-permute-start | bytes 393224 | tf_op jit(solution)/shard_map/ppermute | solution.py:18
  165.3 3.2 %collective-permute-done.8 = f32[128,256]{0,1:T(8,128)S(1)} collective-permute-done((f32[128,256]{0,1:T(8,128)S(1)}, f32[128,256]{0,1:T(8,128)S(1)}, u32[]{:S(2)}, u32[]{:S(2)}) %collective-permute-start.8) | collective-permute-done | bytes 131104 | tf_op jit(solution)/shard_map/ppermute | solution.py:18
  173.6 1.9 %fusion.2 = bf16[4,128,256]{2,1,0:T(8,128)(2,1)S(1)} fusion(f32[4,128,256]{2,1,0:T(8,128)} %bitcast.343, f32[4,128,256]{2,1,0:T(8,128)S(1)} %bitcast.344, f32[1,6,128,128]{3,2,1,0:T(8,128)} %param.14), kind=kOutput, calls=%fused_computation.10 | convolution fusion | flops 201588736 | bytes 1572864 | tf_op jit(solution)/shard_map/...iab,...ibk->...iak/dot_general | solution.py:47
  177.0 7.5 %gather_fusion.2 = bf16[2048,256]{1,0:T(8,128)(2,1)S(1)} fusion(bf16[2048,256]{1,0:T(8,128)(2,1)S(1)} %bitcast.337, s32[2048]{0:T(1024)S(1)} %copy-done.12), kind=kCustom, calls=%fused_computation.1.clone | custom fusion | bytes 2105344 | tf_op jit(solution)/shard_map/jit(_take)/gather | solution.py:142
  (100 shorter events, 37.3 us)
Async XLA Ops:
  0.0 1.5 copy-start
  9.0 1.0 copy-start.4
  9.0 1.6 copy-start.5
  10.0 8.1 %copy-start.2 = (f32[9,1,128,128]{3,2,1,0:T(8,128)S(1)}, f32[9,1,128,128]{3,2,1,0:T(8,128)}, u32[]{:S(2)}) copy-start(f32[9,1,128,128]{3,2,1,0:T(8,128)} %param.17) | copy-start | bytes 1769476
  10.6 11.5 %copy-start.9 = (s32[1,2048]{1,0:T(1,128)S(1)}, s32[1,2048]{1,0:T(1,128)}, u32[]{:S(2)}) copy-start(s32[1,2048]{1,0:T(1,128)} %param.11) | copy-start | bytes 24580
  10.6 22.1 %copy-start.10 = (f32[8,2048]{1,0:T(8,128)S(1)}, f32[8,2048]{1,0:T(8,128)}, u32[]{:S(2)}) copy-start(f32[8,2048]{1,0:T(8,128)} %param.10) | copy-start | bytes 196612
  11.6 0.7 copy-start.6
  14.1 42.0 %collective-permute-start.1 = (f32[128,256]{0,1:T(8,128)}, f32[128,256]{0,1:T(8,128)}, u32[]{:S(2)}, u32[]{:S(2)}) collective-permute-start(f32[128,256]{0,1:T(8,128)} %convolution_bitcast_fusion.37), channel_id=1, source_target_pairs={{0,1},{1,0},{2,3},{3,2},{4,5},{5,4},{6,7},{7,6},{8,9},{9,8},{10,11... | collective-permute-start | bytes 393224 | tf_op jit(solution)/shard_map/ppermute | solution.py:18
  20.1 150.7 %collective-permute-start = (f32[128,256]{0,1:T(8,128)}, f32[128,256]{0,1:T(8,128)}, u32[]{:S(2)}, u32[]{:S(2)}) collective-permute-start(f32[128,256]{0,1:T(8,128)} %fusion.21), channel_id=1, source_target_pairs={{0,1},{1,0},{2,3},{3,2},{4,5},{5,4},{6,7},{7,6},{8,9},{9,8},{10,11... | collective-permute-start | bytes 393224 | tf_op jit(solution)/shard_map/ppermute | solution.py:18
  22.1 0.6 copy-start.11
  52.4 2.0 %copy-start.7 = (f32[1,3,128,128]{3,2,1,0:T(8,128)S(1)}, f32[1,3,128,128]{3,2,1,0:T(8,128)}, u32[]{:S(2)}) copy-start(f32[1,3,128,128]{3,2,1,0:T(8,128)} %param.15) | copy-start | bytes 589828
  55.3 11.1 %copy-start.3 = (f32[8,1,128,128]{3,2,1,0:T(8,128)S(1)}, f32[8,1,128,128]{3,2,1,0:T(8,128)}, u32[]{:S(2)}) copy-start(f32[8,1,128,128]{3,2,1,0:T(8,128)} %param.16) | copy-start | bytes 1572868
  58.0 8.4 %collective-permute-start.3 = (f32[128,256]{0,1:T(8,128)}, f32[128,256]{0,1:T(8,128)}, u32[]{:S(2)}, u32[]{:S(2)}) collective-permute-start(f32[128,256]{0,1:T(8,128)} %convolution_bitcast_fusion.34), channel_id=1, source_target_pairs={{0,2},{2,0},{1,3},{3,1},{4,6},{6,4},{5,7},{7,5},{8,10},{10,8},{9,1... | collective-permute-start | bytes 393224 | tf_op jit(solution)/shard_map/ppermute | solution.py:18
  67.6 13.8 %collective-permute-start.5 = (f32[128,256]{0,1:T(8,128)S(1)}, f32[128,256]{0,1:T(8,128)S(1)}, u32[]{:S(2)}, u32[]{:S(2)}) collective-permute-start(f32[128,256]{0,1:T(8,128)S(1)} %convolution_bitcast_fusion.31), channel_id=1, source_target_pairs={{0,4},{4,0},{1,5},{5,1},{2,6},{6,2},{3,7},{7,3},{8,12},{12,8},{9,1... | collective-permute-start | bytes 393224 | tf_op jit(solution)/shard_map/ppermute | solution.py:18
  79.5 90.8 %collective-permute-start.2 = (f32[128,256]{0,1:T(8,128)S(1)}, f32[128,256]{0,1:T(8,128)S(1)}, u32[]{:S(2)}, u32[]{:S(2)}) collective-permute-start(f32[128,256]{0,1:T(8,128)S(1)} %fusion.19), channel_id=1, source_target_pairs={{0,2},{2,0},{1,3},{3,1},{4,6},{6,4},{5,7},{7,5},{8,10},{10,8},{9,1... | collective-permute-start | bytes 393224 | tf_op jit(solution)/shard_map/ppermute | solution.py:18
  81.7 11.2 %collective-permute-start.7 = (f32[128,256]{0,1:T(8,128)S(1)}, f32[128,256]{0,1:T(8,128)S(1)}, u32[]{:S(2)}, u32[]{:S(2)}) collective-permute-start(f32[128,256]{0,1:T(8,128)S(1)} %convolution_bitcast_fusion.28), channel_id=1, source_target_pairs={{0,8},{8,0},{1,9},{9,1},{2,10},{10,2},{3,11},{11,3},{4,12},{12,4},... | collective-permute-start | bytes 393224 | tf_op jit(solution)/shard_map/ppermute | solution.py:18
  86.2 83.5 %collective-permute-start.4 = (f32[128,256]{0,1:T(8,128)S(1)}, f32[128,256]{0,1:T(8,128)S(1)}, u32[]{:S(2)}, u32[]{:S(2)}) collective-permute-start(f32[128,256]{0,1:T(8,128)S(1)} %fusion.17), channel_id=1, source_target_pairs={{0,4},{4,0},{1,5},{5,1},{2,6},{6,2},{3,7},{7,3},{8,12},{12,8},{9,1... | collective-permute-start | bytes 393224 | tf_op jit(solution)/shard_map/ppermute | solution.py:18
  93.2 7.5 %collective-permute-start.9 = (f32[128,256]{0,1:T(8,128)S(1)}, f32[128,256]{0,1:T(8,128)S(1)}, u32[]{:S(2)}, u32[]{:S(2)}) collective-permute-start(f32[128,256]{0,1:T(8,128)S(1)} %convolution_bitcast_fusion.25), channel_id=1, source_target_pairs={{0,16},{16,0},{1,17},{17,1},{2,18},{18,2},{3,19},{19,3},{4,20},{20... | collective-permute-start | bytes 393224 | tf_op jit(solution)/shard_map/ppermute | solution.py:18
  97.8 71.3 %collective-permute-start.6 = (f32[128,256]{0,1:T(8,128)S(1)}, f32[128,256]{0,1:T(8,128)S(1)}, u32[]{:S(2)}, u32[]{:S(2)}) collective-permute-start(f32[128,256]{0,1:T(8,128)S(1)} %fusion.15), channel_id=1, source_target_pairs={{0,8},{8,0},{1,9},{9,1},{2,10},{10,2},{3,11},{11,3},{4,12},{12,4},... | collective-permute-start | bytes 393224 | tf_op jit(solution)/shard_map/ppermute | solution.py:18
  100.9 7.7 %collective-permute-start.11 = (f32[128,256]{0,1:T(8,128)S(1)}, f32[128,256]{0,1:T(8,128)S(1)}, u32[]{:S(2)}, u32[]{:S(2)}) collective-permute-start(f32[128,256]{0,1:T(8,128)S(1)} %convolution_bitcast_fusion.22), channel_id=1, source_target_pairs={{0,32},{32,0},{64,96},{96,64},{128,160},{160,128},{192,224},{224,1... | collective-permute-start | bytes 393224 | tf_op jit(solution)/shard_map/ppermute | solution.py:18
  108.9 6.6 %collective-permute-start.13 = (f32[128,256]{0,1:T(8,128)S(1)}, f32[128,256]{0,1:T(8,128)S(1)}, u32[]{:S(2)}, u32[]{:S(2)}) collective-permute-start(f32[128,256]{0,1:T(8,128)S(1)} %convolution_bitcast_fusion.19), channel_id=1, source_target_pairs={{0,64},{64,0},{32,96},{96,32},{128,192},{192,128},{160,224},{224,1... | collective-permute-start | bytes 393224 | tf_op jit(solution)/shard_map/ppermute | solution.py:18
  115.8 11.8 %collective-permute-start.15 = (f32[128,256]{0,1:T(8,128)S(1)}, f32[128,256]{0,1:T(8,128)S(1)}, u32[]{:S(2)}, u32[]{:S(2)}) collective-permute-start(f32[128,256]{0,1:T(8,128)S(1)} %convolution_bitcast_fusion.16), channel_id=1, source_target_pairs={{0,128},{128,0},{32,160},{160,32},{64,192},{192,64},{96,224},{224,... | collective-permute-start | bytes 393224 | tf_op jit(solution)/shard_map/ppermute | solution.py:18
  127.9 10.4 %collective-permute-start.16 = (f32[128,256]{0,1:T(8,128)S(1)}, f32[128,256]{0,1:T(8,128)S(1)}, u32[]{:S(2)}, u32[]{:S(2)}) collective-permute-start(f32[128,256]{0,1:T(8,128)S(1)} %fusion.5), channel_id=1, source_target_pairs={{0,256},{256,0},{32,288},{288,32},{64,320},{320,64},{96,352},{352,... | collective-permute-start | bytes 393224 | tf_op jit(solution)/shard_map/ppermute | solution.py:18
  138.3 6.6 %collective-permute-start.14 = (f32[128,256]{0,1:T(8,128)S(1)}, f32[128,256]{0,1:T(8,128)S(1)}, u32[]{:S(2)}, u32[]{:S(2)}) collective-permute-start(f32[128,256]{0,1:T(8,128)S(1)} %fusion.7), channel_id=1, source_target_pairs={{0,128},{128,0},{32,160},{160,32},{64,192},{192,64},{96,224},{224,... | collective-permute-start | bytes 393224 | tf_op jit(solution)/shard_map/ppermute | solution.py:18
  144.9 7.8 %collective-permute-start.12 = (f32[128,256]{0,1:T(8,128)S(1)}, f32[128,256]{0,1:T(8,128)S(1)}, u32[]{:S(2)}, u32[]{:S(2)}) collective-permute-start(f32[128,256]{0,1:T(8,128)S(1)} %fusion.9), channel_id=1, source_target_pairs={{0,64},{64,0},{32,96},{96,32},{128,192},{192,128},{160,224},{224,1... | collective-permute-start | bytes 393224 | tf_op jit(solution)/shard_map/ppermute | solution.py:18
  152.7 7.7 %collective-permute-start.10 = (f32[128,256]{0,1:T(8,128)S(1)}, f32[128,256]{0,1:T(8,128)S(1)}, u32[]{:S(2)}, u32[]{:S(2)}) collective-permute-start(f32[128,256]{0,1:T(8,128)S(1)} %fusion.11), channel_id=1, source_target_pairs={{0,32},{32,0},{64,96},{96,64},{128,160},{160,128},{192,224},{224,1... | collective-permute-start | bytes 393224 | tf_op jit(solution)/shard_map/ppermute | solution.py:18
  160.0 12.1 %copy-start.8 = (f32[1,1,1,128,256]{3,4,2,1,0:T(8,128)S(1)}, f32[1,1,1,128,256]{3,4,2,1,0:T(8,128)}, u32[]{:S(2)}) copy-start(f32[1,1,1,128,256]{3,4,2,1,0:T(8,128)} %convolution_bitcast_fusion.40) | copy-start | bytes 393220
  160.4 8.1 %collective-permute-start.8 = (f32[128,256]{0,1:T(8,128)S(1)}, f32[128,256]{0,1:T(8,128)S(1)}, u32[]{:S(2)}, u32[]{:S(2)}) collective-permute-start(f32[128,256]{0,1:T(8,128)S(1)} %fusion.13), channel_id=1, source_target_pairs={{0,16},{16,0},{1,17},{17,1},{2,18},{18,2},{3,19},{19,3},{4,20},{20... | collective-permute-start | bytes 393224 | tf_op jit(solution)/shard_map/ppermute | solution.py:18
  173.6 1.9 %copy-start.1 = (f32[4,512,256]{2,1,0:T(8,128)S(1)}, f32[4,512,256]{2,1,0:T(8,128)}, u32[]{:S(2)}) copy-start(f32[4,512,256]{2,1,0:T(8,128)} %fusion.149) | copy-start | bytes 6291460
  175.5 1.5 copy-start.12
  177.0 7.5 %copy-start.13 = (pred[2048]{0:T(1024)(128)(4,1)S(1)}, pred[2048]{0:T(1024)(128)(4,1)}, u32[]{:S(2)}) copy-start(pred[2048]{0:T(1024)(128)(4,1)} %compare_and_fusion) | copy-start | bytes 6148
where the time goes:
time: 187 us; the launch traced here: 186 us
  starting transfers between devices  81 us (43%)
  local copies, waits for them, and re-layouts  38.6 us (21%)
  matrix products  35.1 us (19%)
  waiting for transfers between devices  22.1 us (12%)
  other arithmetic  8.24 us (4%)
    ppermute x17, starting transfers between devices, partner(): return lax.ppermute(block, axis, route)  81 us
    ppermute x17, waiting for transfers between devices, partner(): return lax.ppermute(block, axis, route)  22.1 us
    dot_general x17, matrix products, apply_transposed(): jnp.dot(matrix.T, vectors, precision=highest, preferred_element_type=jnp....  12.4 us
    gather x1, local copies, waits for them, and re-layouts, body(): jnp.take(points, ordering, axis=1)  9.53 us
    scatter x1, local copies, waits for them, and re-layouts, body(): inverse = jnp.zeros((per_device,), jnp.int32).at[ordering].set(jnp.arange...  8.19 us
    gather x1, local copies, waits for them, and re-layouts, body(): return jnp.take(tree_out, inverse, axis=0)  7.5 us
    gather x1, local copies, waits for them, and re-layouts, body(): jnp.take(rhs, ordering, axis=0).reshape(leaves_dev, leaf_size, rhs.shape[1])  7.49 us
    dot_general x1, matrix products, kernel_block(): jnp.dot(features.T, features, precision=highest, preferred_element_type=j...  5.96 us
  transfers between devices with their start and end apart: 17, of which 9 were waited for; matrix products, arithmetic and copies ran while one was open for 29% of the time, Pallas kernels for 0%

commit v1 on v0

v1 whole, which is shorter than its diff:
```python
import functools
import math

import jax
import jax.numpy as jnp
from jax import lax
from jax.experimental import pallas as pl
from jax.experimental.pallas import tpu as pltpu
from jax.sharding import PartitionSpec as P


kernel_rate = 0.125
f32 = jnp.float32
bf16 = jnp.bfloat16
vmem_bytes = 48 * 1024 * 1024


def split(a):
    high = a.astype(bf16)
    return high, (a - high.astype(f32)).astype(bf16)


def mm(a, b, turned=False):
    dims = (((1,), (1 if turned else 0,)), ((), ()))
    return lax.dot_general(a, b, dims, preferred_element_type=f32)


def mm3(a, b, turned=False):
    a_high, a_low = split(a)
    b_high, b_low = split(b)
    return mm(a_high, b_high, turned) + (mm(a_high, b_low, turned) + mm(a_low, b_high, turned))


def sibling_levels(width):
    return [0] + [k.bit_length() - 1 for k in range(1, width)]


def rise_kernel(
    order_ref, rhs_ref, basis_ref, local_ref, edge_ref, uexp_ref, member_ref, leaf_ref, node_ref, top_ref, send_ref
):
    points, cols = rhs_ref.shape
    leaves, size, rank = basis_ref.shape
    step = 256
    lane = lax.broadcasted_iota(jnp.int32, (size, rank), 1)
    sides = [
        jnp.concatenate([basis_ref[j], jnp.where(lane == j, 1.0, 0.0).astype(bf16)], axis=1)
        for j in range(leaves)
    ]
    for start in range(0, points, step):
        row = lax.broadcasted_iota(jnp.int32, (step, size), 0) + start
        member = jnp.zeros((step, rank), f32)
        for j in range(leaves):
            chosen = order_ref[:, j * size : (j + 1) * size] == row
            placed = mm(jnp.where(chosen, 1.0, 0.0).astype(bf16), sides[j])
            uexp_ref[start : start + step, j * rank : (j + 1) * rank] = placed[:, :rank].astype(bf16)
            member = member + placed[:, rank:]
        member_ref[start : start + step, :] = member.astype(bf16)
    coefficients = mm(rhs_ref[...].T, uexp_ref[...])
    nodes = [coefficients[:, j * rank : (j + 1) * rank] for j in range(leaves)]
    for j in range(leaves):
        leaf_ref[j] = nodes[j]
    lifted = [mm3(nodes[j], local_ref[0, j]) for j in range(leaves)]
    pair = [lifted[0] + lifted[1], lifted[2] + lifted[3]]
    for j in range(2):
        node_ref[j] = pair[j]
    own = mm3(pair[0], local_ref[0, leaves]) + mm3(pair[1], local_ref[0, leaves + 1])
    chain = [own]
    for level in range(3):
        chain.append(mm3(chain[-1], edge_ref[level, 0]))
    top_ref[...] = chain[3]
    me = lax.rem(lax.axis_index("dev"), 8)
    levels = sibling_levels(8)
    for k in range(8):
        send_ref[me ^ k] = chain[levels[k]]


def near_kernel(points_ref, member_ref, rhs_ref, near_ref):
    points, cols = rhs_ref.shape
    scale = math.sqrt(2.0 * kernel_rate / math.log(2.0))
    q = points_ref[...] * scale
    half = 0.5 * jnp.sum(q * q, axis=0, keepdims=True)

    def parts(a):
        one = a.astype(bf16).astype(f32)
        two = (a - one).astype(bf16).astype(f32)
        return one, two, (a - one - two).astype(bf16).astype(f32)

    q1, q2, q3 = parts(q)
    t1, t2, t3 = parts(-half)
    member_rows = member_ref[...].astype(f32).T[:8]
    eight = lax.broadcasted_iota(jnp.int32, (8, points), 0)

    def stack_rows(rows):
        out = jnp.zeros((8, points), f32)
        for index, value in enumerate(rows):
            out = jnp.where(eight == index, value, out)
        return out

    left_rows = stack_rows([t1, t2, t3, 1.0, 1.0, 1.0, -16.0])
    right_rows = stack_rows([1.0, 1.0, 1.0, t1, t2, t3, 16.0])
    blank = jnp.zeros((64, points), f32)
    group = member_rows * 16.0
    left = jnp.concatenate([q1, q1, q2, q2, q1, q3, left_rows, group, blank], axis=0)
    right = jnp.concatenate([q1, q2, q1, q2, q3, q1, right_rows, group, blank], axis=0).astype(bf16)
    left = left.T.astype(bf16)
    step, chunk = 256, 512
    for start in range(0, points, step):
        total = rhs_ref[start : start + step, :].astype(f32)
        for base in range(0, points, chunk):
            power = mm(left[start : start + step], right[:, base : base + chunk])
            total = total + mm(jnp.exp2(power).astype(bf16), rhs_ref[base : base + chunk, :])
        near_ref[start : start + step, :] = total


def turn(left, matrix):
    return jnp.where(left, matrix.T, matrix)


def prepare_kernel(edge_ref, link_ref, local_ref, up_low_ref, up_high_ref, down_low_ref, down_ref, leaf_down_ref):
    levels = link_ref.shape[0]
    place = lax.axis_index("group") * 32 + lax.axis_index("dev")
    edge = [edge_ref[level, 0] for level in range(levels - 1)]
    pair_matrix = [turn(lax.rem(lax.shift_right_logical(place, level), 2) == 0, link_ref[level, 0]) for level in range(levels)]
    path = {3: None}
    product = edge[3]
    path[4] = product
    for level in range(5, levels):
        product = mm3(product, edge[level - 1])
        path[level] = product
    up_low_ref[0] = path[4]
    up_low_ref[1] = path[5]
    up_low_ref[2] = path[6]
    up_high_ref[0] = edge[6]
    up_high_ref[1] = mm3(edge[6], edge[7])
    down_ref[0] = pair_matrix[3]
    for level in range(4, levels):
        down_ref[level - 3] = mm3(pair_matrix[level], path[level], True)
    low = edge[0]
    down_low_ref[0] = pair_matrix[0]
    down_low_ref[1] = mm3(pair_matrix[1], low, True)
    low = mm3(low, edge[1])
    down_low_ref[2] = mm3(pair_matrix[2], low, True)
    low = mm3(low, edge[2])
    for j in range(2):
        inner = mm3(local_ref[0, 4 + j], low)
        for k in range(2):
            leaf_down_ref[2 * j + k] = mm3(local_ref[0, 2 * j + k], inner)


def first_kernel(got_ref, up_ref, send_ref):
    rows = got_ref.shape[0] // 8
    total = got_ref[0:rows]
    for k in range(1, 8):
        total = total + got_ref[k * rows : (k + 1) * rows]
    lifted = [mm3(total, up_ref[k]) for k in range(3)]
    me = lax.rem(lax.axis_index("group"), 2) * 4 + lax.div(lax.axis_index("dev"), 8)
    shares = [total, lifted[0], lifted[1]]
    levels = sibling_levels(8)
    for k in range(8):
        send_ref[me ^ k, :rows] = shares[levels[k]]
        send_ref[me ^ k, rows:] = lifted[2]


def second_kernel(got_ref, up_ref, send_ref):
    rows = got_ref.shape[1] // 2
    total = got_ref[0, rows:]
    for k in range(1, 8):
        total = total + got_ref[k, rows:]
    shares = [total, mm3(total, up_ref[0]), mm3(total, up_ref[1])]
    me = lax.div(lax.axis_index("group"), 2)
    levels = sibling_levels(8)
    for k in range(8):
        send_ref[me ^ k] = shares[levels[k]]


def sibling_sums(load, me):
    return [
        load(me ^ 1),
        load(me ^ 2) + load(me ^ 3),
        (load(me ^ 4) + load(me ^ 5)) + (load(me ^ 6) + load(me ^ 7)),
    ]


def third_kernel(got_mid_ref, got_ref, down_ref, send_ref):
    rows = got_ref.shape[1]
    mid = lax.rem(lax.axis_index("group"), 2) * 4 + lax.div(lax.axis_index("dev"), 8)
    top = lax.div(lax.axis_index("group"), 2)
    sums = sibling_sums(lambda k: got_mid_ref[k, :rows], mid) + sibling_sums(lambda k: got_ref[k], top)
    field = mm3(sums[0], down_ref[0])
    for level in range(1, 6):
        field = field + mm3(sums[level], down_ref[level])
    for k in range(8):
        send_ref[k] = field


def base_kernel(got_ref, leaf_ref, node_ref, local_ref, coupling_ref, down_ref, base_ref):
    me = lax.rem(lax.axis_index("dev"), 8)
    sums = sibling_sums(lambda k: got_ref[k], me)
    own = mm3(sums[0], down_ref[0]) + mm3(sums[1], down_ref[1]) + mm3(sums[2], down_ref[2])
    rank = own.shape[1]
    coupled = [mm3(node_ref[1], coupling_ref[0, 2], True), mm3(node_ref[0], coupling_ref[0, 2])]
    for j in range(2):
        inner = coupled[j] + mm3(own, local_ref[0, 4 + j], True)
        low, high = 2 * j, 2 * j + 1
        link = coupling_ref[0, j]
        base_ref[:, low * rank : (low + 1) * rank] = mm3(leaf_ref[high], link, True) + mm3(
            inner, local_ref[0, low], True
        )
        base_ref[:, high * rank : (high + 1) * rank] = mm3(leaf_ref[low], link) + mm3(
            inner, local_ref[0, high], True
        )


def fall_kernel(field_ref, down_ref, base_ref, uexp_ref, near_ref, out_ref):
    rank = field_ref.shape[1]
    far = [
        (base_ref[:, j * rank : (j + 1) * rank] + mm3(field_ref[...], down_ref[j], True)).astype(bf16)
        for j in range(4)
    ]
    far = jnp.concatenate(far, axis=1)
    step = 256
    for start in range(0, out_ref.shape[0], step):
        rows = slice(start, start + step)
        out_ref[rows, :] = (near_ref[rows, :] + mm(uexp_ref[rows, :], far, True)).astype(bf16)


def call(kernel, outs, *args, flops=0, name=None):
    shapes = [jax.ShapeDtypeStruct(shape, dtype) for shape, dtype in outs]
    moved = sum(a.size * a.dtype.itemsize for a in args)
    moved += sum(math.prod(s.shape) * s.dtype.itemsize for s in shapes)
    result = pl.pallas_call(
        kernel,
        out_shape=shapes,
        in_specs=[pl.BlockSpec(memory_space=pltpu.VMEM)] * len(args),
        out_specs=[pl.BlockSpec(memory_space=pltpu.VMEM)] * len(outs),
        compiler_params=pltpu.CompilerParams(vmem_limit_bytes=vmem_bytes),
        cost_estimate=pl.CostEstimate(flops=flops, bytes_accessed=moved, transcendentals=0),
        name=name,
    )(*args)
    return result[0] if len(outs) == 1 else result


def body(
    points, order, rhs, leaf_basis, local_transfer, local_coupling, cross_transfer, cross_coupling
):
    count, cols = rhs.shape
    leaves, size, rank = leaf_basis.shape
    slice_cols = cols // 8
    block = rank * rank
    y_groups = [[x * 8 + y for y in range(8)] for x in range(4)]
    mid_groups = [
        [(z * 2 + core) * 32 + x * 8 + y for core in range(2) for x in range(4)]
        for z in range(8)
        for y in range(8)
    ]
    z_groups = [[z * 2 + core for z in range(8)] for core in range(2)]

    uexp, member, leaf_nodes, inner_nodes, top_share, low_send = call(
        rise_kernel,
        [
            ((count, leaves * rank), bf16),
            ((count, rank), bf16),
            ((leaves, cols, rank), f32),
            ((2, cols, rank), f32),
            ((cols, rank), f32),
            ((8, cols, rank), f32),
        ],
        order,
        rhs,
        leaf_basis,
        local_transfer,
        cross_transfer,
        flops=2 * count * count * 2 * rank,
        name="rise",
    )
    got_first = lax.all_to_all(top_share, "dev", 0, 0, tiled=True, axis_index_groups=y_groups)
    got_low = lax.all_to_all(low_send, "dev", 0, 0, tiled=True, axis_index_groups=y_groups)
    up_low, up_high, down_low, down_mid, leaf_down = call(
        prepare_kernel,
        [
            ((3, rank, rank), f32),
            ((2, rank, rank), f32),
            ((3, rank, rank), f32),
            ((6, rank, rank), f32),
            ((leaves, rank, rank), f32),
        ],
        cross_transfer,
        cross_coupling,
        local_transfer,
        flops=2 * 60 * block * rank,
        name="prepare",
    )
    near = call(
        near_kernel, [((count, cols), f32)], points, member, rhs, flops=2 * count * count * (cols + rank), name="near"
    )
    first_send = call(
        first_kernel, [((8, 2 * slice_cols, rank), f32)], got_first, up_low, flops=18 * slice_cols * block, name="first"
    )
    got_mid = lax.all_to_all(first_send, ("group", "dev"), 0, 0, tiled=True, axis_index_groups=mid_groups)
    second_send = call(
        second_kernel, [((8, slice_cols, rank), f32)], got_mid, up_high, flops=12 * slice_cols * block, name="second"
    )
    got_top = lax.all_to_all(second_send, "group", 0, 0, tiled=True, axis_index_groups=z_groups)
    third_send = call(
        third_kernel,
        [((8, slice_cols, rank), f32)],
        got_mid,
        got_top,
        down_mid,
        flops=36 * slice_cols * block,
        name="third",
    )
    field = lax.all_to_all(third_send, "dev", 0, 0, tiled=True, axis_index_groups=y_groups)
    base = call(
        base_kernel,
        [((cols, leaves * rank), f32)],
        got_low,
        leaf_nodes,
        inner_nodes,
        local_transfer,
        local_coupling,
        down_low,
        flops=2 * 45 * cols * block,
        name="base",
    )
    return call(
        fall_kernel,
        [((count, cols), bf16)],
        field.reshape(cols, rank),
        leaf_down,
        base,
        uexp,
        near,
        flops=2 * count * cols * leaves * rank,
        name="fall",
    )


def solution(mesh):
    placed = (
        P(None, ("group", "dev")),
        P(("group", "dev"), None),
        P(("group", "dev"), None),
        P(("group", "dev"), None, None),
        P(("group", "dev"), None, None, None),
        P(("group", "dev"), None, None, None),
        P(None, ("group", "dev"), None, None),
        P(None, ("group", "dev"), None, None),
    )
    return jax.shard_map(
        body, mesh=mesh, in_specs=placed, out_specs=P(("group", "dev"), None), check_vma=False
    )
```

time: 187 us -> 112 us (0.60)
  starting transfers between devices: 81 us -> 15.4 us
  matrix products: 35.1 us -> 0 us
  blocking collectives: 0 us -> 30.4 us
  local copies, waits for them, and re-layouts: 38.6 us -> 14.2 us
  Pallas kernels: 0 us -> 17.1 us
  waiting for transfers between devices: 22.1 us -> 33.6 us
  other arithmetic: 8.24 us -> 0 us
    ppermute x17 -> x0, starting transfers between devices: 81 us -> none  [partner(): return lax.ppermute(block, axis, route)]
    dot_general x46 -> x0, matrix products: 35.1 us -> none  [the longest x17 12.4 us: apply_transposed(): jnp.dot(matrix.T, vectors, precision=highest, preferred_element_type=jnp....]
    all_to_all x0 -> x3, waiting for transfers between devices: none -> 33.6 us  [the longest x1 28.2 us: body(): lax.all_to_all(low_send, 'dev', 0, 0, tiled=True, axis_index_groups=y_gro...]
    all_to_all x0 -> x2, blocking collectives: none -> 30.4 us  [the longest x1 17.7 us: body(): lax.all_to_all(second_send, 'group', 0, 0, tiled=True, axis_index_groups=...]
    gather x3 -> x0, local copies, waits for them, and re-layouts: 24.5 us -> none  [the longest x1 9.53 us: body(): jnp.take(points, ordering, axis=1)]
    ppermute x17 -> x0, waiting for transfers between devices: 22.1 us -> none  [partner(): return lax.ppermute(block, axis, route)]
    pallas_call x0 -> x8, Pallas kernels: none -> 17.1 us  [call(): pl.pallas_call(kernel, out_shape=shapes, in_specs=[pl.BlockSpec(memory_sp...]
    all_to_all x0 -> x3, starting transfers between devices: none -> 15.4 us  [the longest x1 7.65 us: body(): lax.all_to_all(top_share, 'dev', 0, 0, tiled=True, axis_index_groups=y_gr...]
  transfers between devices with their start and end apart: 17 -> 3, of which waited for: 9 -> 2; matrix products, arithmetic and copies ran while one was open for 29% -> 0% of each run, Pallas kernels for 0% -> 8%
where the time goes in v1:
time: 112 us; the launch traced here: 111 us
  waiting for transfers between devices  33.6 us (30%)
  blocking collectives  30.4 us (27%)
  Pallas kernels  17.1 us (15%)
  starting transfers between devices  15.4 us (14%)
  local copies, waits for them, and re-layouts  14.2 us (13%)
    all_to_all x1, waiting for transfers between devices, body(): lax.all_to_all(low_send, 'dev', 0, 0, tiled=True, axis_index_groups=y_gro...  28.2 us
    all_to_all x1, blocking collectives, body(): lax.all_to_all(second_send, 'group', 0, 0, tiled=True, axis_index_groups=...  17.7 us
    pallas_call x8, Pallas kernels, call(): pl.pallas_call(kernel, out_shape=shapes, in_specs=[pl.BlockSpec(memory_sp...  17.1 us
    unnamed x48, local copies, waits for them, and re-layouts  14.2 us
    all_to_all x1, blocking collectives, body(): lax.all_to_all(first_send, ('group', 'dev'), 0, 0, tiled=True, axis_index...  12.7 us
    all_to_all x1, starting transfers between devices, body(): lax.all_to_all(top_share, 'dev', 0, 0, tiled=True, axis_index_groups=y_gr...  7.65 us
    all_to_all x1, waiting for transfers between devices, body(): lax.all_to_all(top_share, 'dev', 0, 0, tiled=True, axis_index_groups=y_gr...  5.46 us
    all_to_all x1, starting transfers between devices, body(): lax.all_to_all(third_send, 'dev', 0, 0, tiled=True, axis_index_groups=y_g...  4.18 us
  transfers between devices with their start and end apart: 3, of which 2 were waited for; matrix products, arithmetic and copies ran while one was open for 0% of the time, Pallas kernels for 8%

profile of v1, /device:TPU:1, one launch (start us, length us, event | category | flops | bytes accessed | tf_op | source)
XLA Modules:
  0.0 110.9 jit_solution(666308376509857162)
XLA Ops:
  0.0 1.0 copy-done.5
  1.0 1.0 copy-done.8
  2.0 1.2 %copy-done.19 = bf16[2048,256]{1,0:T(8,128)(2,1)S(1)} copy-done((bf16[2048,256]{1,0:T(8,128)(2,1)S(1)}, bf16[2048,256]{1,0:T(8,128)(2,1)}, u32[]{:S(2)}) %copy-start.19) | copy-done | bytes 1048600
  3.3 1.0 copy-done.21
  4.3 0.7 copy-done.23
  5.0 5.1 %rise.1 = (bf16[2048,512]{1,0:T(8,128)(2,1)}, bf16[2048,128]{1,0:T(8,128)(2,1)S(1)}, f32[4,256,128]{2,1,0:T(8,128)S(1)}, f32[2,256,128]{2,1,0:T(8,128)S(1)}, f32[256,128]{1,0:T(8,128)}, /*index=5*/f32[8,256,128]{2,1,0:T(8,128)}) custom-call(s32[1,2048]{1,0:T(1,128)S(1)} %copy-done.23, bf16[2048,256]{1,0:T(8,128)(2,1)S(1)} %copy-done.19, ...), custom_call_target="tpu_custom_call" | custom-call | flops 2147483648 | bytes 7086080 | tf_op jit(solution)/shard_map/rise/pallas_call | solution.py:231
  10.1 0.8 copy-done.10
  10.9 0.7 copy-done.12
  11.6 7.7 %all-to-all-start = ((f32[8,32,128]{2,1,0:T(8,128)}), f32[8,32,128]{2,1,0:T(8,128)S(1)}, u32[]{:S(2)}, u32[]{:S(2)}) async-start(f32[8,32,128]{2,1,0:T(8,128)} %bitcast), calls=%async_computation | async-start | bytes 262144 | tf_op jit(solution)/shard_map/all_to_all | solution.py:276
  19.3 1.8 %prepare.1 = (f32[3,128,128]{2,1,0:T(8,128)S(1)}, f32[2,128,128]{2,1,0:T(8,128)S(1)}, f32[3,128,128]{2,1,0:T(8,128)S(1)}, f32[6,128,128]{2,1,0:T(8,128)S(1)}, f32[4,128,128]{2,1,0:T(8,128)S(1)}) custom-call(f32[8,1,128,128]{3,2,1,0:T(8,128)S(1)} %copy-done.9, f32[9,1,128,128]{3,2,1,0:T(8,128)S(1)} %copy-done.7, f32[1,6,128,128]{3,2,1,0:T(8,128)S(1)} %copy-done.6), custom_call_target="tpu_custom_call" | custom-call | flops 251658240 | bytes 2686976 | tf_op jit(solution)/shard_map/prepare/pallas_call | solution.py:231
  21.1 0.7 copy-done.14
  21.8 5.5 %all-to-all-done = f32[8,32,128]{2,1,0:T(8,128)S(1)} async-done(((f32[8,32,128]{2,1,0:T(8,128)}), f32[8,32,128]{2,1,0:T(8,128)S(1)}, u32[]{:S(2)}, u32[]{:S(2)}) %all-to-all-start) | async-done | bytes 131104 | tf_op jit(solution)/shard_map/all_to_all | solution.py:276
  27.3 0.2 first.1
  27.5 12.7 %all_to_all.31.got_ref.got_mid_ref = f32[8,64,128]{2,1,0:T(8,128)S(1)} all-to-all(f32[8,64,128]{2,1,0:T(8,128)S(1)} %first.1), channel_id=1, replica_groups={{0,8,16,24,32,40,48,56},{1,9,17,25,33,41,49,57},{2,10,18,26,34,42,50,58..., dimensions={0} | all-to-all | bytes 524288 | tf_op jit(solution)/shard_map/all_to_all | solution.py:299
  40.2 0.2 second.1
  40.4 17.7 %all_to_all.32.got_ref = f32[8,32,128]{2,1,0:T(8,128)S(1)} all-to-all(f32[8,32,128]{2,1,0:T(8,128)S(1)} %second.1), channel_id=1, replica_groups={{0,64,128,192,256,320,384,448},{32,96,160,224,288,352,416,480},{1,65,12..., dimensions={0} | all-to-all | bytes 262144 | tf_op jit(solution)/shard_map/all_to_all | solution.py:303
  58.1 3.6 %all-to-all-start.4 = ((f32[8,256,128]{2,1,0:T(8,128)}), f32[8,256,128]{2,1,0:T(8,128)S(1)}, u32[]{:S(2)}, u32[]{:S(2)}) async-start(f32[8,256,128]{2,1,0:T(8,128)} %get-tuple-element.21), calls=%async_computation.4 | async-start | bytes 2097152 | tf_op jit(solution)/shard_map/all_to_all | solution.py:277
  61.7 0.9 third.1
  62.6 28.2 %all-to-all-done.4.got_ref = f32[8,256,128]{2,1,0:T(8,128)S(1)} async-done(((f32[8,256,128]{2,1,0:T(8,128)}), f32[8,256,128]{2,1,0:T(8,128)S(1)}, u32[]{:S(2)}, u32[]{:S(2)}) %all-to-all-start.4) | async-done | bytes 1048608 | tf_op jit(solution)/shard_map/all_to_all | solution.py:277
  90.8 4.2 %all-to-all-start.3 = ((f32[8,32,128]{2,1,0:T(8,128)}), f32[8,32,128]{2,1,0:T(8,128)}, u32[]{:S(2)}, u32[]{:S(2)}) async-start(f32[8,32,128]{2,1,0:T(8,128)} %third.1), calls=%async_computation.3 | async-start | bytes 262144 | tf_op jit(solution)/shard_map/all_to_all | solution.py:313
  95.0 0.0 copy-start.20
  95.0 1.2 %copy-done.20 = bf16[2048,256]{1,0:T(8,128)(2,1)S(1)} copy-done((bf16[2048,256]{1,0:T(8,128)(2,1)S(1)}, bf16[2048,256]{1,0:T(8,128)(2,1)}, u32[]{:S(2)}) %copy-start.20) | copy-done | bytes 1048600
  96.2 4.8 %near.1.near_ref = f32[2048,256]{1,0:T(8,128)S(1)} custom-call(f32[8,2048]{1,0:T(8,128)S(1)} %copy-done.22, bf16[2048,128]{1,0:T(8,128)(2,1)S(1)} %get-tuple-element.26.member_ref, bf16[2048,256]{1,0:T(8,128)(2,1)S(1)} %copy-done.20), custom_call_target="tpu_custom_call" | custom-call | flops 3221225472 | bytes 3735552 | tf_op jit(solution)/shard_map/near/pallas_call | solution.py:231
  101.1 1.3 %copy-done.1 = f32[2048,256]{1,0:T(8,128)} copy-done((f32[2048,256]{1,0:T(8,128)}, f32[2048,256]{1,0:T(8,128)S(1)}, u32[]{:S(2)}) %copy-start.1) | copy-done | bytes 2097176
  102.4 1.2 %base.1.base_ref = f32[256,512]{1,0:T(8,128)S(1)} custom-call(f32[8,256,128]{2,1,0:T(8,128)S(1)} %all-to-all-done.4.got_ref, f32[4,256,128]{2,1,0:T(8,128)S(1)} %copy-done.11, f32[2,256,128]{2,1,0:T(8,128)S(1)} %copy-done.13, f32[1,6,128,128]{3,2,1,0:T(8,128)S(1)} %copy-done.6, f32[1,3,128,128]{3,2,1,0:T(8,128)S(1)} %copy-done.16, f32[3,128,128]{2,1,0:T(8,128)S(1)} %copy-done.18), custom_call_target="tpu_custom_call" | custom-call | flops 377487360 | bytes 3145728 | tf_op jit(solution)/shard_map/base/pallas_call | solution.py:231
  103.6 0.0 copy-start.3
  103.6 0.8 copy-done.3
  104.4 0.0 all-to-all-done.3
  104.4 1.6 %copy-done.2 = f32[2048,256]{1,0:T(8,128)S(1)} copy-done((f32[2048,256]{1,0:T(8,128)S(1)}, f32[2048,256]{1,0:T(8,128)}, u32[]{:S(2)}) %copy-start.2) | copy-done | bytes 2097176
  106.0 1.0 copy-done.4
  107.0 0.9 copy-done.15
  108.0 2.9 %fall.1 = bf16[2048,256]{1,0:T(8,128)(2,1)} custom-call(f32[256,128]{1,0:T(8,128)} %bitcast.2.field_ref, f32[4,128,128]{2,1,0:T(8,128)S(1)} %copy-done.15, f32[256,512]{1,0:T(8,128)S(1)} %copy-done.4, bf16[2048,512]{1,0:T(8,128)(2,1)S(1)} %copy-done, f32[2048,256]{1,0:T(8,128)S(1)} %copy-done.2), custom_call_target="tpu_custom_call" | custom-call | flops 536870912 | bytes 6160384 | tf_op jit(solution)/shard_map/fall/pallas_call | solution.py:231
  (32 shorter events, 0.1 us)
Async XLA Ops:
  0.0 1.0 copy-start.5
  1.0 1.0 copy-start.8
  2.0 1.2 %copy-start.19 = (bf16[2048,256]{1,0:T(8,128)(2,1)S(1)}, bf16[2048,256]{1,0:T(8,128)(2,1)}, u32[]{:S(2)}) copy-start(bf16[2048,256]{1,0:T(8,128)(2,1)} %rhs_ref.3) | copy-start | bytes 3145732
  3.3 1.0 copy-start.21
  4.3 0.7 copy-start.23
  5.0 14.3 %copy-start.6 = (f32[1,6,128,128]{3,2,1,0:T(8,128)S(1)}, f32[1,6,128,128]{3,2,1,0:T(8,128)}, u32[]{:S(2)}) copy-start(f32[1,6,128,128]{3,2,1,0:T(8,128)} %local_ref.5) | copy-start | bytes 1179652
  5.0 14.3 %copy-start.7 = (f32[9,1,128,128]{3,2,1,0:T(8,128)S(1)}, f32[9,1,128,128]{3,2,1,0:T(8,128)}, u32[]{:S(2)}) copy-start(f32[9,1,128,128]{3,2,1,0:T(8,128)} %link_ref.1) | copy-start | bytes 1769476
  5.0 14.3 %copy-start.9 = (f32[8,1,128,128]{3,2,1,0:T(8,128)S(1)}, f32[8,1,128,128]{3,2,1,0:T(8,128)}, u32[]{:S(2)}) copy-start(f32[8,1,128,128]{3,2,1,0:T(8,128)} %edge_ref.3) | copy-start | bytes 1572868
  10.1 0.8 copy-start.10
  10.9 0.7 copy-start.12
  11.6 15.7 %all-to-all-start = ((f32[8,32,128]{2,1,0:T(8,128)}), f32[8,32,128]{2,1,0:T(8,128)S(1)}, u32[]{:S(2)}, u32[]{:S(2)}) async-start(f32[8,32,128]{2,1,0:T(8,128)} %bitcast), calls=%async_computation | async-start | bytes 262144 | tf_op jit(solution)/shard_map/all_to_all | solution.py:276
  21.1 0.7 copy-start.14
  21.8 40.8 %copy-start.17 = (f32[3,128,128]{2,1,0:T(8,128)}, f32[3,128,128]{2,1,0:T(8,128)S(1)}, u32[]{:S(2)}) copy-start(f32[3,128,128]{2,1,0:T(8,128)S(1)} %get-tuple-element.24.down_ref) | copy-start | bytes 589828
  40.2 54.8 %copy-start.22 = (f32[8,2048]{1,0:T(8,128)S(1)}, f32[8,2048]{1,0:T(8,128)}, u32[]{:S(2)}) copy-start(f32[8,2048]{1,0:T(8,128)} %points_ref.1) | copy-start | bytes 196612
  58.1 32.7 %all-to-all-start.4 = ((f32[8,256,128]{2,1,0:T(8,128)}), f32[8,256,128]{2,1,0:T(8,128)S(1)}, u32[]{:S(2)}, u32[]{:S(2)}) async-start(f32[8,256,128]{2,1,0:T(8,128)} %get-tuple-element.21), calls=%async_computation.4 | async-start | bytes 2097152 | tf_op jit(solution)/shard_map/all_to_all | solution.py:277
  90.8 13.6 %all-to-all-start.3 = ((f32[8,32,128]{2,1,0:T(8,128)}), f32[8,32,128]{2,1,0:T(8,128)}, u32[]{:S(2)}, u32[]{:S(2)}) async-start(f32[8,32,128]{2,1,0:T(8,128)} %third.1), calls=%async_computation.3 | async-start | bytes 262144 | tf_op jit(solution)/shard_map/all_to_all | solution.py:313
  95.0 1.2 %copy-start.20 = (bf16[2048,256]{1,0:T(8,128)(2,1)S(1)}, bf16[2048,256]{1,0:T(8,128)(2,1)}, u32[]{:S(2)}) copy-start(bf16[2048,256]{1,0:T(8,128)(2,1)} %rhs_ref.3) | copy-start | bytes 3145732
  96.2 6.2 %copy-start.11 = (f32[4,256,128]{2,1,0:T(8,128)S(1)}, f32[4,256,128]{2,1,0:T(8,128)}, u32[]{:S(2)}) copy-start(f32[4,256,128]{2,1,0:T(8,128)} %copy-done.10) | copy-start | bytes 1572868
  96.2 6.2 %copy-start.13 = (f32[2,256,128]{2,1,0:T(8,128)S(1)}, f32[2,256,128]{2,1,0:T(8,128)}, u32[]{:S(2)}) copy-start(f32[2,256,128]{2,1,0:T(8,128)} %copy-done.12) | copy-start | bytes 786436
  96.2 6.2 %copy-start.16 = (f32[1,3,128,128]{3,2,1,0:T(8,128)S(1)}, f32[1,3,128,128]{3,2,1,0:T(8,128)}, u32[]{:S(2)}) copy-start(f32[1,3,128,128]{3,2,1,0:T(8,128)} %coupling_ref.1) | copy-start | bytes 589828
  96.2 6.2 %copy-start.18 = (f32[3,128,128]{2,1,0:T(8,128)S(1)}, f32[3,128,128]{2,1,0:T(8,128)}, u32[]{:S(2)}) copy-start(f32[3,128,128]{2,1,0:T(8,128)} %copy-done.17) | copy-start | bytes 589828
  101.1 1.3 %copy-start.1 = (f32[2048,256]{1,0:T(8,128)}, f32[2048,256]{1,0:T(8,128)S(1)}, u32[]{:S(2)}) copy-start(f32[2048,256]{1,0:T(8,128)S(1)} %near.1.near_ref) | copy-start | bytes 6291460
  102.4 2.0 %copy-start = (bf16[2048,512]{1,0:T(8,128)(2,1)S(1)}, bf16[2048,512]{1,0:T(8,128)(2,1)}, u32[]{:S(2)}) copy-start(bf16[2048,512]{1,0:T(8,128)(2,1)} %get-tuple-element.25.uexp_ref) | copy-start | bytes 6291460
  103.6 0.8 copy-start.3
  104.4 1.6 %copy-start.2 = (f32[2048,256]{1,0:T(8,128)S(1)}, f32[2048,256]{1,0:T(8,128)}, u32[]{:S(2)}) copy-start(f32[2048,256]{1,0:T(8,128)} %copy-done.1) | copy-start | bytes 6291460
  106.0 1.0 copy-start.4
  107.0 0.9 copy-start.15

commit v2 on v1

v2 whole, which is shorter than its diff:
```python
import functools
import math

import jax
import jax.numpy as jnp
from jax import lax
from jax.experimental import pallas as pl
from jax.experimental.pallas import tpu as pltpu
from jax.sharding import PartitionSpec as P


kernel_rate = 0.125
f32 = jnp.float32
bf16 = jnp.bfloat16


def split(a):
    high = a.astype(bf16)
    return high, (a - high.astype(f32)).astype(bf16)


def mm(a, b, turned=False):
    dims = (((1,), (1 if turned else 0,)), ((), ()))
    return lax.dot_general(a, b, dims, preferred_element_type=f32)


def mm3(a, b, turned=False):
    a_high, a_low = split(a)
    b_high, b_low = split(b)
    return mm(
        jnp.concatenate([a_high, a_low, a_high], axis=1),
        jnp.concatenate([b_high, b_high, b_low], axis=1 if turned else 0),
        turned,
    )


def sibling_levels(width):
    return [0] + [k.bit_length() - 1 for k in range(1, width)]


def rise_kernel(order_in, basis_in, rhs_in, local_in, edge_in, uexp_out, member_out, leaf_out, node_out, zero_out, send_out):
    order_ref, basis_ref = order_in(), basis_in()
    uexp_ref, member_ref = uexp_out.ref, member_out.ref
    points = order_ref.shape[1]
    leaves, size, rank = basis_ref.shape
    step = 256
    lane = lax.broadcasted_iota(jnp.int32, (size, rank), 1)
    index = lax.broadcasted_iota(jnp.int32, (step, size), 0).astype(jnp.int16)
    sides = [
        jnp.concatenate([basis_ref[j], jnp.where(lane == j, 1.0, 0.0).astype(bf16)], axis=1)
        for j in range(leaves)
    ]
    one = jnp.ones((step, size), bf16)
    zero = jnp.zeros((step, size), bf16)
    for start in range(0, points, step):
        member = jnp.zeros((step, rank), f32)
        for j in range(leaves):
            wanted = (order_ref[:, j * size : (j + 1) * size] - start).astype(jnp.int16)
            placed = mm(jnp.where(wanted == index, one, zero), sides[j])
            uexp_ref[start : start + step, j * rank : (j + 1) * rank] = placed[:, :rank].astype(bf16)
            member = member + placed[:, rank:]
        member_ref[start : start + step, :] = member.astype(bf16)
        uexp_out.send(start, step)
        member_out.send(start, step)
    local_ref, edge_ref = local_in(), edge_in()
    coefficients = mm(rhs_in()[...].T, uexp_ref[...])
    cols = coefficients.shape[0]
    leaf_out.ref[...] = coefficients
    leaf_out.send()
    lifted = [mm3(coefficients[:, j * rank : (j + 1) * rank], local_ref[0, j]) for j in range(leaves)]
    pair = [lifted[0] + lifted[1], lifted[2] + lifted[3]]
    node_out.ref[0], node_out.ref[1] = pair
    node_out.send()
    own = mm3(pair[0], local_ref[0, leaves]) + mm3(pair[1], local_ref[0, leaves + 1])
    zero_out.ref[...] = own
    zero_out.send()
    rows = cols // 8
    for level in range(3):
        own = mm3(own, edge_ref[level, 0])
        send_out.ref[:, level * rows : (level + 1) * rows] = own.reshape(8, rows, rank)


def near_kernel(points_in, member_in, rhs_in, near_out):
    points_ref, member_ref = points_in(), member_in()
    points = points_ref.shape[1]
    scale = math.sqrt(2.0 * kernel_rate / math.log(2.0))
    q = points_ref[...] * scale
    half = 0.5 * jnp.sum(q * q, axis=0, keepdims=True)

    def parts(a):
        one = a.astype(bf16).astype(f32)
        two = (a - one).astype(bf16).astype(f32)
        return one, two, (a - one - two).astype(bf16).astype(f32)

    q1, q2, q3 = parts(q)
    t1, t2, t3 = parts(-half)
    member_rows = member_ref[...].astype(f32).T[:8]
    eight = lax.broadcasted_iota(jnp.int32, (8, points), 0)

    def stack_rows(rows):
        out = jnp.zeros((8, points), f32)
        for index, value in enumerate(rows):
            out = jnp.where(eight == index, value, out)
        return out

    left_rows = stack_rows([t1, t2, t3, 1.0, 1.0, 1.0, -16.0])
    right_rows = stack_rows([1.0, 1.0, 1.0, t1, t2, t3, 16.0])
    blank = jnp.zeros((64, points), f32)
    group = member_rows * 16.0
    left = jnp.concatenate([q1, q1, q2, q2, q1, q3, left_rows, group, blank], axis=0)
    right = jnp.concatenate([q1, q2, q1, q2, q3, q1, right_rows, group, blank], axis=0).astype(bf16)
    left = left.T.astype(bf16)
    rhs_ref, near_ref = rhs_in(), near_out.ref
    step, chunk = 256, 512
    for start in range(0, points, step):
        total = rhs_ref[start : start + step, :].astype(f32)
        for base in range(0, points, chunk):
            power = mm(left[start : start + step], right[:, base : base + chunk])
            total = total + mm(jnp.exp2(power).astype(bf16), rhs_ref[base : base + chunk, :])
        near_ref[start : start + step, :] = total
        near_out.send(start, step)


def turn(left, matrix):
    return jnp.where(left, matrix.T, matrix)


def shadow_kernel(
    edge_in, link_in, local_in, coupling_in, leaf_in, node_in, up_low_out, up_high_out, down_mid_out, down_out, base_out
):
    edge_ref, link_ref, local_ref = edge_in(), link_in(), local_in()
    levels = link_ref.shape[0]
    rank = edge_ref.shape[-1]
    place = lax.axis_index("group") * 32 + lax.axis_index("dev")
    edge = [edge_ref[level, 0] for level in range(levels - 1)]
    pair_matrix = [
        turn(lax.rem(lax.shift_right_logical(place, level), 2) == 0, link_ref[level, 0]) for level in range(levels)
    ]
    path = {4: edge[3]}
    for level in range(5, levels):
        path[level] = mm3(path[level - 1], edge[level - 1])
    for level in range(4, 7):
        up_low_out.ref[level - 4] = path[level]
    up_low_out.send()
    up_high_out.ref[0] = edge[6]
    up_high_out.ref[1] = mm3(edge[6], edge[7])
    up_high_out.send()
    down_mid_out.ref[0] = pair_matrix[3]
    for level in range(4, levels):
        down_mid_out.ref[level - 3] = mm3(pair_matrix[level], path[level], True)
    down_mid_out.send()
    low = {1: edge[0]}
    low[2] = mm3(low[1], edge[1])
    low[3] = mm3(low[2], edge[2])
    leaf_path = []
    for j in range(4):
        leaf_path.append(mm3(local_ref[0, j], local_ref[0, 4 + j // 2]))
    leaf_path = jnp.concatenate(leaf_path, axis=0)
    down_out.ref[0:rank] = mm3(pair_matrix[0], leaf_path, True)
    for level in (1, 2):
        down_out.ref[level * rank : (level + 1) * rank] = mm3(
            mm3(pair_matrix[level], low[level], True), leaf_path, True
        )
    down_out.ref[3 * rank :] = mm3(low[3].T, leaf_path, True)
    down_out.send()
    leaf_ref, node_ref, coupling_ref = leaf_in(), node_in(), coupling_in()
    coupled = [mm3(node_ref[1], coupling_ref[0, 2], True), mm3(node_ref[0], coupling_ref[0, 2])]
    for j in range(2):
        left = slice(2 * j * rank, (2 * j + 1) * rank)
        right = slice((2 * j + 1) * rank, (2 * j + 2) * rank)
        link = coupling_ref[0, j]
        base_out.ref[:, left] = mm3(leaf_ref[:, right], link, True) + mm3(coupled[j], local_ref[0, 2 * j], True)
        base_out.ref[:, right] = mm3(leaf_ref[:, left], link) + mm3(coupled[j], local_ref[0, 2 * j + 1], True)
    base_out.send()


def first_kernel(got_ref, up_ref, send_ref, low_ref):
    rows = got_ref.shape[1] // 3
    one = [got_ref[k, :rows] for k in range(8)]
    two = [got_ref[k, rows : 2 * rows] for k in range(8)]
    top = [got_ref[k, 2 * rows :] for k in range(8)]
    for k in range(4):
        low_ref[k] = one[2 * k] + one[2 * k + 1]
    for k in range(2):
        low_ref[4 + k] = (two[4 * k] + two[4 * k + 1]) + (two[4 * k + 2] + two[4 * k + 3])
    total = ((top[0] + top[1]) + (top[2] + top[3])) + ((top[4] + top[5]) + (top[6] + top[7]))
    lifted = [mm3(total, up_ref[k]) for k in range(3)]
    me = lax.rem(lax.axis_index("group"), 2) * 4 + lax.div(lax.axis_index("dev"), 8)
    shares = [total, lifted[0], lifted[1]]
    levels = sibling_levels(8)
    for k in range(8):
        send_ref[me ^ k, :rows] = shares[levels[k]]
        send_ref[me ^ k, rows:] = lifted[2]


def second_kernel(got_ref, up_ref, send_ref):
    rows = got_ref.shape[1] // 2
    total = got_ref[0, rows:]
    for k in range(1, 8):
        total = total + got_ref[k, rows:]
    shares = [total, mm3(total, up_ref[0]), mm3(total, up_ref[1])]
    me = lax.div(lax.axis_index("group"), 2)
    levels = sibling_levels(8)
    for k in range(8):
        send_ref[me ^ k] = shares[levels[k]]


def sibling_sums(load, me):
    return [
        load(me ^ 1),
        load(me ^ 2) + load(me ^ 3),
        (load(me ^ 4) + load(me ^ 5)) + (load(me ^ 6) + load(me ^ 7)),
    ]


def third_kernel(got_mid_ref, got_ref, down_ref, low_ref, send_ref):
    rows = got_ref.shape[1]
    mid = lax.rem(lax.axis_index("group"), 2) * 4 + lax.div(lax.axis_index("dev"), 8)
    top = lax.div(lax.axis_index("group"), 2)
    sums = sibling_sums(lambda k: got_mid_ref[k, :rows], mid) + sibling_sums(lambda k: got_ref[k], top)
    field = mm3(sums[0], down_ref[0])
    for level in range(1, 6):
        field = field + mm3(sums[level], down_ref[level])
    for k in range(8):
        send_ref[k, :rows] = low_ref[(k // 2) ^ 1]
        send_ref[k, rows : 2 * rows] = low_ref[4 + ((k // 4) ^ 1)]
        send_ref[k, 2 * rows :] = field


def fall_kernel(got_in, zero_in, down_in, base_in, uexp_in, near_in, out):
    cols, rank = zero_in.ref.shape
    got_ref = got_in()
    rows = cols // 8
    sums = [got_ref[:, k * rows : (k + 1) * rows].reshape(cols, rank) for k in range(3)]
    sums = jnp.concatenate([zero_in()[...], *sums], axis=1)
    far = (mm3(sums, down_in()[...]) + base_in()[...]).astype(bf16)
    uexp_ref, near_ref = uexp_in(), near_in()
    step = 256
    for start in range(0, out.ref.shape[0], step):
        total = near_ref[start : start + step, :] + mm(uexp_ref[start : start + step, :], far, True)
        out.ref[start : start + step, :] = total.astype(bf16)
        out.send(start, step)


class Fetched:
    def __init__(self, source, ref, sem, lead):
        self.ref = ref
        self.copy = pltpu.make_async_copy(source if lead is None else source.at[pl.ds(*lead)], ref, sem)
        self.copy.start()
        self.here = False

    def __call__(self):
        if not self.here:
            self.copy.wait()
            self.here = True
        return self.ref


class Sent:
    def __init__(self, target, ref, sems):
        self.target, self.ref, self.sems, self.copies = target, ref, sems, []

    def send(self, start=0, size=None):
        rows = pl.ds(start, self.ref.shape[0] if size is None else size)
        copy = pltpu.make_async_copy(self.ref.at[rows], self.target.at[rows], self.sems.at[len(self.copies)])
        copy.start()
        self.copies.append(copy)

    def finish(self):
        if not self.copies:
            self.send()
        for copy in self.copies:
            copy.wait()


def call(kernel, outs, *args, flops=0, name=None, after=(), leads=None):
    leads = leads or {}
    shapes = [jax.ShapeDtypeStruct(shape, dtype) for shape, dtype in outs]
    moved = sum(a.size * a.dtype.itemsize for a in args)
    moved += sum(math.prod(s.shape) * s.dtype.itemsize for s in shapes)
    if after:
        args = (*lax.optimization_barrier((args[0], *after))[:1], *args[1:])
    count, made = len(args), len(outs)

    def run(*refs):
        places, targets, held = refs[:count], refs[count : count + made], refs[count + made :]
        sems, out_sems = held[count + made], held[count + made + 1]
        fetched = [Fetched(places[i], held[i], sems.at[i], leads.get(i)) for i in range(count)]
        sent = [Sent(targets[i], held[count + i], out_sems.at[i]) for i in range(made)]
        kernel(*fetched, *sent)
        for out in sent:
            if not out.copies:
                out.send()
        for arg in fetched:
            arg()
        for out in sent:
            out.finish()

    def lead_shape(i):
        shape = args[i].shape
        return (leads[i][1], *shape[1:]) if i in leads else shape

    result = pl.pallas_call(
        run,
        out_shape=shapes,
        in_specs=[pl.BlockSpec(memory_space=pl.ANY)] * count,
        out_specs=[pl.BlockSpec(memory_space=pl.ANY)] * made,
        scratch_shapes=[pltpu.VMEM(lead_shape(i), args[i].dtype) for i in range(count)]
        + [pltpu.VMEM(s.shape, s.dtype) for s in shapes]
        + [pltpu.SemaphoreType.DMA((count,)), pltpu.SemaphoreType.DMA((made, 8))],
        compiler_params=pltpu.CompilerParams(vmem_limit_bytes=62 * 1024 * 1024),
        cost_estimate=pl.CostEstimate(flops=flops, bytes_accessed=moved, transcendentals=0),
        name=name,
    )(*args)
    return result[0] if len(outs) == 1 else result


def small_call(kernel, outs, *args, flops=0, name=None, after=()):
    shapes = [jax.ShapeDtypeStruct(shape, dtype) for shape, dtype in outs]
    moved = sum(a.size * a.dtype.itemsize for a in args)
    moved += sum(math.prod(s.shape) * s.dtype.itemsize for s in shapes)
    if after:
        args = (*lax.optimization_barrier((args[0], *after))[:1], *args[1:])
    result = pl.pallas_call(
        kernel,
        out_shape=shapes,
        in_specs=[pl.BlockSpec(memory_space=pltpu.VMEM)] * len(args),
        out_specs=[pl.BlockSpec(memory_space=pltpu.VMEM)] * len(outs),
        compiler_params=pltpu.CompilerParams(vmem_limit_bytes=8 * 1024 * 1024),
        cost_estimate=pl.CostEstimate(flops=flops, bytes_accessed=moved, transcendentals=0),
        name=name,
    )(*args)
    return result[0] if len(outs) == 1 else result


def body(
    points, order, rhs, leaf_basis, local_transfer, local_coupling, cross_transfer, cross_coupling
):
    count, cols = rhs.shape
    leaves, size, rank = leaf_basis.shape
    slice_cols = cols // 8
    block = rank * rank
    y_groups = [[x * 8 + y for y in range(8)] for x in range(4)]
    mid_groups = [
        [(z * 2 + core) * 32 + x * 8 + y for core in range(2) for x in range(4)]
        for z in range(8)
        for y in range(8)
    ]
    z_groups = [[z * 2 + core for z in range(8)] for core in range(2)]

    uexp, member, leaf_nodes, nodes, zero_send, shares = call(
        rise_kernel,
        [
            ((count, leaves * rank), bf16),
            ((count, rank), bf16),
            ((cols, leaves * rank), f32),
            ((2, cols, rank), f32),
            ((cols, rank), f32),
            ((8, 3 * slice_cols, rank), f32),
        ],
        order,
        leaf_basis,
        rhs,
        local_transfer,
        cross_transfer,
        leads={4: (0, 3)},
        flops=2 * count * count * 2 * rank,
        name="rise",
    )

    got_first = lax.all_to_all(shares, "dev", 0, 0, tiled=True, axis_index_groups=y_groups)
    got_zero = lax.ppermute(zero_send, "dev", [(i, i ^ 1) for i in range(lax.axis_size("dev"))])
    up_low, up_high, down_mid, down, base = call(
        shadow_kernel,
        [
            ((3, rank, rank), f32),
            ((2, rank, rank), f32),
            ((6, rank, rank), f32),
            ((4 * rank, leaves * rank), f32),
            ((cols, leaves * rank), f32),
        ],
        cross_transfer,
        cross_coupling,
        local_transfer,
        local_coupling,
        leaf_nodes,
        nodes,
        flops=2 * 100 * block * rank,
        name="shadow",
    )
    first_send, low_sums = small_call(
        first_kernel,
        [((8, 2 * slice_cols, rank), f32), ((6, slice_cols, rank), f32)],
        got_first,
        up_low,
        flops=18 * slice_cols * block,
        name="first",
        after=[got_zero],
    )

    got_mid = lax.all_to_all(first_send, ("group", "dev"), 0, 0, tiled=True, axis_index_groups=mid_groups)
    near = call(
        near_kernel,
        [((count, cols), f32)],
        points,
        member,
        rhs,
        flops=2 * count * count * (cols + rank),
        name="near",
        after=[first_send],
    )
    second_send = small_call(
        second_kernel,
        [((8, slice_cols, rank), f32)],
        got_mid,
        up_high,
        flops=12 * slice_cols * block,
        name="second",
        after=[near],
    )
    got_top = lax.all_to_all(second_send, "group", 0, 0, tiled=True, axis_index_groups=z_groups)
    third_send = small_call(
        third_kernel,
        [((8, 3 * slice_cols, rank), f32)],
        got_mid,
        got_top,
        down_mid,
        low_sums,
        flops=36 * slice_cols * block,
        name="third",
    )
    got_low = lax.all_to_all(third_send, "dev", 0, 0, tiled=True, axis_index_groups=y_groups)
    return call(
        fall_kernel,
        [((count, cols), bf16)],
        got_low,
        got_zero,
        down,
        base,
        uexp,
        near,
        flops=2 * count * cols * leaves * rank,
        name="fall",
    )


def solution(mesh):
    placed = (
        P(None, ("group", "dev")),
        P(("group", "dev"), None),
        P(("group", "dev"), None),
        P(("group", "dev"), None, None),
        P(("group", "dev"), None, None, None),
        P(("group", "dev"), None, None, None),
        P(None, ("group", "dev"), None, None),
        P(None, ("group", "dev"), None, None),
    )
    return jax.shard_map(
        body, mesh=mesh, in_specs=placed, out_specs=P(("group", "dev"), None), check_vma=False
    )
```

time: 112 us -> 84.7 us (0.76)
  the two profiles are of different devices: /device:TPU:1 before, /device:TPU:2 now
where the time goes in v2:
time: 84.7 us; the launch traced here: 84.2 us
  blocking collectives  36.9 us (44%)
  Pallas kernels  24.3 us (29%)
  starting transfers between devices  15.9 us (19%)
  waiting for transfers between devices  6.05 us (7%)
  local copies, waits for them, and re-layouts  0.94 us (1%)
    pallas_call x4, Pallas kernels, call(): pl.pallas_call(run, out_shape=shapes, in_specs=[pl.BlockSpec(memory_space...  23 us
    all_to_all x1, blocking collectives, body(): lax.all_to_all(second_send, 'group', 0, 0, tiled=True, axis_index_groups=...  19.5 us
    all_to_all x1, blocking collectives, body(): lax.all_to_all(third_send, 'dev', 0, 0, tiled=True, axis_index_groups=y_g...  17.4 us
    all_to_all x1, starting transfers between devices, body(): lax.all_to_all(shares, 'dev', 0, 0, tiled=True, axis_index_groups=y_groups)  7.12 us
    all_to_all x1, starting transfers between devices, body(): lax.all_to_all(first_send, ('group', 'dev'), 0, 0, tiled=True, axis_index...  4.83 us
    ppermute x1, waiting for transfers between devices, body(): lax.ppermute(zero_send, 'dev', [(i, i ^ 1) for i in range(lax.axis_size('...  4.53 us
    ppermute x1, starting transfers between devices, body(): lax.ppermute(zero_send, 'dev', [(i, i ^ 1) for i in range(lax.axis_size('...  3.92 us
  transfers between devices with their start and end apart: 3, of which 2 were waited for; matrix products, arithmetic and copies ran while one was open for 0% of the time, Pallas kernels for 14%

profile of v2, /device:TPU:2, one launch (start us, length us, event | category | flops | bytes accessed | tf_op | source)
XLA Modules:
  0.0 84.2 jit_solution(2870027416554457722)
XLA Ops:
  0.0 6.4 %rise.1 = (bf16[2048,512]{1,0:T(8,128)(2,1)}, bf16[2048,128]{1,0:T(8,128)(2,1)}, f32[256,512]{1,0:T(8,128)}, f32[2,256,128]{2,1,0:T(8,128)}, f32[256,128]{1,0:T(8,128)}, /*index=5*/f32[8,96,128]{2,1,0:T(8,128)}) custom-call(s32[1,2048]{1,0:T(1,128)} %refs_0_.2, bf16[4,512,128]{2,1,0:T(8,128)(2,1)} %refs_1_.2, bf16[2048,256]{1,0:T(8,128)(2,1)} %refs_2_.5, ...), custom_call_target="tpu_custom_call" | custom-call | flops 2147483648 | bytes 6430720 | tf_op jit(solution)/shard_map/rise/pallas_call | solution.py:303
  6.4 7.1 %all-to-all-start = ((f32[8,96,128]{2,1,0:T(8,128)}), f32[8,96,128]{2,1,0:T(8,128)S(1)}, u32[]{:S(2)}, u32[]{:S(2)}) async-start(f32[8,96,128]{2,1,0:T(8,128)} %get-tuple-element.21), calls=%async_computation | async-start | bytes 786432 | tf_op jit(solution)/shard_map/all_to_all | solution.py:371
  13.6 3.9 %collective-permute-start = (f32[256,128]{1,0:T(8,128)}, f32[256,128]{1,0:T(8,128)S(1)}, u32[]{:S(2)}, u32[]{:S(2)}) collective-permute-start(f32[256,128]{1,0:T(8,128)} %get-tuple-element.22), channel_id=1, source_target_pairs={{0,1},{1,0},{2,3},{3,2},{4,5},{5,4},{6,7},{7,6},{8,9},{9,8},{10,11... | collective-permute-start | bytes 393224 | tf_op jit(solution)/shard_map/ppermute | solution.py:372
  17.5 5.1 %shadow.1 = (f32[3,128,128]{2,1,0:T(8,128)}, f32[2,128,128]{2,1,0:T(8,128)}, f32[6,128,128]{2,1,0:T(8,128)}, f32[512,512]{1,0:T(8,128)}, f32[256,512]{1,0:T(8,128)}) custom-call(f32[8,1,128,128]{3,2,1,0:T(8,128)} %refs_0_.3, f32[9,1,128,128]{3,2,1,0:T(8,128)} %refs_1_.3, f32[1,6,128,128]{3,2,1,0:T(8,128)} %refs_2_.4, f32[1,3,128,128]{3,2,1,0:T(8,128)} %refs_3_.3, ...), custom_call_target="tpu_custom_call" | custom-call | flops 419430400 | bytes 4784128 | tf_op jit(solution)/shard_map/shadow/pallas_call | solution.py:303
  22.6 4.5 %collective-permute-done.refs_1_ = f32[256,128]{1,0:T(8,128)S(1)} collective-permute-done((f32[256,128]{1,0:T(8,128)}, f32[256,128]{1,0:T(8,128)S(1)}, u32[]{:S(2)}, u32[]{:S(2)}) %collective-permute-start) | collective-permute-done | bytes 131104 | tf_op jit(solution)/shard_map/ppermute | solution.py:372
  27.2 0.0 copy-start.3
  27.2 1.5 %all-to-all-done.got_ref = f32[8,96,128]{2,1,0:T(8,128)S(1)} async-done(((f32[8,96,128]{2,1,0:T(8,128)}), f32[8,96,128]{2,1,0:T(8,128)S(1)}, u32[]{:S(2)}, u32[]{:S(2)}) %all-to-all-start) | async-done | bytes 393248 | tf_op jit(solution)/shard_map/all_to_all | solution.py:371
  28.7 0.0 copy-start.1
  28.7 0.9 %copy-done.1 = f32[3,128,128]{2,1,0:T(8,128)S(1)} copy-done((f32[3,128,128]{2,1,0:T(8,128)S(1)}, f32[3,128,128]{2,1,0:T(8,128)}, u32[]{:S(2)}) %copy-start.1) | copy-done | bytes 196632
  29.6 0.9 %first.1 = (f32[8,64,128]{2,1,0:T(8,128)}, f32[6,32,128]{2,1,0:T(8,128)S(1)}) custom-call(f32[8,96,128]{2,1,0:T(8,128)S(1)} %all-to-all-done.got_ref, f32[3,128,128]{2,1,0:T(8,128)S(1)} %copy-done.1), custom_call_target="tpu_custom_call" | custom-call | flops 9437184 | bytes 950272 | tf_op jit(solution)/shard_map/first/pallas_call | solution.py:324
  30.5 4.8 %all-to-all-start.1 = ((f32[8,64,128]{2,1,0:T(8,128)}), f32[8,64,128]{2,1,0:T(8,128)S(1)}, u32[]{:S(2)}, u32[]{:S(2)}) async-start(f32[8,64,128]{2,1,0:T(8,128)} %get-tuple-element.27), calls=%async_computation.1 | async-start | bytes 524288 | tf_op jit(solution)/shard_map/all_to_all | solution.py:401
  35.3 0.0 copy-start.2
  35.3 0.0 copy-start
  35.3 7.0 %near.1.refs_5_ = f32[2048,256]{1,0:T(8,128)} custom-call(f32[8,2048]{1,0:T(8,128)} %refs_0_.4, bf16[2048,128]{1,0:T(8,128)(2,1)} %get-tuple-element.29.refs_1_, bf16[2048,256]{1,0:T(8,128)(2,1)} %refs_2_.5), custom_call_target="tpu_custom_call" | custom-call | flops 3221225472 | bytes 3735552 | tf_op jit(solution)/shard_map/near/pallas_call | solution.py:303
  42.3 0.0 copy-done.3
  42.3 0.0 all-to-all-done.1.got_ref.got_mid_ref
  42.3 0.0 copy-done.2
  42.4 0.2 second.1
  42.5 19.5 %all_to_all.20.got_ref = f32[8,32,128]{2,1,0:T(8,128)S(1)} all-to-all(f32[8,32,128]{2,1,0:T(8,128)S(1)} %second.1), channel_id=1, replica_groups={{0,64,128,192,256,320,384,448},{32,96,160,224,288,352,416,480},{1,65,12..., dimensions={0} | all-to-all | bytes 262144 | tf_op jit(solution)/shard_map/all_to_all | solution.py:421
  62.0 0.0 copy-done
  62.0 0.2 third.1
  62.2 17.4 %all_to_all.21.refs_0_ = f32[8,96,128]{2,1,0:T(8,128)} all-to-all(f32[8,96,128]{2,1,0:T(8,128)S(1)} %third.1), channel_id=1, replica_groups={{0,1,2,3,4,5,6,7},{8,9,10,11,12,13,14,15},{16,17,18,19,20,21,22,23},{24..., dimensions={0} | all-to-all | bytes 786432 | tf_op jit(solution)/shard_map/all_to_all | solution.py:432
  79.7 4.5 %fall.1 = bf16[2048,256]{1,0:T(8,128)(2,1)} custom-call(f32[8,96,128]{2,1,0:T(8,128)} %all_to_all.21.refs_0_, f32[256,128]{1,0:T(8,128)} %copy-done.3, f32[512,512]{1,0:T(8,128)} %get-tuple-element.34.refs_2_, f32[256,512]{1,0:T(8,128)} %get-tuple-element.35.refs_3_, bf16[2048,512]{1,0:T(8,128)(2,1)} %get-tuple-element.36.refs_4_, f32[2048,256]{1,0:T(8,128)} %near.1.refs_5_), custom_call_target="tpu_custom_call" | custom-call | flops 536870912 | bytes 7340032 | tf_op jit(solution)/shard_map/fall/pallas_call | solution.py:303
Async XLA Ops:
  6.4 22.2 %all-to-all-start = ((f32[8,96,128]{2,1,0:T(8,128)}), f32[8,96,128]{2,1,0:T(8,128)S(1)}, u32[]{:S(2)}, u32[]{:S(2)}) async-start(f32[8,96,128]{2,1,0:T(8,128)} %get-tuple-element.21), calls=%async_computation | async-start | bytes 786432 | tf_op jit(solution)/shard_map/all_to_all | solution.py:371
  13.6 13.6 %collective-permute-start = (f32[256,128]{1,0:T(8,128)}, f32[256,128]{1,0:T(8,128)S(1)}, u32[]{:S(2)}, u32[]{:S(2)}) collective-permute-start(f32[256,128]{1,0:T(8,128)} %get-tuple-element.22), channel_id=1, source_target_pairs={{0,1},{1,0},{2,3},{3,2},{4,5},{5,4},{6,7},{7,6},{8,9},{9,8},{10,11... | collective-permute-start | bytes 393224 | tf_op jit(solution)/shard_map/ppermute | solution.py:372
  27.2 15.2 %copy-start.3 = (f32[256,128]{1,0:T(8,128)}, f32[256,128]{1,0:T(8,128)S(1)}, u32[]{:S(2)}) copy-start(f32[256,128]{1,0:T(8,128)S(1)} %collective-permute-done.refs_1_) | copy-start | bytes 393220
  28.7 0.9 %copy-start.1 = (f32[3,128,128]{2,1,0:T(8,128)S(1)}, f32[3,128,128]{2,1,0:T(8,128)}, u32[]{:S(2)}) copy-start(f32[3,128,128]{2,1,0:T(8,128)} %get-tuple-element.26.up_ref) | copy-start | bytes 589828
  30.5 11.8 %all-to-all-start.1 = ((f32[8,64,128]{2,1,0:T(8,128)}), f32[8,64,128]{2,1,0:T(8,128)S(1)}, u32[]{:S(2)}, u32[]{:S(2)}) async-start(f32[8,64,128]{2,1,0:T(8,128)} %get-tuple-element.27), calls=%async_computation.1 | async-start | bytes 524288 | tf_op jit(solution)/shard_map/all_to_all | solution.py:401
  35.3 7.0 %copy-start.2 = (f32[2,128,128]{2,1,0:T(8,128)S(1)}, f32[2,128,128]{2,1,0:T(8,128)}, u32[]{:S(2)}) copy-start(f32[2,128,128]{2,1,0:T(8,128)} %get-tuple-element.31.up_ref) | copy-start | bytes 393220
  35.3 26.7 %copy-start = (f32[6,128,128]{2,1,0:T(8,128)S(1)}, f32[6,128,128]{2,1,0:T(8,128)}, u32[]{:S(2)}) copy-start(f32[6,128,128]{2,1,0:T(8,128)} %get-tuple-element.32.down_ref) | copy-start | bytes 1179652

commit v3 on v2

--- a/solution.py
+++ b/solution.py
@@ -80,7 +80,7 @@
         send_out.ref[:, level * rows : (level + 1) * rows] = own.reshape(8, rows, rank)
 
 
-def near_kernel(points_in, member_in, rhs_in, near_out):
+def near_kernel(first_row, points_in, member_in, rhs_in, near_out):
     points_ref, member_ref = points_in(), member_in()
     points = points_ref.shape[1]
     scale = math.sqrt(2.0 * kernel_rate / math.log(2.0))
@@ -112,13 +112,14 @@
     left = left.T.astype(bf16)
     rhs_ref, near_ref = rhs_in(), near_out.ref
     step, chunk = 256, 512
-    for start in range(0, points, step):
+    for out_row in range(0, near_ref.shape[0], step):
+        start = first_row + out_row
         total = rhs_ref[start : start + step, :].astype(f32)
         for base in range(0, points, chunk):
             power = mm(left[start : start + step], right[:, base : base + chunk])
             total = total + mm(jnp.exp2(power).astype(bf16), rhs_ref[base : base + chunk, :])
-        near_ref[start : start + step, :] = total
-        near_out.send(start, step)
+        near_ref[out_row : out_row + step, :] = total
+        near_out.send(out_row, step)
 
 
 def turn(left, matrix):
@@ -156,12 +157,13 @@
     for j in range(4):
         leaf_path.append(mm3(local_ref[0, j], local_ref[0, 4 + j // 2]))
     leaf_path = jnp.concatenate(leaf_path, axis=0)
-    down_out.ref[0:rank] = mm3(pair_matrix[0], leaf_path, True)
+    down = [mm3(pair_matrix[0], leaf_path, True)]
     for level in (1, 2):
-        down_out.ref[level * rank : (level + 1) * rank] = mm3(
-            mm3(pair_matrix[level], low[level], True), leaf_path, True
-        )
-    down_out.ref[3 * rank :] = mm3(low[3].T, leaf_path, True)
+        down.append(mm3(mm3(pair_matrix[level], low[level], True), leaf_path, True))
+    down.append(mm3(low[3].T, leaf_path, True))
+    for k in range(4):
+        rows = slice(k * rank, (k + 1) * rank)
+        down_out.ref[rows], down_out.ref[4 * rank + k * rank : 5 * rank + k * rank] = split(down[k])
     down_out.send()
     leaf_ref, node_ref, coupling_ref = leaf_in(), node_in(), coupling_in()
     coupled = [mm3(node_ref[1], coupling_ref[0, 2], True), mm3(node_ref[0], coupling_ref[0, 2])]
@@ -227,17 +229,23 @@
         send_ref[k, 2 * rows :] = field
 
 
-def fall_kernel(got_in, zero_in, down_in, base_in, uexp_in, near_in, out):
+def fall_kernel(got_in, zero_in, down_in, base_in, uexp_in, near_low_in, near_high_in, out):
     cols, rank = zero_in.ref.shape
     got_ref = got_in()
     rows = cols // 8
     sums = [got_ref[:, k * rows : (k + 1) * rows].reshape(cols, rank) for k in range(3)]
     sums = jnp.concatenate([zero_in()[...], *sums], axis=1)
-    far = (mm3(sums, down_in()[...]) + base_in()[...]).astype(bf16)
-    uexp_ref, near_ref = uexp_in(), near_in()
+    high, low = split(sums)
+    down_ref = down_in()
+    depth = sums.shape[1]
+    far = mm(high, down_ref[:depth]) + (mm(low, down_ref[:depth]) + mm(high, down_ref[depth:]))
+    far = (far + base_in()[...]).astype(bf16)
+    uexp_ref = uexp_in()
     step = 256
+    half = out.ref.shape[0] // 2
     for start in range(0, out.ref.shape[0], step):
-        total = near_ref[start : start + step, :] + mm(uexp_ref[start : start + step, :], far, True)
+        near_ref, base = (near_low_in(), start) if start < half else (near_high_in(), start - half)
+        total = near_ref[base : base + step, :] + mm(uexp_ref[start : start + step, :], far, True)
         out.ref[start : start + step, :] = total.astype(bf16)
         out.send(start, step)
 
@@ -368,15 +376,26 @@
         name="rise",
     )
 
+    def near_half(first_row, after):
+        return call(
+            functools.partial(near_kernel, first_row),
+            [((count // 2, cols), f32)],
+            points,
+            member,
+            rhs,
+            flops=count * count * (cols + rank),
+            name="near",
+            after=after,
+        )
+
     got_first = lax.all_to_all(shares, "dev", 0, 0, tiled=True, axis_index_groups=y_groups)
-    got_zero = lax.ppermute(zero_send, "dev", [(i, i ^ 1) for i in range(lax.axis_size("dev"))])
     up_low, up_high, down_mid, down, base = call(
         shadow_kernel,
         [
             ((3, rank, rank), f32),
             ((2, rank, rank), f32),
             ((6, rank, rank), f32),
-            ((4 * rank, leaves * rank), f32),
+            ((8 * rank, leaves * rank), bf16),
             ((cols, leaves * rank), f32),
         ],
         cross_transfer,
@@ -388,6 +407,7 @@
         flops=2 * 100 * block * rank,
         name="shadow",
     )
+    near_low = near_half(0, [up_low])
     first_send, low_sums = small_call(
         first_kernel,
         [((8, 2 * slice_cols, rank), f32), ((6, slice_cols, rank), f32)],
@@ -395,20 +415,11 @@
         up_low,
         flops=18 * slice_cols * block,
         name="first",
-        after=[got_zero],
+        after=[near_low],
     )
 
     got_mid = lax.all_to_all(first_send, ("group", "dev"), 0, 0, tiled=True, axis_index_groups=mid_groups)
-    near = call(
-        near_kernel,
-        [((count, cols), f32)],
-        points,
-        member,
-        rhs,
-        flops=2 * count * count * (cols + rank),
-        name="near",
-        after=[first_send],
-    )
+    near_high = near_half(count // 2, [first_send])
     second_send = small_call(
         second_kernel,
         [((8, slice_cols, rank), f32)],
@@ -416,9 +427,12 @@
         up_high,
         flops=12 * slice_cols * block,
         name="second",
-        after=[near],
-    )
+        after=[near_high],
+    )
+
     got_top = lax.all_to_all(second_send, "group", 0, 0, tiled=True, axis_index_groups=z_groups)
+    zero_send, _ = lax.optimization_barrier((zero_send, second_send))
+    got_zero = lax.ppermute(zero_send, "dev", [(i, i ^ 1) for i in range(lax.axis_size("dev"))])
     third_send = small_call(
         third_kernel,
         [((8, 3 * slice_cols, rank), f32)],
@@ -428,6 +442,7 @@
         low_sums,
         flops=36 * slice_cols * block,
         name="third",
+        after=[got_zero],
     )
     got_low = lax.all_to_all(third_send, "dev", 0, 0, tiled=True, axis_index_groups=y_groups)
     return call(
@@ -438,7 +453,8 @@
         down,
         base,
         uexp,
-        near,
+        near_low,
+        near_high,
         flops=2 * count * cols * leaves * rank,
         name="fall",
     )

time: 84.7 us -> 82 us (0.968)
  blocking collectives: 36.9 us -> 16.6 us
  starting transfers between devices: 15.9 us -> 24.7 us
  waiting for transfers between devices: 6.05 us -> 12.6 us
  Pallas kernels: 24.3 us -> 27.4 us
  local copies, waits for them, and re-layouts: 0.94 us -> 0.02 us
    all_to_all x1 -> x0, blocking collectives: 19.5 us -> none  [body(): lax.all_to_all(second_send, 'group', 0, 0, tiled=True, axis_index_groups=...]
    all_to_all x0 -> x1, starting transfers between devices: none -> 10.3 us  [body(): lax.all_to_all(second_send, 'group', 0, 0, tiled=True, axis_index_groups=...]
    all_to_all x1, waiting for transfers between devices: 1.51 us -> 4.76 us  [body(): lax.all_to_all(shares, 'dev', 0, 0, tiled=True, axis_index_groups=y_groups)]
    pallas_call x4 -> x5, Pallas kernels: 23 us -> 25.5 us  [call(): pl.pallas_call(run, out_shape=shapes, in_specs=[pl.BlockSpec(memory_space...]
    all_to_all x0 -> x1, waiting for transfers between devices: none -> 2.21 us  [body(): lax.all_to_all(second_send, 'group', 0, 0, tiled=True, axis_index_groups=...]
    ppermute x1, starting transfers between devices: 3.92 us -> 2.47 us  [body(): lax.ppermute(zero_send, 'dev', [(i, i ^ 1) for i in range(lax.axis_size('...]
    unnamed x8 -> x10, local copies, waits for them, and re-layouts: 0.94 us -> 0.02 us
    all_to_all x1, waiting for transfers between devices: 0.01 us -> 0.9 us  [body(): lax.all_to_all(first_send, ('group', 'dev'), 0, 0, tiled=True, axis_index...]
  transfers between devices with their start and end apart: 3 -> 4, of which waited for: 2 -> 4; matrix products, arithmetic and copies ran while one was open for 0% -> 0% of each run, Pallas kernels for 14% -> 18%
where the time goes in v3:
time: 82 us; the launch traced here: 81.4 us
  Pallas kernels  27.4 us (33%)
  starting transfers between devices  24.7 us (30%)
  blocking collectives  16.6 us (20%)
  waiting for transfers between devices  12.6 us (15%)
    pallas_call x5, Pallas kernels, call(): pl.pallas_call(run, out_shape=shapes, in_specs=[pl.BlockSpec(memory_space...  25.5 us
    all_to_all x1, blocking collectives, body(): lax.all_to_all(third_send, 'dev', 0, 0, tiled=True, axis_index_groups=y_g...  16.6 us
    all_to_all x1, starting transfers between devices, body(): lax.all_to_all(second_send, 'group', 0, 0, tiled=True, axis_index_groups=...  10.3 us
    all_to_all x1, starting transfers between devices, body(): lax.all_to_all(shares, 'dev', 0, 0, tiled=True, axis_index_groups=y_groups)  7.12 us
    all_to_all x1, starting transfers between devices, body(): lax.all_to_all(first_send, ('group', 'dev'), 0, 0, tiled=True, axis_index...  4.82 us
    all_to_all x1, waiting for transfers between devices, body(): lax.all_to_all(shares, 'dev', 0, 0, tiled=True, axis_index_groups=y_groups)  4.76 us
    ppermute x1, waiting for transfers between devices, body(): lax.ppermute(zero_send, 'dev', [(i, i ^ 1) for i in range(lax.axis_size('...  4.71 us
    ppermute x1, starting transfers between devices, body(): lax.ppermute(zero_send, 'dev', [(i, i ^ 1) for i in range(lax.axis_size('...  2.47 us
  transfers between devices with their start and end apart: 4, of which 4 were waited for; matrix products, arithmetic and copies ran while one was open for 0% of the time, Pallas kernels for 18%

profile of v3, /device:TPU:2, one launch (start us, length us, event | category | flops | bytes accessed | tf_op | source)
XLA Modules:
  0.0 81.4 jit_solution(12617083039389122633)
XLA Ops:
  0.0 6.4 %rise.1 = (bf16[2048,512]{1,0:T(8,128)(2,1)}, bf16[2048,128]{1,0:T(8,128)(2,1)}, f32[256,512]{1,0:T(8,128)}, f32[2,256,128]{2,1,0:T(8,128)}, f32[256,128]{1,0:T(8,128)}, /*index=5*/f32[8,96,128]{2,1,0:T(8,128)}) custom-call(s32[1,2048]{1,0:T(1,128)} %refs_0_.2, bf16[4,512,128]{2,1,0:T(8,128)(2,1)} %refs_1_.2, bf16[2048,256]{1,0:T(8,128)(2,1)} %refs_2_.7, ...), custom_call_target="tpu_custom_call" | custom-call | flops 2147483648 | bytes 6430720 | tf_op jit(solution)/shard_map/rise/pallas_call | solution.py:311
  6.4 7.1 %all-to-all-start = ((f32[8,96,128]{2,1,0:T(8,128)}), f32[8,96,128]{2,1,0:T(8,128)S(1)}, u32[]{:S(2)}, u32[]{:S(2)}) async-start(f32[8,96,128]{2,1,0:T(8,128)} %get-tuple-element.24), calls=%async_computation | async-start | bytes 786432 | tf_op jit(solution)/shard_map/all_to_all | solution.py:391
  13.6 5.1 %shadow.1 = (f32[3,128,128]{2,1,0:T(8,128)}, f32[2,128,128]{2,1,0:T(8,128)}, f32[6,128,128]{2,1,0:T(8,128)}, bf16[1024,512]{1,0:T(8,128)(2,1)}, f32[256,512]{1,0:T(8,128)}) custom-call(f32[8,1,128,128]{3,2,1,0:T(8,128)} %refs_0_.3, f32[9,1,128,128]{3,2,1,0:T(8,128)} %refs_1_.3, f32[1,6,128,128]{3,2,1,0:T(8,128)} %refs_2_.5, f32[1,3,128,128]{3,2,1,0:T(8,128)} %refs_3_.3, ...), custom_call_target="tpu_custom_call" | custom-call | flops 419430400 | bytes 4784128 | tf_op jit(solution)/shard_map/shadow/pallas_call | solution.py:311
  18.7 0.0 copy-start.1
  18.7 4.8 %near.2.refs_5_ = f32[1024,256]{1,0:T(8,128)} custom-call(f32[8,2048]{1,0:T(8,128)} %refs_0_.5, bf16[2048,128]{1,0:T(8,128)(2,1)} %get-tuple-element.29.refs_1_, bf16[2048,256]{1,0:T(8,128)(2,1)} %refs_2_.7), custom_call_target="tpu_custom_call" | custom-call | flops 1610612736 | bytes 2686976 | tf_op jit(solution)/shard_map/near/pallas_call | solution.py:311
  23.5 4.8 %all-to-all-done.got_ref = f32[8,96,128]{2,1,0:T(8,128)S(1)} async-done(((f32[8,96,128]{2,1,0:T(8,128)}), f32[8,96,128]{2,1,0:T(8,128)S(1)}, u32[]{:S(2)}, u32[]{:S(2)}) %all-to-all-start) | async-done | bytes 393248 | tf_op jit(solution)/shard_map/all_to_all | solution.py:391
  28.3 0.0 copy-done.1
  28.3 0.9 %first.1 = (f32[8,64,128]{2,1,0:T(8,128)}, f32[6,32,128]{2,1,0:T(8,128)S(1)}) custom-call(f32[8,96,128]{2,1,0:T(8,128)S(1)} %all-to-all-done.got_ref, f32[3,128,128]{2,1,0:T(8,128)S(1)} %copy-done.1), custom_call_target="tpu_custom_call" | custom-call | flops 9437184 | bytes 950272 | tf_op jit(solution)/shard_map/first/pallas_call | solution.py:332
  29.1 4.8 %all-to-all-start.1 = ((f32[8,64,128]{2,1,0:T(8,128)}), f32[8,64,128]{2,1,0:T(8,128)S(1)}, u32[]{:S(2)}, u32[]{:S(2)}) async-start(f32[8,64,128]{2,1,0:T(8,128)} %get-tuple-element.31), calls=%async_computation.1 | async-start | bytes 524288 | tf_op jit(solution)/shard_map/all_to_all | solution.py:421
  34.0 0.0 copy-start.2
  34.0 0.0 copy-start.4
  34.0 0.0 copy-start
  34.0 4.8 %near.3.refs_6_ = f32[1024,256]{1,0:T(8,128)} custom-call(f32[8,2048]{1,0:T(8,128)} %refs_0_.5, bf16[2048,128]{1,0:T(8,128)(2,1)} %get-tuple-element.29.refs_1_, bf16[2048,256]{1,0:T(8,128)(2,1)} %refs_2_.7), custom_call_target="tpu_custom_call" | custom-call | flops 1610612736 | bytes 2686976 | tf_op jit(solution)/shard_map/near/pallas_call | solution.py:311
  38.8 0.9 %all-to-all-done.1.got_ref.got_mid_ref = f32[8,64,128]{2,1,0:T(8,128)S(1)} async-done(((f32[8,64,128]{2,1,0:T(8,128)}), f32[8,64,128]{2,1,0:T(8,128)S(1)}, u32[]{:S(2)}, u32[]{:S(2)}) %all-to-all-start.1) | async-done | bytes 262176 | tf_op jit(solution)/shard_map/all_to_all | solution.py:421
  39.7 0.0 copy-done.2
  39.7 0.8 %second.1 = f32[8,32,128]{2,1,0:T(8,128)} custom-call(f32[8,64,128]{2,1,0:T(8,128)S(1)} %all-to-all-done.1.got_ref.got_mid_ref, f32[2,128,128]{2,1,0:T(8,128)S(1)} %copy-done.2), custom_call_target="tpu_custom_call" | custom-call | flops 6291456 | bytes 524288 | tf_op jit(solution)/shard_map/second/pallas_call | solution.py:332
  40.5 10.3 %all-to-all-start.2 = ((f32[8,32,128]{2,1,0:T(8,128)}), f32[8,32,128]{2,1,0:T(8,128)S(1)}, u32[]{:S(2)}, u32[]{:S(2)}) async-start(f32[8,32,128]{2,1,0:T(8,128)} %second.1), calls=%async_computation.2 | async-start | bytes 262144 | tf_op jit(solution)/shard_map/all_to_all | solution.py:433
  50.8 0.0 copy-done.4
  50.8 2.5 %collective-permute-start = (f32[256,128]{1,0:T(8,128)S(1)}, f32[256,128]{1,0:T(8,128)S(1)}, u32[]{:S(2)}, u32[]{:S(2)}) collective-permute-start(f32[256,128]{1,0:T(8,128)S(1)} %copy-done.4), channel_id=1, source_target_pairs={{0,1},{1,0},{2,3},{3,2},{4,5},{5,4},{6,7},{7,6},{8,9},{9,8},{10,11... | collective-permute-start | bytes 393224 | tf_op jit(solution)/shard_map/ppermute | solution.py:435
  53.3 4.7 %collective-permute-done.refs_1_ = f32[256,128]{1,0:T(8,128)S(1)} collective-permute-done((f32[256,128]{1,0:T(8,128)S(1)}, f32[256,128]{1,0:T(8,128)S(1)}, u32[]{:S(2)}, u32[]{:S(2)}) %collective-permute-start) | collective-permute-done | bytes 131104 | tf_op jit(solution)/shard_map/ppermute | solution.py:435
  58.0 0.0 copy-start.3
  58.0 2.2 %all-to-all-done.2.got_ref = f32[8,32,128]{2,1,0:T(8,128)S(1)} async-done(((f32[8,32,128]{2,1,0:T(8,128)}), f32[8,32,128]{2,1,0:T(8,128)S(1)}, u32[]{:S(2)}, u32[]{:S(2)}) %all-to-all-start.2) | async-done | bytes 131104 | tf_op jit(solution)/shard_map/all_to_all | solution.py:433
  60.2 0.0 copy-done
  60.3 0.2 third.1
  60.5 16.6 %all_to_all.20.refs_0_ = f32[8,96,128]{2,1,0:T(8,128)} all-to-all(f32[8,96,128]{2,1,0:T(8,128)S(1)} %third.1), channel_id=1, replica_groups={{0,1,2,3,4,5,6,7},{8,9,10,11,12,13,14,15},{16,17,18,19,20,21,22,23},{24..., dimensions={0} | all-to-all | bytes 786432 | tf_op jit(solution)/shard_map/all_to_all | solution.py:447
  77.1 0.0 copy-done.3
  77.1 4.3 %fall.1 = bf16[2048,256]{1,0:T(8,128)(2,1)} custom-call(f32[8,96,128]{2,1,0:T(8,128)} %all_to_all.20.refs_0_, f32[256,128]{1,0:T(8,128)} %copy-done.3, bf16[1024,512]{1,0:T(8,128)(2,1)} %get-tuple-element.40.refs_2_, f32[256,512]{1,0:T(8,128)} %get-tuple-element.41.refs_3_, bf16[2048,512]{1,0:T(8,128)(2,1)} %get-tuple-element.42.refs_4_, ...), custom_call_target="tpu_custom_call" | custom-call | flops 536870912 | bytes 7340032 | tf_op jit(solution)/shard_map/fall/pallas_call | solution.py:311
Async XLA Ops:
  6.4 21.8 %all-to-all-start = ((f32[8,96,128]{2,1,0:T(8,128)}), f32[8,96,128]{2,1,0:T(8,128)S(1)}, u32[]{:S(2)}, u32[]{:S(2)}) async-start(f32[8,96,128]{2,1,0:T(8,128)} %get-tuple-element.24), calls=%async_computation | async-start | bytes 786432 | tf_op jit(solution)/shard_map/all_to_all | solution.py:391
  18.7 9.6 %copy-start.1 = (f32[3,128,128]{2,1,0:T(8,128)S(1)}, f32[3,128,128]{2,1,0:T(8,128)}, u32[]{:S(2)}) copy-start(f32[3,128,128]{2,1,0:T(8,128)} %get-tuple-element.27.up_ref) | copy-start | bytes 589828
  29.1 10.6 %all-to-all-start.1 = ((f32[8,64,128]{2,1,0:T(8,128)}), f32[8,64,128]{2,1,0:T(8,128)S(1)}, u32[]{:S(2)}, u32[]{:S(2)}) async-start(f32[8,64,128]{2,1,0:T(8,128)} %get-tuple-element.31), calls=%async_computation.1 | async-start | bytes 524288 | tf_op jit(solution)/shard_map/all_to_all | solution.py:421
  34.0 5.7 %copy-start.2 = (f32[2,128,128]{2,1,0:T(8,128)S(1)}, f32[2,128,128]{2,1,0:T(8,128)}, u32[]{:S(2)}) copy-start(f32[2,128,128]{2,1,0:T(8,128)} %get-tuple-element.35.up_ref) | copy-start | bytes 393220
  34.0 16.9 %copy-start.4 = (f32[256,128]{1,0:T(8,128)S(1)}, f32[256,128]{1,0:T(8,128)}, u32[]{:S(2)}) copy-start(f32[256,128]{1,0:T(8,128)} %get-tuple-element.36) | copy-start | bytes 393220
  34.0 26.3 %copy-start = (f32[6,128,128]{2,1,0:T(8,128)S(1)}, f32[6,128,128]{2,1,0:T(8,128)}, u32[]{:S(2)}) copy-start(f32[6,128,128]{2,1,0:T(8,128)} %get-tuple-element.38.down_ref) | copy-start | bytes 1179652
  40.5 19.7 %all-to-all-start.2 = ((f32[8,32,128]{2,1,0:T(8,128)}), f32[8,32,128]{2,1,0:T(8,128)S(1)}, u32[]{:S(2)}, u32[]{:S(2)}) async-start(f32[8,32,128]{2,1,0:T(8,128)} %second.1), calls=%async_computation.2 | async-start | bytes 262144 | tf_op jit(solution)/shard_map/all_to_all | solution.py:433
  50.8 7.2 %collective-permute-start = (f32[256,128]{1,0:T(8,128)S(1)}, f32[256,128]{1,0:T(8,128)S(1)}, u32[]{:S(2)}, u32[]{:S(2)}) collective-permute-start(f32[256,128]{1,0:T(8,128)S(1)} %copy-done.4), channel_id=1, source_target_pairs={{0,1},{1,0},{2,3},{3,2},{4,5},{5,4},{6,7},{7,6},{8,9},{9,8},{10,11... | collective-permute-start | bytes 393224 | tf_op jit(solution)/shard_map/ppermute | solution.py:435
  58.0 19.1 %copy-start.3 = (f32[256,128]{1,0:T(8,128)}, f32[256,128]{1,0:T(8,128)S(1)}, u32[]{:S(2)}) copy-start(f32[256,128]{1,0:T(8,128)S(1)} %collective-permute-done.refs_1_) | copy-start | bytes 393220

commit v4 on v3

--- a/solution.py
+++ b/solution.py
@@ -38,7 +38,7 @@
     return [0] + [k.bit_length() - 1 for k in range(1, width)]
 
 
-def rise_kernel(order_in, basis_in, rhs_in, local_in, edge_in, uexp_out, member_out, leaf_out, node_out, zero_out, send_out):
+def rise_kernel(order_in, basis_in, rhs_in, local_in, edge_in, uexp_out, member_out, leaf_out, node_out, zero_out, edge_out, send_out):
     order_ref, basis_ref = order_in(), basis_in()
     uexp_ref, member_ref = uexp_out.ref, member_out.ref
     points = order_ref.shape[1]
@@ -63,6 +63,8 @@
         uexp_out.send(start, step)
         member_out.send(start, step)
     local_ref, edge_ref = local_in(), edge_in()
+    edge_out.ref[...] = edge_ref[2, 0]
+    edge_out.send()
     coefficients = mm(rhs_in()[...].T, uexp_ref[...])
     cols = coefficients.shape[0]
     leaf_out.ref[...] = coefficients
@@ -75,7 +77,7 @@
     zero_out.ref[...] = own
     zero_out.send()
     rows = cols // 8
-    for level in range(3):
+    for level in range(2):
         own = mm3(own, edge_ref[level, 0])
         send_out.ref[:, level * rows : (level + 1) * rows] = own.reshape(8, rows, rank)
 
@@ -127,7 +129,7 @@
 
 
 def shadow_kernel(
-    edge_in, link_in, local_in, coupling_in, leaf_in, node_in, up_low_out, up_high_out, down_mid_out, down_out, base_out
+    edge_in, link_in, local_in, coupling_in, leaf_in, node_in, down_mid_out, down_out, base_out
 ):
     edge_ref, link_ref, local_ref = edge_in(), link_in(), local_in()
     levels = link_ref.shape[0]
@@ -140,30 +142,24 @@
     path = {4: edge[3]}
     for level in range(5, levels):
         path[level] = mm3(path[level - 1], edge[level - 1])
-    for level in range(4, 7):
-        up_low_out.ref[level - 4] = path[level]
-    up_low_out.send()
-    up_high_out.ref[0] = edge[6]
-    up_high_out.ref[1] = mm3(edge[6], edge[7])
-    up_high_out.send()
     down_mid_out.ref[0] = pair_matrix[3]
     for level in range(4, levels):
         down_mid_out.ref[level - 3] = mm3(pair_matrix[level], path[level], True)
+    down_mid_out.ref[6] = edge[2]
+    down_mid_out.ref[7] = link_ref[2, 0]
     down_mid_out.send()
-    low = {1: edge[0]}
-    low[2] = mm3(low[1], edge[1])
-    low[3] = mm3(low[2], edge[2])
     leaf_path = []
     for j in range(4):
         leaf_path.append(mm3(local_ref[0, j], local_ref[0, 4 + j // 2]))
     leaf_path = jnp.concatenate(leaf_path, axis=0)
-    down = [mm3(pair_matrix[0], leaf_path, True)]
-    for level in (1, 2):
-        down.append(mm3(mm3(pair_matrix[level], low[level], True), leaf_path, True))
-    down.append(mm3(low[3].T, leaf_path, True))
-    for k in range(4):
+    down = [
+        mm3(pair_matrix[0], leaf_path, True),
+        mm3(mm3(pair_matrix[1], edge[0], True), leaf_path, True),
+        mm3(mm3(edge[0], edge[1]).T, leaf_path, True),
+    ]
+    for k in range(3):
         rows = slice(k * rank, (k + 1) * rank)
-        down_out.ref[rows], down_out.ref[4 * rank + k * rank : 5 * rank + k * rank] = split(down[k])
+        down_out.ref[rows], down_out.ref[3 * rank + k * rank : 4 * rank + k * rank] = split(down[k])
     down_out.send()
     leaf_ref, node_ref, coupling_ref = leaf_in(), node_in(), coupling_in()
     coupled = [mm3(node_ref[1], coupling_ref[0, 2], True), mm3(node_ref[0], coupling_ref[0, 2])]
@@ -176,31 +172,38 @@
     base_out.send()
 
 
-def first_kernel(got_ref, up_ref, send_ref, low_ref):
-    rows = got_ref.shape[1] // 3
+def half_edges(own, other):
+    left = lax.rem(lax.axis_index("dev"), 8) < 4
+    return jnp.where(left, own, other), jnp.where(left, other, own)
+
+
+def first_kernel(got_ref, edge_ref, other_ref, send_ref, low_ref):
+    rows = got_ref.shape[1] // 2
     one = [got_ref[k, :rows] for k in range(8)]
-    two = [got_ref[k, rows : 2 * rows] for k in range(8)]
-    top = [got_ref[k, 2 * rows :] for k in range(8)]
+    two = [got_ref[k, rows:] for k in range(8)]
     for k in range(4):
         low_ref[k] = one[2 * k] + one[2 * k + 1]
+    halves = [(two[4 * k] + two[4 * k + 1]) + (two[4 * k + 2] + two[4 * k + 3]) for k in range(2)]
     for k in range(2):
-        low_ref[4 + k] = (two[4 * k] + two[4 * k + 1]) + (two[4 * k + 2] + two[4 * k + 3])
-    total = ((top[0] + top[1]) + (top[2] + top[3])) + ((top[4] + top[5]) + (top[6] + top[7]))
-    lifted = [mm3(total, up_ref[k]) for k in range(3)]
+        low_ref[4 + k] = halves[k]
+    left, right = half_edges(edge_ref[2, 0], other_ref[...])
+    shares = [mm3(halves[0], left) + mm3(halves[1], right)]
+    for level in (3, 4, 5):
+        shares.append(mm3(shares[-1], edge_ref[level, 0]))
     me = lax.rem(lax.axis_index("group"), 2) * 4 + lax.div(lax.axis_index("dev"), 8)
-    shares = [total, lifted[0], lifted[1]]
     levels = sibling_levels(8)
     for k in range(8):
         send_ref[me ^ k, :rows] = shares[levels[k]]
-        send_ref[me ^ k, rows:] = lifted[2]
-
-
-def second_kernel(got_ref, up_ref, send_ref):
+        send_ref[me ^ k, rows:] = shares[3]
+
+
+def second_kernel(got_ref, edge_ref, send_ref):
     rows = got_ref.shape[1] // 2
     total = got_ref[0, rows:]
     for k in range(1, 8):
         total = total + got_ref[k, rows:]
-    shares = [total, mm3(total, up_ref[0]), mm3(total, up_ref[1])]
+    shares = [total, mm3(total, edge_ref[6, 0])]
+    shares.append(mm3(shares[1], edge_ref[7, 0]))
     me = lax.div(lax.axis_index("group"), 2)
     levels = sibling_levels(8)
     for k in range(8):
@@ -215,7 +218,7 @@
     ]
 
 
-def third_kernel(got_mid_ref, got_ref, down_ref, low_ref, send_ref):
+def third_kernel(got_mid_ref, got_ref, down_ref, other_ref, low_ref, send_ref):
     rows = got_ref.shape[1]
     mid = lax.rem(lax.axis_index("group"), 2) * 4 + lax.div(lax.axis_index("dev"), 8)
     top = lax.div(lax.axis_index("group"), 2)
@@ -223,17 +226,22 @@
     field = mm3(sums[0], down_ref[0])
     for level in range(1, 6):
         field = field + mm3(sums[level], down_ref[level])
+    left, right = half_edges(down_ref[6], other_ref[...])
+    link = down_ref[7]
+    fields = [
+        mm3(low_ref[5], link, True) + mm3(field, left, True),
+        mm3(low_ref[4], link) + mm3(field, right, True),
+    ]
     for k in range(8):
         send_ref[k, :rows] = low_ref[(k // 2) ^ 1]
-        send_ref[k, rows : 2 * rows] = low_ref[4 + ((k // 4) ^ 1)]
-        send_ref[k, 2 * rows :] = field
+        send_ref[k, rows:] = fields[k // 4]
 
 
 def fall_kernel(got_in, zero_in, down_in, base_in, uexp_in, near_low_in, near_high_in, out):
     cols, rank = zero_in.ref.shape
     got_ref = got_in()
     rows = cols // 8
-    sums = [got_ref[:, k * rows : (k + 1) * rows].reshape(cols, rank) for k in range(3)]
+    sums = [got_ref[:, k * rows : (k + 1) * rows].reshape(cols, rank) for k in range(2)]
     sums = jnp.concatenate([zero_in()[...], *sums], axis=1)
     high, low = split(sums)
     down_ref = down_in()
@@ -341,6 +349,10 @@
     return result[0] if len(outs) == 1 else result
 
 
+def swap(block, stride):
+    return lax.ppermute(block, "dev", [(i, i ^ stride) for i in range(lax.axis_size("dev"))])
+
+
 def body(
     points, order, rhs, leaf_basis, local_transfer, local_coupling, cross_transfer, cross_coupling
 ):
@@ -356,7 +368,7 @@
     ]
     z_groups = [[z * 2 + core for z in range(8)] for core in range(2)]
 
-    uexp, member, leaf_nodes, nodes, zero_send, shares = call(
+    uexp, member, leaf_nodes, nodes, zero_send, edge_send, shares = call(
         rise_kernel,
         [
             ((count, leaves * rank), bf16),
@@ -364,7 +376,8 @@
             ((cols, leaves * rank), f32),
             ((2, cols, rank), f32),
             ((cols, rank), f32),
-            ((8, 3 * slice_cols, rank), f32),
+            ((rank, rank), f32),
+            ((8, 2 * slice_cols, rank), f32),
         ],
         order,
         leaf_basis,
@@ -389,13 +402,12 @@
         )
 
     got_first = lax.all_to_all(shares, "dev", 0, 0, tiled=True, axis_index_groups=y_groups)
-    up_low, up_high, down_mid, down, base = call(
+    got_edge = swap(edge_send, 7)
+    down_mid, down, base = call(
         shadow_kernel,
         [
-            ((3, rank, rank), f32),
-            ((2, rank, rank), f32),
-            ((6, rank, rank), f32),
-            ((8 * rank, leaves * rank), bf16),
+            ((8, rank, rank), f32),
+            ((6 * rank, leaves * rank), bf16),
             ((cols, leaves * rank), f32),
         ],
         cross_transfer,
@@ -407,44 +419,46 @@
         flops=2 * 100 * block * rank,
         name="shadow",
     )
-    near_low = near_half(0, [up_low])
     first_send, low_sums = small_call(
         first_kernel,
         [((8, 2 * slice_cols, rank), f32), ((6, slice_cols, rank), f32)],
         got_first,
-        up_low,
+        cross_transfer,
+        got_edge,
         flops=18 * slice_cols * block,
         name="first",
-        after=[near_low],
+        after=[down_mid],
     )
 
     got_mid = lax.all_to_all(first_send, ("group", "dev"), 0, 0, tiled=True, axis_index_groups=mid_groups)
-    near_high = near_half(count // 2, [first_send])
+    near_low = near_half(0, [first_send])
     second_send = small_call(
         second_kernel,
         [((8, slice_cols, rank), f32)],
         got_mid,
-        up_high,
+        cross_transfer,
         flops=12 * slice_cols * block,
         name="second",
-        after=[near_high],
+        after=[near_low],
     )
 
     got_top = lax.all_to_all(second_send, "group", 0, 0, tiled=True, axis_index_groups=z_groups)
     zero_send, _ = lax.optimization_barrier((zero_send, second_send))
-    got_zero = lax.ppermute(zero_send, "dev", [(i, i ^ 1) for i in range(lax.axis_size("dev"))])
+    got_zero = swap(zero_send, 1)
     third_send = small_call(
         third_kernel,
-        [((8, 3 * slice_cols, rank), f32)],
+        [((8, 2 * slice_cols, rank), f32)],
         got_mid,
         got_top,
         down_mid,
+        got_edge,
         low_sums,
         flops=36 * slice_cols * block,
         name="third",
         after=[got_zero],
     )
     got_low = lax.all_to_all(third_send, "dev", 0, 0, tiled=True, axis_index_groups=y_groups)
+    near_high = near_half(count // 2, [third_send])
     return call(
         fall_kernel,
         [((count, cols), bf16)],

time: 82 us -> 79.9 us (0.974)
  blocking collectives: 16.6 us -> 0 us
  starting transfers between devices: 24.7 us -> 35.3 us
  waiting for transfers between devices: 12.6 us -> 14.9 us
    all_to_all x1 -> x0, blocking collectives: 16.6 us -> none  [body(): lax.all_to_all(third_send, 'dev', 0, 0, tiled=True, axis_index_groups=y_g...]
    ppermute x1 -> x2, starting transfers between devices: 2.47 us -> 9.01 us  [swap(): lax.ppermute(block, 'dev', [(i, i ^ stride) for i in range(lax.axis_size(...]
    all_to_all x0 -> x1, waiting for transfers between devices: none -> 5.73 us  [body(): lax.all_to_all(third_send, 'dev', 0, 0, tiled=True, axis_index_groups=y_g...]
    all_to_all x0 -> x1, starting transfers between devices: none -> 3.94 us  [body(): lax.all_to_all(third_send, 'dev', 0, 0, tiled=True, axis_index_groups=y_g...]
    all_to_all x1, waiting for transfers between devices: 4.76 us -> 2.74 us  [body(): lax.all_to_all(shares, 'dev', 0, 0, tiled=True, axis_index_groups=y_groups)]
    pallas_call x3, Pallas kernels: 1.93 us -> 3.32 us  [small_call(): pl.pallas_call(kernel, out_shape=shapes, in_specs=[pl.BlockSpec(memory_sp...]
    ppermute x1 -> x2, waiting for transfers between devices: 4.71 us -> 3.54 us  [swap(): lax.ppermute(block, 'dev', [(i, i ^ stride) for i in range(lax.axis_size(...]
  transfers between devices with their start and end apart: 4 -> 6, of which waited for: 4 -> 5; matrix products, arithmetic and copies ran while one was open for 0% -> 0% of each run, Pallas kernels for 18% -> 18%
where the time goes in v4:
time: 79.9 us; the launch traced here: 79.3 us
  starting transfers between devices  35.3 us (44%)
  Pallas kernels  28 us (35%)
  waiting for transfers between devices  14.9 us (19%)
    pallas_call x5, Pallas kernels, call(): pl.pallas_call(run, out_shape=shapes, in_specs=[pl.BlockSpec(memory_space...  24.7 us
    all_to_all x1, starting transfers between devices, body(): lax.all_to_all(second_send, 'group', 0, 0, tiled=True, axis_index_groups=...  10.3 us
    ppermute x2, starting transfers between devices, swap(): lax.ppermute(block, 'dev', [(i, i ^ stride) for i in range(lax.axis_size(...  9.01 us
    all_to_all x1, starting transfers between devices, body(): lax.all_to_all(shares, 'dev', 0, 0, tiled=True, axis_index_groups=y_groups)  7.24 us
    all_to_all x1, waiting for transfers between devices, body(): lax.all_to_all(third_send, 'dev', 0, 0, tiled=True, axis_index_groups=y_g...  5.73 us
    all_to_all x1, starting transfers between devices, body(): lax.all_to_all(first_send, ('group', 'dev'), 0, 0, tiled=True, axis_index...  4.83 us
    all_to_all x1, starting transfers between devices, body(): lax.all_to_all(third_send, 'dev', 0, 0, tiled=True, axis_index_groups=y_g...  3.94 us
    ppermute x2, waiting for transfers between devices, swap(): lax.ppermute(block, 'dev', [(i, i ^ stride) for i in range(lax.axis_size(...  3.54 us
  transfers between devices with their start and end apart: 6, of which 5 were waited for; matrix products, arithmetic and copies ran while one was open for 0% of the time, Pallas kernels for 18%

profile of v4, /device:TPU:2, one launch (start us, length us, event | category | flops | bytes accessed | tf_op | source)
XLA Modules:
  0.0 79.3 jit_solution(3175761426668127487)
XLA Ops:
  0.0 6.3 %rise.1 = (bf16[2048,512]{1,0:T(8,128)(2,1)}, bf16[2048,128]{1,0:T(8,128)(2,1)}, f32[256,512]{1,0:T(8,128)}, f32[2,256,128]{2,1,0:T(8,128)}, f32[256,128]{1,0:T(...) custom-call(s32[1,2048]{1,0:T(1,128)} %refs_0_.2, bf16[4,512,128]{2,1,0:T(8,128)(2,1)} %refs_1_.2, ...), custom_call_target="tpu_custom_call" | custom-call | flops 2147483648 | bytes 6365184 | tf_op jit(solution)/shard_map/rise/pallas_call | solution.py:319
  6.3 0.0 copy-start
  6.3 7.2 %all-to-all-start = ((f32[8,64,128]{2,1,0:T(8,128)}), f32[8,64,128]{2,1,0:T(8,128)S(1)}, u32[]{:S(2)}, u32[]{:S(2)}) async-start(f32[8,64,128]{2,1,0:T(8,128)} %get-tuple-element.23), calls=%async_computation | async-start | bytes 524288 | tf_op jit(solution)/shard_map/all_to_all | solution.py:404
  13.6 5.1 %collective-permute-start = (f32[128,128]{1,0:T(8,128)}, f32[128,128]{1,0:T(8,128)S(1)}, u32[]{:S(2)}, u32[]{:S(2)}) collective-permute-start(f32[128,128]{1,0:T(8,128)} %get-tuple-element.28), channel_id=1, source_target_pairs={{0,7},{1,6},{2,5},{3,4},{4,3},{5,2},{6,1},{7,0},{8,15},{9,14},{10,... | collective-permute-start | bytes 196616 | tf_op jit(solution)/shard_map/ppermute | solution.py:353
  18.7 4.7 %shadow.1 = (f32[8,128,128]{2,1,0:T(8,128)}, bf16[768,512]{1,0:T(8,128)(2,1)}, f32[256,512]{1,0:T(8,128)}) custom-call(f32[8,1,128,128]{3,2,1,0:T(8,128)} %edge_ref.3, f32[9,1,128,128]{3,2,1,0:T(8,128)} %refs_1_.3, f32[1,6,128,128]{3,2,1,0:T(8,128)} %refs_2_.5, f32[1,3,128,128]{3,2,1,0:T(8,128)} %refs_3_.3, f32[256,512]{1,0:T(8,128)} %get-tuple-element.24.refs_4_, ...), custom_call_target="tpu_custom_call" | custom-call | flops 419430400 | bytes 4325376 | tf_op jit(solution)/shard_map/shadow/pallas_call | solution.py:319
  23.4 2.7 %all-to-all-done.got_ref = f32[8,64,128]{2,1,0:T(8,128)S(1)} async-done(((f32[8,64,128]{2,1,0:T(8,128)}), f32[8,64,128]{2,1,0:T(8,128)S(1)}, u32[]{:S(2)}, u32[]{:S(2)}) %all-to-all-start) | async-done | bytes 262176 | tf_op jit(solution)/shard_map/all_to_all | solution.py:404
  26.1 0.0 collective-permute-done.other_ref
  26.1 0.0 copy-done
  26.1 1.3 %first.1 = (f32[8,64,128]{2,1,0:T(8,128)}, f32[6,32,128]{2,1,0:T(8,128)S(1)}) custom-call(f32[8,64,128]{2,1,0:T(8,128)S(1)} %all-to-all-done.got_ref, f32[8,1,128,128]{3,2,1,0:T(8,128)S(1)} %copy-done, f32[128,128]{1,0:T(8,128)S(1)} %collective-permute-done.other_ref), custom_call_target="tpu_custom_call" | custom-call | flops 9437184 | bytes 1212416 | tf_op jit(solution)/shard_map/first/pallas_call | solution.py:340
  27.4 4.8 %all-to-all-start.1 = ((f32[8,64,128]{2,1,0:T(8,128)}), f32[8,64,128]{2,1,0:T(8,128)S(1)}, u32[]{:S(2)}, u32[]{:S(2)}) async-start(f32[8,64,128]{2,1,0:T(8,128)} %get-tuple-element.29), calls=%async_computation.1 | async-start | bytes 524288 | tf_op jit(solution)/shard_map/all_to_all | solution.py:433
  32.2 0.0 copy-start.4
  32.2 0.0 copy-start.1
  32.2 4.8 %near.2.refs_5_ = f32[1024,256]{1,0:T(8,128)} custom-call(f32[8,2048]{1,0:T(8,128)} %refs_0_.5, bf16[2048,128]{1,0:T(8,128)(2,1)} %get-tuple-element.32.refs_1_, bf16[2048,256]{1,0:T(8,128)(2,1)} %refs_2_.7), custom_call_target="tpu_custom_call" | custom-call | flops 1610612736 | bytes 2686976 | tf_op jit(solution)/shard_map/near/pallas_call | solution.py:319
  37.0 0.9 %all-to-all-done.1.got_ref.got_mid_ref = f32[8,64,128]{2,1,0:T(8,128)S(1)} async-done(((f32[8,64,128]{2,1,0:T(8,128)}), f32[8,64,128]{2,1,0:T(8,128)S(1)}, u32[]{:S(2)}, u32[]{:S(2)}) %all-to-all-start.1) | async-done | bytes 262176 | tf_op jit(solution)/shard_map/all_to_all | solution.py:433
  38.0 0.9 %second.1 = f32[8,32,128]{2,1,0:T(8,128)} custom-call(f32[8,64,128]{2,1,0:T(8,128)S(1)} %all-to-all-done.1.got_ref.got_mid_ref, f32[8,1,128,128]{3,2,1,0:T(8,128)S(1)} %copy-done), custom_call_target="tpu_custom_call" | custom-call | flops 6291456 | bytes 917504 | tf_op jit(solution)/shard_map/second/pallas_call | solution.py:340
  38.9 10.3 %all-to-all-start.2 = ((f32[8,32,128]{2,1,0:T(8,128)}), f32[8,32,128]{2,1,0:T(8,128)S(1)}, u32[]{:S(2)}, u32[]{:S(2)}) async-start(f32[8,32,128]{2,1,0:T(8,128)} %second.1), calls=%async_computation.2 | async-start | bytes 262144 | tf_op jit(solution)/shard_map/all_to_all | solution.py:445
  49.2 0.0 copy-done.4
  49.2 3.9 %collective-permute-start.1 = (f32[256,128]{1,0:T(8,128)S(1)}, f32[256,128]{1,0:T(8,128)S(1)}, u32[]{:S(2)}, u32[]{:S(2)}) collective-permute-start(f32[256,128]{1,0:T(8,128)S(1)} %copy-done.4), channel_id=1, source_target_pairs={{0,1},{1,0},{2,3},{3,2},{4,5},{5,4},{6,7},{7,6},{8,9},{9,8},{10,11... | collective-permute-start | bytes 393224 | tf_op jit(solution)/shard_map/ppermute | solution.py:353
  53.1 3.5 %collective-permute-done.1.refs_1_ = f32[256,128]{1,0:T(8,128)S(1)} collective-permute-done((f32[256,128]{1,0:T(8,128)S(1)}, f32[256,128]{1,0:T(8,128)S(1)}, u32[]{:S(2)}, u32[]{:S(2)}) %collective-permute-start.1) | collective-permute-done | bytes 131104 | tf_op jit(solution)/shard_map/ppermute | solution.py:353
  56.6 0.0 copy-start.3
  56.6 2.0 %all-to-all-done.2.got_ref = f32[8,32,128]{2,1,0:T(8,128)S(1)} async-done(((f32[8,32,128]{2,1,0:T(8,128)}), f32[8,32,128]{2,1,0:T(8,128)S(1)}, u32[]{:S(2)}, u32[]{:S(2)}) %all-to-all-start.2) | async-done | bytes 131104 | tf_op jit(solution)/shard_map/all_to_all | solution.py:445
  58.6 0.0 copy-done.1
  58.6 1.2 %third.1 = f32[8,64,128]{2,1,0:T(8,128)} custom-call(f32[8,64,128]{2,1,0:T(8,128)S(1)} %all-to-all-done.1.got_ref.got_mid_ref, f32[8,32,128]{2,1,0:T(8,128)S(1)} %all-to-all-done.2.got_ref, f32[8,128,128]{2,1,0:T(8,128)S(1)} %copy-done.1, f32[128,128]{1,0:T(8,128)S(1)} %collective-permute-done.other_ref, f32[6,32,128]{2,1,0:T(8,128)S(1)} %get-tuple-element.36.low_ref), custom_call_target="tpu_custom_call" | custom-call | flops 18874368 | bytes 1343488 | tf_op jit(solution)/shard_map/third/pallas_call | solution.py:340
  59.8 3.9 %all-to-all-start.3 = ((f32[8,64,128]{2,1,0:T(8,128)}), f32[8,64,128]{2,1,0:T(8,128)S(1)}, u32[]{:S(2)}, u32[]{:S(2)}) async-start(f32[8,64,128]{2,1,0:T(8,128)} %third.1), calls=%async_computation.3 | async-start | bytes 524288 | tf_op jit(solution)/shard_map/all_to_all | solution.py:460
  63.7 4.7 %near.3.refs_6_ = f32[1024,256]{1,0:T(8,128)} custom-call(f32[8,2048]{1,0:T(8,128)} %refs_0_.5, bf16[2048,128]{1,0:T(8,128)(2,1)} %get-tuple-element.32.refs_1_, bf16[2048,256]{1,0:T(8,128)(2,1)} %refs_2_.7), custom_call_target="tpu_custom_call" | custom-call | flops 1610612736 | bytes 2686976 | tf_op jit(solution)/shard_map/near/pallas_call | solution.py:319
  68.4 0.0 copy-done.3
  68.5 5.7 %all-to-all-done.3.refs_0_ = f32[8,64,128]{2,1,0:T(8,128)S(1)} async-done(((f32[8,64,128]{2,1,0:T(8,128)}), f32[8,64,128]{2,1,0:T(8,128)S(1)}, u32[]{:S(2)}, u32[]{:S(2)}) %all-to-all-start.3) | async-done | bytes 262176 | tf_op jit(solution)/shard_map/all_to_all | solution.py:460
  74.2 0.0 copy-start.2
  74.2 0.7 copy-done.2
  74.9 4.2 %fall.1 = bf16[2048,256]{1,0:T(8,128)(2,1)} custom-call(f32[8,64,128]{2,1,0:T(8,128)} %copy-done.2, f32[256,128]{1,0:T(8,128)} %copy-done.3, bf16[768,512]{1,0:T(8,128)(2,1)} %get-tuple-element.37.refs_2_, f32[256,512]{1,0:T(8,128)} %get-tuple-element.38.refs_3_, bf16[2048,512]{1,0:T(8,128)(2,1)} %get-tuple-element.39.refs_4_, f32[1024,256]{1,0:T(8,128)} %near.2.refs_5_, ...), custom_call_target="tpu_custom_call" | custom-call | flops 536870912 | bytes 6946816 | tf_op jit(solution)/shard_map/fall/pallas_call | solution.py:319
Async XLA Ops:
  6.3 19.8 %copy-start = (f32[8,1,128,128]{3,2,1,0:T(8,128)S(1)}, f32[8,1,128,128]{3,2,1,0:T(8,128)}, u32[]{:S(2)}) copy-start(f32[8,1,128,128]{3,2,1,0:T(8,128)} %edge_ref.3) | copy-start | bytes 1572868
  6.3 19.8 %all-to-all-start = ((f32[8,64,128]{2,1,0:T(8,128)}), f32[8,64,128]{2,1,0:T(8,128)S(1)}, u32[]{:S(2)}, u32[]{:S(2)}) async-start(f32[8,64,128]{2,1,0:T(8,128)} %get-tuple-element.23), calls=%async_computation | async-start | bytes 524288 | tf_op jit(solution)/shard_map/all_to_all | solution.py:404
  13.6 12.6 %collective-permute-start = (f32[128,128]{1,0:T(8,128)}, f32[128,128]{1,0:T(8,128)S(1)}, u32[]{:S(2)}, u32[]{:S(2)}) collective-permute-start(f32[128,128]{1,0:T(8,128)} %get-tuple-element.28), channel_id=1, source_target_pairs={{0,7},{1,6},{2,5},{3,4},{4,3},{5,2},{6,1},{7,0},{8,15},{9,14},{10,... | collective-permute-start | bytes 196616 | tf_op jit(solution)/shard_map/ppermute | solution.py:353
  27.4 10.6 %all-to-all-start.1 = ((f32[8,64,128]{2,1,0:T(8,128)}), f32[8,64,128]{2,1,0:T(8,128)S(1)}, u32[]{:S(2)}, u32[]{:S(2)}) async-start(f32[8,64,128]{2,1,0:T(8,128)} %get-tuple-element.29), calls=%async_computation.1 | async-start | bytes 524288 | tf_op jit(solution)/shard_map/all_to_all | solution.py:433
  32.2 17.0 %copy-start.4 = (f32[256,128]{1,0:T(8,128)S(1)}, f32[256,128]{1,0:T(8,128)}, u32[]{:S(2)}) copy-start(f32[256,128]{1,0:T(8,128)} %get-tuple-element.34) | copy-start | bytes 393220
  32.2 26.4 %copy-start.1 = (f32[8,128,128]{2,1,0:T(8,128)S(1)}, f32[8,128,128]{2,1,0:T(8,128)}, u32[]{:S(2)}) copy-start(f32[8,128,128]{2,1,0:T(8,128)} %get-tuple-element.26.down_ref) | copy-start | bytes 1572868
  38.9 19.7 %all-to-all-start.2 = ((f32[8,32,128]{2,1,0:T(8,128)}), f32[8,32,128]{2,1,0:T(8,128)S(1)}, u32[]{:S(2)}, u32[]{:S(2)}) async-start(f32[8,32,128]{2,1,0:T(8,128)} %second.1), calls=%async_computation.2 | async-start | bytes 262144 | tf_op jit(solution)/shard_map/all_to_all | solution.py:445
  49.2 7.4 %collective-permute-start.1 = (f32[256,128]{1,0:T(8,128)S(1)}, f32[256,128]{1,0:T(8,128)S(1)}, u32[]{:S(2)}, u32[]{:S(2)}) collective-permute-start(f32[256,128]{1,0:T(8,128)S(1)} %copy-done.4), channel_id=1, source_target_pairs={{0,1},{1,0},{2,3},{3,2},{4,5},{5,4},{6,7},{7,6},{8,9},{9,8},{10,11... | collective-permute-start | bytes 393224 | tf_op jit(solution)/shard_map/ppermute | solution.py:353
  56.6 11.8 %copy-start.3 = (f32[256,128]{1,0:T(8,128)}, f32[256,128]{1,0:T(8,128)S(1)}, u32[]{:S(2)}) copy-start(f32[256,128]{1,0:T(8,128)S(1)} %collective-permute-done.1.refs_1_) | copy-start | bytes 393220
  59.8 14.4 %all-to-all-start.3 = ((f32[8,64,128]{2,1,0:T(8,128)}), f32[8,64,128]{2,1,0:T(8,128)S(1)}, u32[]{:S(2)}, u32[]{:S(2)}) async-start(f32[8,64,128]{2,1,0:T(8,128)} %third.1), calls=%async_computation.3 | async-start | bytes 524288 | tf_op jit(solution)/shard_map/all_to_all | solution.py:460
  74.2 0.7 copy-start.2

commit v5 on v4

--- a/solution.py
+++ b/solution.py
@@ -60,8 +60,9 @@
             uexp_ref[start : start + step, j * rank : (j + 1) * rank] = placed[:, :rank].astype(bf16)
             member = member + placed[:, rank:]
         member_ref[start : start + step, :] = member.astype(bf16)
-        uexp_out.send(start, step)
-        member_out.send(start, step)
+        if (start + step) % (4 * step) == 0:
+            uexp_out.send(start - 3 * step, 4 * step)
+            member_out.send(start - 3 * step, 4 * step)
     local_ref, edge_ref = local_in(), edge_in()
     edge_out.ref[...] = edge_ref[2, 0]
     edge_out.send()
@@ -82,7 +83,7 @@
         send_out.ref[:, level * rows : (level + 1) * rows] = own.reshape(8, rows, rank)
 
 
-def near_kernel(first_row, points_in, member_in, rhs_in, near_out):
+def near_field(first_row, points_in, member_in, rhs_in, near_out):
     points_ref, member_ref = points_in(), member_in()
     points = points_ref.shape[1]
     scale = math.sqrt(2.0 * kernel_rate / math.log(2.0))
@@ -121,15 +122,31 @@
             power = mm(left[start : start + step], right[:, base : base + chunk])
             total = total + mm(jnp.exp2(power).astype(bf16), rhs_ref[base : base + chunk, :])
         near_ref[out_row : out_row + step, :] = total
-        near_out.send(out_row, step)
+        if (out_row + step) % (2 * step) == 0:
+            near_out.send(out_row - step, 2 * step)
 
 
 def turn(left, matrix):
     return jnp.where(left, matrix.T, matrix)
 
 
+def local_kernel(points_in, member_in, rhs_in, local_in, coupling_in, leaf_in, node_in, near_out, base_out):
+    near_field(near_out.ref.shape[0], points_in, member_in, rhs_in, near_out)
+    local_ref = local_in()
+    rank = local_ref.shape[-1]
+    leaf_ref, node_ref, coupling_ref = leaf_in(), node_in(), coupling_in()
+    coupled = [mm3(node_ref[1], coupling_ref[0, 2], True), mm3(node_ref[0], coupling_ref[0, 2])]
+    for j in range(2):
+        left = slice(2 * j * rank, (2 * j + 1) * rank)
+        right = slice((2 * j + 1) * rank, (2 * j + 2) * rank)
+        link = coupling_ref[0, j]
+        base_out.ref[:, left] = mm3(leaf_ref[:, right], link, True) + mm3(coupled[j], local_ref[0, 2 * j], True)
+        base_out.ref[:, right] = mm3(leaf_ref[:, left], link) + mm3(coupled[j], local_ref[0, 2 * j + 1], True)
+    base_out.send()
+
+
 def shadow_kernel(
-    edge_in, link_in, local_in, coupling_in, leaf_in, node_in, down_mid_out, down_out, base_out
+    edge_in, link_in, local_in, points_in, member_in, rhs_in, down_mid_out, down_out, near_out
 ):
     edge_ref, link_ref, local_ref = edge_in(), link_in(), local_in()
     levels = link_ref.shape[0]
@@ -161,15 +178,7 @@
         rows = slice(k * rank, (k + 1) * rank)
         down_out.ref[rows], down_out.ref[3 * rank + k * rank : 4 * rank + k * rank] = split(down[k])
     down_out.send()
-    leaf_ref, node_ref, coupling_ref = leaf_in(), node_in(), coupling_in()
-    coupled = [mm3(node_ref[1], coupling_ref[0, 2], True), mm3(node_ref[0], coupling_ref[0, 2])]
-    for j in range(2):
-        left = slice(2 * j * rank, (2 * j + 1) * rank)
-        right = slice((2 * j + 1) * rank, (2 * j + 2) * rank)
-        link = coupling_ref[0, j]
-        base_out.ref[:, left] = mm3(leaf_ref[:, right], link, True) + mm3(coupled[j], local_ref[0, 2 * j], True)
-        base_out.ref[:, right] = mm3(leaf_ref[:, left], link) + mm3(coupled[j], local_ref[0, 2 * j + 1], True)
-    base_out.send()
+    near_field(0, points_in, member_in, rhs_in, near_out)
 
 
 def half_edges(own, other):
@@ -255,7 +264,8 @@
         near_ref, base = (near_low_in(), start) if start < half else (near_high_in(), start - half)
         total = near_ref[base : base + step, :] + mm(uexp_ref[start : start + step, :], far, True)
         out.ref[start : start + step, :] = total.astype(bf16)
-        out.send(start, step)
+        if (start + step) % (2 * step) == 0:
+            out.send(start - step, 2 * step)
 
 
 class Fetched:
@@ -273,20 +283,16 @@
 
 
 class Sent:
-    def __init__(self, target, ref, sems):
-        self.target, self.ref, self.sems, self.copies = target, ref, sems, []
+    def __init__(self, target, ref, sem):
+        self.target, self.ref, self.sem, self.sent = target, ref, sem, False
 
     def send(self, start=0, size=None):
         rows = pl.ds(start, self.ref.shape[0] if size is None else size)
-        copy = pltpu.make_async_copy(self.ref.at[rows], self.target.at[rows], self.sems.at[len(self.copies)])
-        copy.start()
-        self.copies.append(copy)
+        pltpu.make_async_copy(self.ref.at[rows], self.target.at[rows], self.sem).start()
+        self.sent = True
 
     def finish(self):
-        if not self.copies:
-            self.send()
-        for copy in self.copies:
-            copy.wait()
+        pltpu.make_async_copy(self.ref, self.target, self.sem).wait()
 
 
 def call(kernel, outs, *args, flops=0, name=None, after=(), leads=None):
@@ -305,7 +311,7 @@
         sent = [Sent(targets[i], held[count + i], out_sems.at[i]) for i in range(made)]
         kernel(*fetched, *sent)
         for out in sent:
-            if not out.copies:
+            if not out.sent:
                 out.send()
         for arg in fetched:
             arg()
@@ -323,7 +329,7 @@
         out_specs=[pl.BlockSpec(memory_space=pl.ANY)] * made,
         scratch_shapes=[pltpu.VMEM(lead_shape(i), args[i].dtype) for i in range(count)]
         + [pltpu.VMEM(s.shape, s.dtype) for s in shapes]
-        + [pltpu.SemaphoreType.DMA((count,)), pltpu.SemaphoreType.DMA((made, 8))],
+        + [pltpu.SemaphoreType.DMA((count,)), pltpu.SemaphoreType.DMA((made,))],
         compiler_params=pltpu.CompilerParams(vmem_limit_bytes=62 * 1024 * 1024),
         cost_estimate=pl.CostEstimate(flops=flops, bytes_accessed=moved, transcendentals=0),
         name=name,
@@ -389,34 +395,22 @@
         name="rise",
     )
 
-    def near_half(first_row, after):
-        return call(
-            functools.partial(near_kernel, first_row),
-            [((count // 2, cols), f32)],
-            points,
-            member,
-            rhs,
-            flops=count * count * (cols + rank),
-            name="near",
-            after=after,
-        )
-
     got_first = lax.all_to_all(shares, "dev", 0, 0, tiled=True, axis_index_groups=y_groups)
     got_edge = swap(edge_send, 7)
-    down_mid, down, base = call(
+    down_mid, down, near_low = call(
         shadow_kernel,
         [
             ((8, rank, rank), f32),
             ((6 * rank, leaves * rank), bf16),
-            ((cols, leaves * rank), f32),
+            ((count // 2, cols), f32),
         ],
         cross_transfer,
         cross_coupling,
         local_transfer,
-        local_coupling,
-        leaf_nodes,
-        nodes,
-        flops=2 * 100 * block * rank,
+        points,
+        member,
+        rhs,
+        flops=2 * 100 * block * rank + count * count * (cols + rank),
         name="shadow",
     )
     first_send, low_sums = small_call(
@@ -431,7 +425,20 @@
     )
 
     got_mid = lax.all_to_all(first_send, ("group", "dev"), 0, 0, tiled=True, axis_index_groups=mid_groups)
-    near_low = near_half(0, [first_send])
+    near_high, base = call(
+        local_kernel,
+        [((count // 2, cols), f32), ((cols, leaves * rank), f32)],
+        points,
+        member,
+        rhs,
+        local_transfer,
+        local_coupling,
+        leaf_nodes,
+        nodes,
+        flops=count * count * (cols + rank),
+        name="local",
+        after=[first_send],
+    )
     second_send = small_call(
         second_kernel,
         [((8, slice_cols, rank), f32)],
@@ -439,7 +446,7 @@
         cross_transfer,
         flops=12 * slice_cols * block,
         name="second",
-        after=[near_low],
+        after=[near_high],
     )
 
     got_top = lax.all_to_all(second_send, "group", 0, 0, tiled=True, axis_index_groups=z_groups)
@@ -458,7 +465,6 @@
         after=[got_zero],
     )
     got_low = lax.all_to_all(third_send, "dev", 0, 0, tiled=True, axis_index_groups=y_groups)
-    near_high = near_half(count // 2, [third_send])
     return call(
         fall_kernel,
         [((count, cols), bf16)],

time: 79.9 us -> 77.4 us (0.969)
  blocking collectives: 0 us -> 14.3 us
  waiting for transfers between devices: 14.9 us -> 6.55 us
  starting transfers between devices: 35.3 us -> 31.3 us
  Pallas kernels: 28 us -> 24.7 us
    all_to_all x0 -> x1, blocking collectives: none -> 14.3 us  [body(): lax.all_to_all(third_send, 'dev', 0, 0, tiled=True, axis_index_groups=y_g...]
    all_to_all x1 -> x0, waiting for transfers between devices: 5.73 us -> none  [body(): lax.all_to_all(third_send, 'dev', 0, 0, tiled=True, axis_index_groups=y_g...]
    all_to_all x1 -> x0, starting transfers between devices: 3.94 us -> none  [body(): lax.all_to_all(third_send, 'dev', 0, 0, tiled=True, axis_index_groups=y_g...]
    pallas_call x5 -> x4, Pallas kernels: 24.7 us -> 22.1 us  [call(): pl.pallas_call(run, out_shape=shapes, in_specs=[pl.BlockSpec(memory_space...]
    all_to_all x1, waiting for transfers between devices: 2.74 us -> 0.92 us  [body(): lax.all_to_all(shares, 'dev', 0, 0, tiled=True, axis_index_groups=y_groups)]
    all_to_all x1, waiting for transfers between devices: 0.92 us -> 0.12 us  [body(): lax.all_to_all(first_send, ('group', 'dev'), 0, 0, tiled=True, axis_index...]
  transfers between devices with their start and end apart: 6 -> 5, of which waited for: 5 -> 4; matrix products, arithmetic and copies ran while one was open for 0% -> 0% of each run, Pallas kernels for 18% -> 16%
where the time goes in v5:
time: 77.4 us; the launch traced here: 76.9 us
  starting transfers between devices  31.3 us (40%)
  Pallas kernels  24.7 us (32%)
  blocking collectives  14.3 us (18%)
  waiting for transfers between devices  6.55 us (8%)
    pallas_call x4, Pallas kernels, call(): pl.pallas_call(run, out_shape=shapes, in_specs=[pl.BlockSpec(memory_space...  22.1 us
    all_to_all x1, blocking collectives, body(): lax.all_to_all(third_send, 'dev', 0, 0, tiled=True, axis_index_groups=y_g...  14.3 us
    all_to_all x1, starting transfers between devices, body(): lax.all_to_all(second_send, 'group', 0, 0, tiled=True, axis_index_groups=...  10.3 us
    ppermute x2, starting transfers between devices, swap(): lax.ppermute(block, 'dev', [(i, i ^ stride) for i in range(lax.axis_size(...  9.01 us
    all_to_all x1, starting transfers between devices, body(): lax.all_to_all(shares, 'dev', 0, 0, tiled=True, axis_index_groups=y_groups)  7.11 us
    all_to_all x1, starting transfers between devices, body(): lax.all_to_all(first_send, ('group', 'dev'), 0, 0, tiled=True, axis_index...  4.82 us
    ppermute x2, waiting for transfers between devices, swap(): lax.ppermute(block, 'dev', [(i, i ^ stride) for i in range(lax.axis_size(...  3.54 us
    pallas_call x3, Pallas kernels, small_call(): pl.pallas_call(kernel, out_shape=shapes, in_specs=[pl.BlockSpec(memory_sp...  2.61 us
  transfers between devices with their start and end apart: 5, of which 4 were waited for; matrix products, arithmetic and copies ran while one was open for 0% of the time, Pallas kernels for 16%

profile of v5, /device:TPU:2, one launch (start us, length us, event | category | flops | bytes accessed | tf_op | source)
XLA Modules:
  0.0 76.9 jit_solution(13272314801257879086)
XLA Ops:
  0.0 5.9 %rise.1 = (bf16[2048,512]{1,0:T(8,128)(2,1)}, bf16[2048,128]{1,0:T(8,128)(2,1)}, f32[256,512]{1,0:T(8,128)}, f32[2,256,128]{2,1,0:T(8,128)}, f32[256,128]{1,0:T(...) custom-call(s32[1,2048]{1,0:T(1,128)} %refs_0_.2, bf16[4,512,128]{2,1,0:T(8,128)(2,1)} %refs_1_.2, ...), custom_call_target="tpu_custom_call" | custom-call | flops 2147483648 | bytes 6365184 | tf_op jit(solution)/shard_map/rise/pallas_call | solution.py:325
  5.9 7.1 %all-to-all-start = ((f32[8,64,128]{2,1,0:T(8,128)}), f32[8,64,128]{2,1,0:T(8,128)S(1)}, u32[]{:S(2)}, u32[]{:S(2)}) async-start(f32[8,64,128]{2,1,0:T(8,128)} %get-tuple-element.24), calls=%async_computation | async-start | bytes 524288 | tf_op jit(solution)/shard_map/all_to_all | solution.py:398
  13.0 5.1 %collective-permute-start = (f32[128,128]{1,0:T(8,128)}, f32[128,128]{1,0:T(8,128)S(1)}, u32[]{:S(2)}, u32[]{:S(2)}) collective-permute-start(f32[128,128]{1,0:T(8,128)} %get-tuple-element.28), channel_id=1, source_target_pairs={{0,7},{1,6},{2,5},{3,4},{4,3},{5,2},{6,1},{7,0},{8,15},{9,14},{10,... | collective-permute-start | bytes 196616 | tf_op jit(solution)/shard_map/ppermute | solution.py:359
  18.1 0.0 copy-start
  18.1 6.5 %shadow.1 = (f32[8,128,128]{2,1,0:T(8,128)}, bf16[768,512]{1,0:T(8,128)(2,1)}, f32[1024,256]{1,0:T(8,128)}) custom-call(f32[8,1,128,128]{3,2,1,0:T(8,128)} %edge_ref.3, f32[9,1,128,128]{3,2,1,0:T(8,128)} %refs_1_.3, f32[1,6,128,128]{3,2,1,0:T(8,128)} %refs_3_.5, f32[8,2048]{1,0:T(8,128)} %refs_0_.4, bf16[2048,128]{1,0:T(8,128)(2,1)} %get-tuple-element.25.refs_4_.refs_1_, ...), custom_call_target="tpu_custom_call" | custom-call | flops 2030043136 | bytes 5505024 | tf_op jit(solution)/shard_map/shadow/pallas_call | solution.py:325
  24.6 0.9 %all-to-all-done.got_ref = f32[8,64,128]{2,1,0:T(8,128)S(1)} async-done(((f32[8,64,128]{2,1,0:T(8,128)}), f32[8,64,128]{2,1,0:T(8,128)S(1)}, u32[]{:S(2)}, u32[]{:S(2)}) %all-to-all-start) | async-done | bytes 262176 | tf_op jit(solution)/shard_map/all_to_all | solution.py:398
  25.6 0.0 collective-permute-done.other_ref
  25.6 0.0 copy-done
  25.6 1.3 %first.1 = (f32[8,64,128]{2,1,0:T(8,128)}, f32[6,32,128]{2,1,0:T(8,128)S(1)}) custom-call(f32[8,64,128]{2,1,0:T(8,128)S(1)} %all-to-all-done.got_ref, f32[8,1,128,128]{3,2,1,0:T(8,128)S(1)} %copy-done, f32[128,128]{1,0:T(8,128)S(1)} %collective-permute-done.other_ref), custom_call_target="tpu_custom_call" | custom-call | flops 9437184 | bytes 1212416 | tf_op jit(solution)/shard_map/first/pallas_call | solution.py:346
  26.8 4.8 %all-to-all-start.1 = ((f32[8,64,128]{2,1,0:T(8,128)}), f32[8,64,128]{2,1,0:T(8,128)S(1)}, u32[]{:S(2)}, u32[]{:S(2)}) async-start(f32[8,64,128]{2,1,0:T(8,128)} %get-tuple-element.29), calls=%async_computation.1 | async-start | bytes 524288 | tf_op jit(solution)/shard_map/all_to_all | solution.py:427
  31.7 0.0 copy-start.3
  31.7 0.0 copy-start.1
  31.7 5.6 %local.1 = (f32[1024,256]{1,0:T(8,128)}, f32[256,512]{1,0:T(8,128)}) custom-call(f32[8,2048]{1,0:T(8,128)} %refs_0_.4, bf16[2048,128]{1,0:T(8,128)(2,1)} %get-tuple-element.25.refs_4_.refs_1_, bf16[2048,256]{1,0:T(8,128)(2,1)} %refs_2_.5, f32[1,6,128,128]{3,2,1,0:T(8,128)} %refs_3_.5, f32[1,3,128,128]{3,2,1,0:T(8,128)} %refs_4_.3, ...), custom_call_target="tpu_custom_call" | custom-call | flops 1610612736 | bytes 4587520 | tf_op jit(solution)/shard_map/local/pallas_call | solution.py:325
  37.3 0.1 all-to-all-done.1.got_ref.got_mid_ref
  37.4 0.9 %second.1 = f32[8,32,128]{2,1,0:T(8,128)} custom-call(f32[8,64,128]{2,1,0:T(8,128)S(1)} %all-to-all-done.1.got_ref.got_mid_ref, f32[8,1,128,128]{3,2,1,0:T(8,128)S(1)} %copy-done), custom_call_target="tpu_custom_call" | custom-call | flops 6291456 | bytes 917504 | tf_op jit(solution)/shard_map/second/pallas_call | solution.py:346
  38.3 10.3 %all-to-all-start.2 = ((f32[8,32,128]{2,1,0:T(8,128)}), f32[8,32,128]{2,1,0:T(8,128)S(1)}, u32[]{:S(2)}, u32[]{:S(2)}) async-start(f32[8,32,128]{2,1,0:T(8,128)} %second.1), calls=%async_computation.2 | async-start | bytes 262144 | tf_op jit(solution)/shard_map/all_to_all | solution.py:452
  48.6 0.0 copy-done.3
  48.6 3.9 %collective-permute-start.1 = (f32[256,128]{1,0:T(8,128)S(1)}, f32[256,128]{1,0:T(8,128)S(1)}, u32[]{:S(2)}, u32[]{:S(2)}) collective-permute-start(f32[256,128]{1,0:T(8,128)S(1)} %copy-done.3), channel_id=1, source_target_pairs={{0,1},{1,0},{2,3},{3,2},{4,5},{5,4},{6,7},{7,6},{8,9},{9,8},{10,11... | collective-permute-start | bytes 393224 | tf_op jit(solution)/shard_map/ppermute | solution.py:359
  52.5 3.5 %collective-permute-done.1.refs_1_ = f32[256,128]{1,0:T(8,128)S(1)} collective-permute-done((f32[256,128]{1,0:T(8,128)S(1)}, f32[256,128]{1,0:T(8,128)S(1)}, u32[]{:S(2)}, u32[]{:S(2)}) %collective-permute-start.1) | collective-permute-done | bytes 131104 | tf_op jit(solution)/shard_map/ppermute | solution.py:359
  56.1 0.0 copy-start.2
  56.1 2.0 %all-to-all-done.2.got_ref = f32[8,32,128]{2,1,0:T(8,128)S(1)} async-done(((f32[8,32,128]{2,1,0:T(8,128)}), f32[8,32,128]{2,1,0:T(8,128)S(1)}, u32[]{:S(2)}, u32[]{:S(2)}) %all-to-all-start.2) | async-done | bytes 131104 | tf_op jit(solution)/shard_map/all_to_all | solution.py:452
  58.0 0.0 copy-done.1
  58.0 0.4 third.1
  58.5 14.3 %all_to_all.20.refs_0_ = f32[8,64,128]{2,1,0:T(8,128)} all-to-all(f32[8,64,128]{2,1,0:T(8,128)S(1)} %third.1), channel_id=1, replica_groups={{0,1,2,3,4,5,6,7},{8,9,10,11,12,13,14,15},{16,17,18,19,20,21,22,23},{24..., dimensions={0} | all-to-all | bytes 524288 | tf_op jit(solution)/shard_map/all_to_all | solution.py:467
  72.8 0.0 copy-done.2
  72.8 4.1 %fall.1 = bf16[2048,256]{1,0:T(8,128)(2,1)} custom-call(f32[8,64,128]{2,1,0:T(8,128)} %all_to_all.20.refs_0_, f32[256,128]{1,0:T(8,128)} %copy-done.2, bf16[768,512]{1,0:T(8,128)(2,1)} %get-tuple-element.39.refs_2_, f32[256,512]{1,0:T(8,128)} %get-tuple-element.40.refs_3_, bf16[2048,512]{1,0:T(8,128)(2,1)} %get-tuple-element.41.refs_4_, ...), custom_call_target="tpu_custom_call" | custom-call | flops 536870912 | bytes 6946816 | tf_op jit(solution)/shard_map/fall/pallas_call | solution.py:325
Async XLA Ops:
  5.9 19.7 %all-to-all-start = ((f32[8,64,128]{2,1,0:T(8,128)}), f32[8,64,128]{2,1,0:T(8,128)S(1)}, u32[]{:S(2)}, u32[]{:S(2)}) async-start(f32[8,64,128]{2,1,0:T(8,128)} %get-tuple-element.24), calls=%async_computation | async-start | bytes 524288 | tf_op jit(solution)/shard_map/all_to_all | solution.py:398
  13.0 12.6 %collective-permute-start = (f32[128,128]{1,0:T(8,128)}, f32[128,128]{1,0:T(8,128)S(1)}, u32[]{:S(2)}, u32[]{:S(2)}) collective-permute-start(f32[128,128]{1,0:T(8,128)} %get-tuple-element.28), channel_id=1, source_target_pairs={{0,7},{1,6},{2,5},{3,4},{4,3},{5,2},{6,1},{7,0},{8,15},{9,14},{10,... | collective-permute-start | bytes 196616 | tf_op jit(solution)/shard_map/ppermute | solution.py:359
  18.1 7.5 %copy-start = (f32[8,1,128,128]{3,2,1,0:T(8,128)S(1)}, f32[8,1,128,128]{3,2,1,0:T(8,128)}, u32[]{:S(2)}) copy-start(f32[8,1,128,128]{3,2,1,0:T(8,128)} %edge_ref.3) | copy-start | bytes 1572868
  26.8 10.6 %all-to-all-start.1 = ((f32[8,64,128]{2,1,0:T(8,128)}), f32[8,64,128]{2,1,0:T(8,128)S(1)}, u32[]{:S(2)}, u32[]{:S(2)}) async-start(f32[8,64,128]{2,1,0:T(8,128)} %get-tuple-element.29), calls=%async_computation.1 | async-start | bytes 524288 | tf_op jit(solution)/shard_map/all_to_all | solution.py:427
  31.7 17.0 %copy-start.3 = (f32[256,128]{1,0:T(8,128)S(1)}, f32[256,128]{1,0:T(8,128)}, u32[]{:S(2)}) copy-start(f32[256,128]{1,0:T(8,128)} %get-tuple-element.36) | copy-start | bytes 393220
  31.7 26.4 %copy-start.1 = (f32[8,128,128]{2,1,0:T(8,128)S(1)}, f32[8,128,128]{2,1,0:T(8,128)}, u32[]{:S(2)}) copy-start(f32[8,128,128]{2,1,0:T(8,128)} %get-tuple-element.26.down_ref) | copy-start | bytes 1572868
  38.3 19.7 %all-to-all-start.2 = ((f32[8,32,128]{2,1,0:T(8,128)}), f32[8,32,128]{2,1,0:T(8,128)S(1)}, u32[]{:S(2)}, u32[]{:S(2)}) async-start(f32[8,32,128]{2,1,0:T(8,128)} %second.1), calls=%async_computation.2 | async-start | bytes 262144 | tf_op jit(solution)/shard_map/all_to_all | solution.py:452
  48.6 7.4 %collective-permute-start.1 = (f32[256,128]{1,0:T(8,128)S(1)}, f32[256,128]{1,0:T(8,128)S(1)}, u32[]{:S(2)}, u32[]{:S(2)}) collective-permute-start(f32[256,128]{1,0:T(8,128)S(1)} %copy-done.3), channel_id=1, source_target_pairs={{0,1},{1,0},{2,3},{3,2},{4,5},{5,4},{6,7},{7,6},{8,9},{9,8},{10,11... | collective-permute-start | bytes 393224 | tf_op jit(solution)/shard_map/ppermute | solution.py:359
  56.1 16.7 %copy-start.2 = (f32[256,128]{1,0:T(8,128)}, f32[256,128]{1,0:T(8,128)S(1)}, u32[]{:S(2)}) copy-start(f32[256,128]{1,0:T(8,128)S(1)} %collective-permute-done.1.refs_1_) | copy-start | bytes 393220

commit v6 on v5

--- a/solution.py
+++ b/solution.py
@@ -169,14 +169,9 @@
     for j in range(4):
         leaf_path.append(mm3(local_ref[0, j], local_ref[0, 4 + j // 2]))
     leaf_path = jnp.concatenate(leaf_path, axis=0)
-    down = [
-        mm3(pair_matrix[0], leaf_path, True),
-        mm3(mm3(pair_matrix[1], edge[0], True), leaf_path, True),
-        mm3(mm3(edge[0], edge[1]).T, leaf_path, True),
-    ]
-    for k in range(3):
-        rows = slice(k * rank, (k + 1) * rank)
-        down_out.ref[rows], down_out.ref[3 * rank + k * rank : 4 * rank + k * rank] = split(down[k])
+    down = [pair_matrix[0], mm3(pair_matrix[1], edge[0], True), mm3(edge[0], edge[1]).T]
+    down = mm3(jnp.concatenate(down, axis=0), leaf_path, True)
+    down_out.ref[: 3 * rank], down_out.ref[3 * rank :] = split(down)
     down_out.send()
     near_field(0, points_in, member_in, rhs_in, near_out)
 
@@ -256,13 +251,13 @@
     down_ref = down_in()
     depth = sums.shape[1]
     far = mm(high, down_ref[:depth]) + (mm(low, down_ref[:depth]) + mm(high, down_ref[depth:]))
-    far = (far + base_in()[...]).astype(bf16)
+    far = (far + base_in()[...]).T.astype(bf16)
     uexp_ref = uexp_in()
     step = 256
     half = out.ref.shape[0] // 2
     for start in range(0, out.ref.shape[0], step):
         near_ref, base = (near_low_in(), start) if start < half else (near_high_in(), start - half)
-        total = near_ref[base : base + step, :] + mm(uexp_ref[start : start + step, :], far, True)
+        total = near_ref[base : base + step, :] + mm(uexp_ref[start : start + step, :], far)
         out.ref[start : start + step, :] = total.astype(bf16)
         if (start + step) % (2 * step) == 0:
             out.send(start - step, 2 * step)
@@ -295,7 +290,7 @@
         pltpu.make_async_copy(self.ref, self.target, self.sem).wait()
 
 
-def call(kernel, outs, *args, flops=0, name=None, after=(), leads=None):
+def call(kernel, outs, *args, flops=0, name=None, after=(), leads=None, mebibytes=62):
     leads = leads or {}
     shapes = [jax.ShapeDtypeStruct(shape, dtype) for shape, dtype in outs]
     moved = sum(a.size * a.dtype.itemsize for a in args)
@@ -330,7 +325,7 @@
         scratch_shapes=[pltpu.VMEM(lead_shape(i), args[i].dtype) for i in range(count)]
         + [pltpu.VMEM(s.shape, s.dtype) for s in shapes]
         + [pltpu.SemaphoreType.DMA((count,)), pltpu.SemaphoreType.DMA((made,))],
-        compiler_params=pltpu.CompilerParams(vmem_limit_bytes=62 * 1024 * 1024),
+        compiler_params=pltpu.CompilerParams(vmem_limit_bytes=mebibytes * 1024 * 1024),
         cost_estimate=pl.CostEstimate(flops=flops, bytes_accessed=moved, transcendentals=0),
         name=name,
     )(*args)
@@ -477,6 +472,7 @@
         near_high,
         flops=2 * count * cols * leaves * rank,
         name="fall",
+        mebibytes=60,
     )
 
 

time: 77.4 us -> 77.4 us (level)
  no operation moved by 1% of the time
where the time goes in v6:
time: 77.4 us; the launch traced here: 76.8 us
  starting transfers between devices  31.3 us (40%)
  Pallas kernels  24.5 us (32%)
  blocking collectives  14.3 us (18%)
  waiting for transfers between devices  6.71 us (9%)
    pallas_call x4, Pallas kernels, call(): pl.pallas_call(run, out_shape=shapes, in_specs=[pl.BlockSpec(memory_space...  21.9 us
    all_to_all x1, blocking collectives, body(): lax.all_to_all(third_send, 'dev', 0, 0, tiled=True, axis_index_groups=y_g...  14.3 us
    all_to_all x1, starting transfers between devices, body(): lax.all_to_all(second_send, 'group', 0, 0, tiled=True, axis_index_groups=...  10.3 us
    ppermute x2, starting transfers between devices, swap(): lax.ppermute(block, 'dev', [(i, i ^ stride) for i in range(lax.axis_size(...  9.01 us
    all_to_all x1, starting transfers between devices, body(): lax.all_to_all(shares, 'dev', 0, 0, tiled=True, axis_index_groups=y_groups)  7.11 us
    all_to_all x1, starting transfers between devices, body(): lax.all_to_all(first_send, ('group', 'dev'), 0, 0, tiled=True, axis_index...  4.82 us
    ppermute x2, waiting for transfers between devices, swap(): lax.ppermute(block, 'dev', [(i, i ^ stride) for i in range(lax.axis_size(...  3.54 us
    pallas_call x3, Pallas kernels, small_call(): pl.pallas_call(kernel, out_shape=shapes, in_specs=[pl.BlockSpec(memory_sp...  2.61 us
  transfers between devices with their start and end apart: 5, of which 4 were waited for; matrix products, arithmetic and copies ran while one was open for 0% of the time, Pallas kernels for 16%

profile of v6, /device:TPU:2, one launch (start us, length us, event | category | flops | bytes accessed | tf_op | source)
XLA Modules:
  0.0 76.8 jit_solution(5909859859328931941)
XLA Ops:
  0.0 5.9 %rise.1 = (bf16[2048,512]{1,0:T(8,128)(2,1)}, bf16[2048,128]{1,0:T(8,128)(2,1)}, f32[256,512]{1,0:T(8,128)}, f32[2,256,128]{2,1,0:T(8,128)}, f32[256,128]{1,0:T(...) custom-call(s32[1,2048]{1,0:T(1,128)} %refs_0_.2, bf16[4,512,128]{2,1,0:T(8,128)(2,1)} %refs_1_.2, ...), custom_call_target="tpu_custom_call" | custom-call | flops 2147483648 | bytes 6365184 | tf_op jit(solution)/shard_map/rise/pallas_call | solution.py:320
  5.9 7.1 %all-to-all-start = ((f32[8,64,128]{2,1,0:T(8,128)}), f32[8,64,128]{2,1,0:T(8,128)S(1)}, u32[]{:S(2)}, u32[]{:S(2)}) async-start(f32[8,64,128]{2,1,0:T(8,128)} %get-tuple-element.24), calls=%async_computation | async-start | bytes 524288 | tf_op jit(solution)/shard_map/all_to_all | solution.py:393
  13.0 5.1 %collective-permute-start = (f32[128,128]{1,0:T(8,128)}, f32[128,128]{1,0:T(8,128)S(1)}, u32[]{:S(2)}, u32[]{:S(2)}) collective-permute-start(f32[128,128]{1,0:T(8,128)} %get-tuple-element.28), channel_id=1, source_target_pairs={{0,7},{1,6},{2,5},{3,4},{4,3},{5,2},{6,1},{7,0},{8,15},{9,14},{10,... | collective-permute-start | bytes 196616 | tf_op jit(solution)/shard_map/ppermute | solution.py:354
  18.1 0.0 copy-start
  18.1 6.4 %shadow.1 = (f32[8,128,128]{2,1,0:T(8,128)}, bf16[768,512]{1,0:T(8,128)(2,1)}, f32[1024,256]{1,0:T(8,128)}) custom-call(f32[8,1,128,128]{3,2,1,0:T(8,128)} %edge_ref.3, f32[9,1,128,128]{3,2,1,0:T(8,128)} %refs_1_.3, f32[1,6,128,128]{3,2,1,0:T(8,128)} %refs_3_.5, f32[8,2048]{1,0:T(8,128)} %refs_0_.4, bf16[2048,128]{1,0:T(8,128)(2,1)} %get-tuple-element.25.refs_4_.refs_1_, ...), custom_call_target="tpu_custom_call" | custom-call | flops 2030043136 | bytes 5505024 | tf_op jit(solution)/shard_map/shadow/pallas_call | solution.py:320
  24.5 1.1 %all-to-all-done.got_ref = f32[8,64,128]{2,1,0:T(8,128)S(1)} async-done(((f32[8,64,128]{2,1,0:T(8,128)}), f32[8,64,128]{2,1,0:T(8,128)S(1)}, u32[]{:S(2)}, u32[]{:S(2)}) %all-to-all-start) | async-done | bytes 262176 | tf_op jit(solution)/shard_map/all_to_all | solution.py:393
  25.6 0.0 collective-permute-done.other_ref
  25.6 0.0 copy-done
  25.6 1.3 %first.1 = (f32[8,64,128]{2,1,0:T(8,128)}, f32[6,32,128]{2,1,0:T(8,128)S(1)}) custom-call(f32[8,64,128]{2,1,0:T(8,128)S(1)} %all-to-all-done.got_ref, f32[8,1,128,128]{3,2,1,0:T(8,128)S(1)} %copy-done, f32[128,128]{1,0:T(8,128)S(1)} %collective-permute-done.other_ref), custom_call_target="tpu_custom_call" | custom-call | flops 9437184 | bytes 1212416 | tf_op jit(solution)/shard_map/first/pallas_call | solution.py:341
  26.8 4.8 %all-to-all-start.1 = ((f32[8,64,128]{2,1,0:T(8,128)}), f32[8,64,128]{2,1,0:T(8,128)S(1)}, u32[]{:S(2)}, u32[]{:S(2)}) async-start(f32[8,64,128]{2,1,0:T(8,128)} %get-tuple-element.29), calls=%async_computation.1 | async-start | bytes 524288 | tf_op jit(solution)/shard_map/all_to_all | solution.py:422
  31.7 0.0 copy-start.3
  31.7 0.0 copy-start.1
  31.7 5.6 %local.1 = (f32[1024,256]{1,0:T(8,128)}, f32[256,512]{1,0:T(8,128)}) custom-call(f32[8,2048]{1,0:T(8,128)} %refs_0_.4, bf16[2048,128]{1,0:T(8,128)(2,1)} %get-tuple-element.25.refs_4_.refs_1_, bf16[2048,256]{1,0:T(8,128)(2,1)} %refs_2_.5, f32[1,6,128,128]{3,2,1,0:T(8,128)} %refs_3_.5, f32[1,3,128,128]{3,2,1,0:T(8,128)} %refs_4_.3, ...), custom_call_target="tpu_custom_call" | custom-call | flops 1610612736 | bytes 4587520 | tf_op jit(solution)/shard_map/local/pallas_call | solution.py:320
  37.3 0.1 all-to-all-done.1.got_ref.got_mid_ref
  37.4 0.9 %second.1 = f32[8,32,128]{2,1,0:T(8,128)} custom-call(f32[8,64,128]{2,1,0:T(8,128)S(1)} %all-to-all-done.1.got_ref.got_mid_ref, f32[8,1,128,128]{3,2,1,0:T(8,128)S(1)} %copy-done), custom_call_target="tpu_custom_call" | custom-call | flops 6291456 | bytes 917504 | tf_op jit(solution)/shard_map/second/pallas_call | solution.py:341
  38.3 10.3 %all-to-all-start.2 = ((f32[8,32,128]{2,1,0:T(8,128)}), f32[8,32,128]{2,1,0:T(8,128)S(1)}, u32[]{:S(2)}, u32[]{:S(2)}) async-start(f32[8,32,128]{2,1,0:T(8,128)} %second.1), calls=%async_computation.2 | async-start | bytes 262144 | tf_op jit(solution)/shard_map/all_to_all | solution.py:447
  48.6 0.0 copy-done.3
  48.6 3.9 %collective-permute-start.1 = (f32[256,128]{1,0:T(8,128)S(1)}, f32[256,128]{1,0:T(8,128)S(1)}, u32[]{:S(2)}, u32[]{:S(2)}) collective-permute-start(f32[256,128]{1,0:T(8,128)S(1)} %copy-done.3), channel_id=1, source_target_pairs={{0,1},{1,0},{2,3},{3,2},{4,5},{5,4},{6,7},{7,6},{8,9},{9,8},{10,11... | collective-permute-start | bytes 393224 | tf_op jit(solution)/shard_map/ppermute | solution.py:354
  52.5 3.5 %collective-permute-done.1.refs_1_ = f32[256,128]{1,0:T(8,128)S(1)} collective-permute-done((f32[256,128]{1,0:T(8,128)S(1)}, f32[256,128]{1,0:T(8,128)S(1)}, u32[]{:S(2)}, u32[]{:S(2)}) %collective-permute-start.1) | collective-permute-done | bytes 131104 | tf_op jit(solution)/shard_map/ppermute | solution.py:354
  56.1 0.0 copy-start.2
  56.1 2.0 %all-to-all-done.2.got_ref = f32[8,32,128]{2,1,0:T(8,128)S(1)} async-done(((f32[8,32,128]{2,1,0:T(8,128)}), f32[8,32,128]{2,1,0:T(8,128)S(1)}, u32[]{:S(2)}, u32[]{:S(2)}) %all-to-all-start.2) | async-done | bytes 131104 | tf_op jit(solution)/shard_map/all_to_all | solution.py:447
  58.0 0.0 copy-done.1
  58.0 0.4 third.1
  58.5 14.3 %all_to_all.20.refs_0_ = f32[8,64,128]{2,1,0:T(8,128)} all-to-all(f32[8,64,128]{2,1,0:T(8,128)S(1)} %third.1), channel_id=1, replica_groups={{0,1,2,3,4,5,6,7},{8,9,10,11,12,13,14,15},{16,17,18,19,20,21,22,23},{24..., dimensions={0} | all-to-all | bytes 524288 | tf_op jit(solution)/shard_map/all_to_all | solution.py:462
  72.8 0.0 copy-done.2
  72.8 4.1 %fall.1 = bf16[2048,256]{1,0:T(8,128)(2,1)} custom-call(f32[8,64,128]{2,1,0:T(8,128)} %all_to_all.20.refs_0_, f32[256,128]{1,0:T(8,128)} %copy-done.2, bf16[768,512]{1,0:T(8,128)(2,1)} %get-tuple-element.39.refs_2_, f32[256,512]{1,0:T(8,128)} %get-tuple-element.40.refs_3_, bf16[2048,512]{1,0:T(8,128)(2,1)} %get-tuple-element.41.refs_4_, ...), custom_call_target="tpu_custom_call" | custom-call | flops 536870912 | bytes 6946816 | tf_op jit(solution)/shard_map/fall/pallas_call | solution.py:320
Async XLA Ops:
  5.9 19.7 %all-to-all-start = ((f32[8,64,128]{2,1,0:T(8,128)}), f32[8,64,128]{2,1,0:T(8,128)S(1)}, u32[]{:S(2)}, u32[]{:S(2)}) async-start(f32[8,64,128]{2,1,0:T(8,128)} %get-tuple-element.24), calls=%async_computation | async-start | bytes 524288 | tf_op jit(solution)/shard_map/all_to_all | solution.py:393
  13.0 12.6 %collective-permute-start = (f32[128,128]{1,0:T(8,128)}, f32[128,128]{1,0:T(8,128)S(1)}, u32[]{:S(2)}, u32[]{:S(2)}) collective-permute-start(f32[128,128]{1,0:T(8,128)} %get-tuple-element.28), channel_id=1, source_target_pairs={{0,7},{1,6},{2,5},{3,4},{4,3},{5,2},{6,1},{7,0},{8,15},{9,14},{10,... | collective-permute-start | bytes 196616 | tf_op jit(solution)/shard_map/ppermute | solution.py:354
  18.1 7.5 %copy-start = (f32[8,1,128,128]{3,2,1,0:T(8,128)S(1)}, f32[8,1,128,128]{3,2,1,0:T(8,128)}, u32[]{:S(2)}) copy-start(f32[8,1,128,128]{3,2,1,0:T(8,128)} %edge_ref.3) | copy-start | bytes 1572868
  26.8 10.6 %all-to-all-start.1 = ((f32[8,64,128]{2,1,0:T(8,128)}), f32[8,64,128]{2,1,0:T(8,128)S(1)}, u32[]{:S(2)}, u32[]{:S(2)}) async-start(f32[8,64,128]{2,1,0:T(8,128)} %get-tuple-element.29), calls=%async_computation.1 | async-start | bytes 524288 | tf_op jit(solution)/shard_map/all_to_all | solution.py:422
  31.7 17.0 %copy-start.3 = (f32[256,128]{1,0:T(8,128)S(1)}, f32[256,128]{1,0:T(8,128)}, u32[]{:S(2)}) copy-start(f32[256,128]{1,0:T(8,128)} %get-tuple-element.36) | copy-start | bytes 393220
  31.7 26.4 %copy-start.1 = (f32[8,128,128]{2,1,0:T(8,128)S(1)}, f32[8,128,128]{2,1,0:T(8,128)}, u32[]{:S(2)}) copy-start(f32[8,128,128]{2,1,0:T(8,128)} %get-tuple-element.26.down_ref) | copy-start | bytes 1572868
  38.3 19.7 %all-to-all-start.2 = ((f32[8,32,128]{2,1,0:T(8,128)}), f32[8,32,128]{2,1,0:T(8,128)S(1)}, u32[]{:S(2)}, u32[]{:S(2)}) async-start(f32[8,32,128]{2,1,0:T(8,128)} %second.1), calls=%async_computation.2 | async-start | bytes 262144 | tf_op jit(solution)/shard_map/all_to_all | solution.py:447
  48.6 7.4 %collective-permute-start.1 = (f32[256,128]{1,0:T(8,128)S(1)}, f32[256,128]{1,0:T(8,128)S(1)}, u32[]{:S(2)}, u32[]{:S(2)}) collective-permute-start(f32[256,128]{1,0:T(8,128)S(1)} %copy-done.3), channel_id=1, source_target_pairs={{0,1},{1,0},{2,3},{3,2},{4,5},{5,4},{6,7},{7,6},{8,9},{9,8},{10,11... | collective-permute-start | bytes 393224 | tf_op jit(solution)/shard_map/ppermute | solution.py:354
  56.1 16.7 %copy-start.2 = (f32[256,128]{1,0:T(8,128)}, f32[256,128]{1,0:T(8,128)S(1)}, u32[]{:S(2)}) copy-start(f32[256,128]{1,0:T(8,128)S(1)} %collective-permute-done.1.refs_1_) | copy-start | bytes 393220

commit v7 on v5

--- a/solution.py
+++ b/solution.py
@@ -126,14 +126,24 @@
             near_out.send(out_row - step, 2 * step)
 
 
-def turn(left, matrix):
-    return jnp.where(left, matrix.T, matrix)
-
-
-def local_kernel(points_in, member_in, rhs_in, local_in, coupling_in, leaf_in, node_in, near_out, base_out):
-    near_field(near_out.ref.shape[0], points_in, member_in, rhs_in, near_out)
-    local_ref = local_in()
+def pair(level, matrix):
+    place = lax.axis_index("group") * 32 + lax.axis_index("dev")
+    return jnp.where(lax.rem(lax.shift_right_logical(place, level), 2) == 0, matrix.T, matrix)
+
+
+def tail_kernel(edge_in, link_in, local_in, coupling_in, leaf_in, node_in, down_out, base_out):
+    edge_ref, link_ref, local_ref = edge_in(), link_in(), local_in()
     rank = local_ref.shape[-1]
+    edge = [edge_ref[level, 0] for level in range(2)]
+    pair_matrix = [pair(level, link_ref[level, 0]) for level in range(2)]
+    leaf_path = []
+    for j in range(4):
+        leaf_path.append(mm3(local_ref[0, j], local_ref[0, 4 + j // 2]))
+    leaf_path = jnp.concatenate(leaf_path, axis=0)
+    down = [pair_matrix[0], mm3(pair_matrix[1], edge[0], True), mm3(edge[0], edge[1]).T]
+    down = mm3(jnp.concatenate(down, axis=0), leaf_path, True)
+    down_out.ref[: 3 * rank], down_out.ref[3 * rank :] = split(down)
+    down_out.send()
     leaf_ref, node_ref, coupling_ref = leaf_in(), node_in(), coupling_in()
     coupled = [mm3(node_ref[1], coupling_ref[0, 2], True), mm3(node_ref[0], coupling_ref[0, 2])]
     for j in range(2):
@@ -146,16 +156,12 @@
 
 
 def shadow_kernel(
-    edge_in, link_in, local_in, points_in, member_in, rhs_in, down_mid_out, down_out, near_out
+    edge_in, link_in, points_in, member_in, rhs_in, down_mid_out, near_out
 ):
-    edge_ref, link_ref, local_ref = edge_in(), link_in(), local_in()
+    edge_ref, link_ref = edge_in(), link_in()
     levels = link_ref.shape[0]
-    rank = edge_ref.shape[-1]
-    place = lax.axis_index("group") * 32 + lax.axis_index("dev")
     edge = [edge_ref[level, 0] for level in range(levels - 1)]
-    pair_matrix = [
-        turn(lax.rem(lax.shift_right_logical(place, level), 2) == 0, link_ref[level, 0]) for level in range(levels)
-    ]
+    pair_matrix = {level: pair(level, link_ref[level, 0]) for level in range(3, levels)}
     path = {4: edge[3]}
     for level in range(5, levels):
         path[level] = mm3(path[level - 1], edge[level - 1])
@@ -165,19 +171,6 @@
     down_mid_out.ref[6] = edge[2]
     down_mid_out.ref[7] = link_ref[2, 0]
     down_mid_out.send()
-    leaf_path = []
-    for j in range(4):
-        leaf_path.append(mm3(local_ref[0, j], local_ref[0, 4 + j // 2]))
-    leaf_path = jnp.concatenate(leaf_path, axis=0)
-    down = [
-        mm3(pair_matrix[0], leaf_path, True),
-        mm3(mm3(pair_matrix[1], edge[0], True), leaf_path, True),
-        mm3(mm3(edge[0], edge[1]).T, leaf_path, True),
-    ]
-    for k in range(3):
-        rows = slice(k * rank, (k + 1) * rank)
-        down_out.ref[rows], down_out.ref[3 * rank + k * rank : 4 * rank + k * rank] = split(down[k])
-    down_out.send()
     near_field(0, points_in, member_in, rhs_in, near_out)
 
 
@@ -397,16 +390,14 @@
 
     got_first = lax.all_to_all(shares, "dev", 0, 0, tiled=True, axis_index_groups=y_groups)
     got_edge = swap(edge_send, 7)
-    down_mid, down, near_low = call(
+    down_mid, near_low = call(
         shadow_kernel,
         [
             ((8, rank, rank), f32),
-            ((6 * rank, leaves * rank), bf16),
             ((count // 2, cols), f32),
         ],
         cross_transfer,
         cross_coupling,
-        local_transfer,
         points,
         member,
         rhs,
@@ -425,18 +416,14 @@
     )
 
     got_mid = lax.all_to_all(first_send, ("group", "dev"), 0, 0, tiled=True, axis_index_groups=mid_groups)
-    near_high, base = call(
-        local_kernel,
-        [((count // 2, cols), f32), ((cols, leaves * rank), f32)],
+    near_high = call(
+        functools.partial(near_field, count // 2),
+        [((count // 2, cols), f32)],
         points,
         member,
         rhs,
-        local_transfer,
-        local_coupling,
-        leaf_nodes,
-        nodes,
         flops=count * count * (cols + rank),
-        name="local",
+        name="near",
         after=[first_send],
     )
     second_send = small_call(
@@ -452,6 +439,20 @@
     got_top = lax.all_to_all(second_send, "group", 0, 0, tiled=True, axis_index_groups=z_groups)
     zero_send, _ = lax.optimization_barrier((zero_send, second_send))
     got_zero = swap(zero_send, 1)
+    down, base = call(
+        tail_kernel,
+        [((6 * rank, leaves * rank), bf16), ((cols, leaves * rank), f32)],
+        cross_transfer,
+        cross_coupling,
+        local_transfer,
+        local_coupling,
+        leaf_nodes,
+        nodes,
+        leads={0: (0, 2), 1: (0, 2)},
+        flops=2 * 80 * cols * block,
+        name="tail",
+        after=[second_send],
+    )
     third_send = small_call(
         third_kernel,
         [((8, 2 * slice_cols, rank), f32)],
@@ -462,7 +463,7 @@
         low_sums,
         flops=36 * slice_cols * block,
         name="third",
-        after=[got_zero],
+        after=[got_zero, base],
     )
     got_low = lax.all_to_all(third_send, "dev", 0, 0, tiled=True, axis_index_groups=y_groups)
     return call(

time: 77.4 us -> 77.5 us (level)
  waiting for transfers between devices: 6.55 us -> 4.73 us
  Pallas kernels: 24.7 us -> 26.5 us
    ppermute x2, waiting for transfers between devices: 3.54 us -> 0.13 us  [swap(): lax.ppermute(block, 'dev', [(i, i ^ stride) for i in range(lax.axis_size(...]
    pallas_call x4 -> x5, Pallas kernels: 22.1 us -> 23.9 us  [call(): pl.pallas_call(run, out_shape=shapes, in_specs=[pl.BlockSpec(memory_space...]
    all_to_all x1, waiting for transfers between devices: 0.92 us -> 1.73 us  [body(): lax.all_to_all(shares, 'dev', 0, 0, tiled=True, axis_index_groups=y_groups)]
    all_to_all x1, waiting for transfers between devices: 0.12 us -> 0.91 us  [body(): lax.all_to_all(first_send, ('group', 'dev'), 0, 0, tiled=True, axis_index...]
  transfers between devices with their start and end apart: 5 -> 5, of which waited for: 4 -> 4; matrix products, arithmetic and copies ran while one was open for 0% -> 0% of each run, Pallas kernels for 16% -> 18%
where the time goes in v7:
time: 77.5 us; the launch traced here: 76.9 us
  starting transfers between devices  31.3 us (40%)
  Pallas kernels  26.5 us (34%)
  blocking collectives  14.3 us (18%)
  waiting for transfers between devices  4.73 us (6%)
    pallas_call x5, Pallas kernels, call(): pl.pallas_call(run, out_shape=shapes, in_specs=[pl.BlockSpec(memory_space...  23.9 us
    all_to_all x1, blocking collectives, body(): lax.all_to_all(third_send, 'dev', 0, 0, tiled=True, axis_index_groups=y_g...  14.3 us
    all_to_all x1, starting transfers between devices, body(): lax.all_to_all(second_send, 'group', 0, 0, tiled=True, axis_index_groups=...  10.3 us
    ppermute x2, starting transfers between devices, swap(): lax.ppermute(block, 'dev', [(i, i ^ stride) for i in range(lax.axis_size(...  9.01 us
    all_to_all x1, starting transfers between devices, body(): lax.all_to_all(shares, 'dev', 0, 0, tiled=True, axis_index_groups=y_groups)  7.11 us
    all_to_all x1, starting transfers between devices, body(): lax.all_to_all(first_send, ('group', 'dev'), 0, 0, tiled=True, axis_index...  4.82 us
    pallas_call x3, Pallas kernels, small_call(): pl.pallas_call(kernel, out_shape=shapes, in_specs=[pl.BlockSpec(memory_sp...  2.6 us
    all_to_all x1, waiting for transfers between devices, body(): lax.all_to_all(second_send, 'group', 0, 0, tiled=True, axis_index_groups=...  1.97 us
  transfers between devices with their start and end apart: 5, of which 4 were waited for; matrix products, arithmetic and copies ran while one was open for 0% of the time, Pallas kernels for 18%

profile of v7, /device:TPU:2, one launch (start us, length us, event | category | flops | bytes accessed | tf_op | source)
XLA Modules:
  0.0 76.9 jit_solution(5777756323454004951)
XLA Ops:
  0.0 5.9 %rise.1 = (bf16[2048,512]{1,0:T(8,128)(2,1)}, bf16[2048,128]{1,0:T(8,128)(2,1)}, f32[256,512]{1,0:T(8,128)}, f32[2,256,128]{2,1,0:T(8,128)}, f32[256,128]{1,0:T(...) custom-call(s32[1,2048]{1,0:T(1,128)} %refs_0_.2, bf16[4,512,128]{2,1,0:T(8,128)(2,1)} %refs_1_.3, ...), custom_call_target="tpu_custom_call" | custom-call | flops 2147483648 | bytes 6365184 | tf_op jit(solution)/shard_map/rise/pallas_call | solution.py:318
  5.9 7.1 %all-to-all-start = ((f32[8,64,128]{2,1,0:T(8,128)}), f32[8,64,128]{2,1,0:T(8,128)S(1)}, u32[]{:S(2)}, u32[]{:S(2)}) async-start(f32[8,64,128]{2,1,0:T(8,128)} %get-tuple-element.24), calls=%async_computation | async-start | bytes 524288 | tf_op jit(solution)/shard_map/all_to_all | solution.py:391
  13.0 5.1 %collective-permute-start = (f32[128,128]{1,0:T(8,128)}, f32[128,128]{1,0:T(8,128)S(1)}, u32[]{:S(2)}, u32[]{:S(2)}) collective-permute-start(f32[128,128]{1,0:T(8,128)} %get-tuple-element.28), channel_id=1, source_target_pairs={{0,7},{1,6},{2,5},{3,4},{4,3},{5,2},{6,1},{7,0},{8,15},{9,14},{10,... | collective-permute-start | bytes 196616 | tf_op jit(solution)/shard_map/ppermute | solution.py:352
  18.1 0.0 copy-start
  18.1 5.7 %shadow.1 = (f32[8,128,128]{2,1,0:T(8,128)}, f32[1024,256]{1,0:T(8,128)}) custom-call(f32[8,1,128,128]{3,2,1,0:T(8,128)} %refs_0_.5, f32[9,1,128,128]{3,2,1,0:T(8,128)} %refs_1_.5, f32[8,2048]{1,0:T(8,128)} %refs_0_.4, bf16[2048,128]{1,0:T(8,128)(2,1)} %get-tuple-element.25.refs_3_.refs_1_, bf16[2048,256]{1,0:T(8,128)(2,1)} %refs_2_.6), custom_call_target="tpu_custom_call" | custom-call | flops 2030043136 | bytes 4325376 | tf_op jit(solution)/shard_map/shadow/pallas_call | solution.py:318
  23.8 1.7 %all-to-all-done.got_ref = f32[8,64,128]{2,1,0:T(8,128)S(1)} async-done(((f32[8,64,128]{2,1,0:T(8,128)}), f32[8,64,128]{2,1,0:T(8,128)S(1)}, u32[]{:S(2)}, u32[]{:S(2)}) %all-to-all-start) | async-done | bytes 262176 | tf_op jit(solution)/shard_map/all_to_all | solution.py:391
  25.6 0.0 collective-permute-done.other_ref
  25.6 0.0 copy-done
  25.6 1.3 %first.1 = (f32[8,64,128]{2,1,0:T(8,128)}, f32[6,32,128]{2,1,0:T(8,128)S(1)}) custom-call(f32[8,64,128]{2,1,0:T(8,128)S(1)} %all-to-all-done.got_ref, f32[8,1,128,128]{3,2,1,0:T(8,128)S(1)} %copy-done, f32[128,128]{1,0:T(8,128)S(1)} %collective-permute-done.other_ref), custom_call_target="tpu_custom_call" | custom-call | flops 9437184 | bytes 1212416 | tf_op jit(solution)/shard_map/first/pallas_call | solution.py:339
  26.8 4.8 %all-to-all-start.1 = ((f32[8,64,128]{2,1,0:T(8,128)}), f32[8,64,128]{2,1,0:T(8,128)S(1)}, u32[]{:S(2)}, u32[]{:S(2)}) async-start(f32[8,64,128]{2,1,0:T(8,128)} %get-tuple-element.29), calls=%async_computation.1 | async-start | bytes 524288 | tf_op jit(solution)/shard_map/all_to_all | solution.py:418
  31.7 0.0 copy-start.3
  31.7 4.8 %near.1.refs_6_ = f32[1024,256]{1,0:T(8,128)} custom-call(f32[8,2048]{1,0:T(8,128)} %refs_0_.4, bf16[2048,128]{1,0:T(8,128)(2,1)} %get-tuple-element.25.refs_3_.refs_1_, bf16[2048,256]{1,0:T(8,128)(2,1)} %refs_2_.6), custom_call_target="tpu_custom_call" | custom-call | flops 1610612736 | bytes 2686976 | tf_op jit(solution)/shard_map/near/pallas_call | solution.py:318
  36.5 0.0 copy-start.1
  36.5 0.9 %all-to-all-done.1.got_ref.got_mid_ref = f32[8,64,128]{2,1,0:T(8,128)S(1)} async-done(((f32[8,64,128]{2,1,0:T(8,128)}), f32[8,64,128]{2,1,0:T(8,128)S(1)}, u32[]{:S(2)}, u32[]{:S(2)}) %all-to-all-start.1) | async-done | bytes 262176 | tf_op jit(solution)/shard_map/all_to_all | solution.py:418
  37.4 0.9 %second.1 = f32[8,32,128]{2,1,0:T(8,128)} custom-call(f32[8,64,128]{2,1,0:T(8,128)S(1)} %all-to-all-done.1.got_ref.got_mid_ref, f32[8,1,128,128]{3,2,1,0:T(8,128)S(1)} %copy-done), custom_call_target="tpu_custom_call" | custom-call | flops 6291456 | bytes 917504 | tf_op jit(solution)/shard_map/second/pallas_call | solution.py:339
  38.3 10.3 %all-to-all-start.2 = ((f32[8,32,128]{2,1,0:T(8,128)}), f32[8,32,128]{2,1,0:T(8,128)S(1)}, u32[]{:S(2)}, u32[]{:S(2)}) async-start(f32[8,32,128]{2,1,0:T(8,128)} %second.1), calls=%async_computation.2 | async-start | bytes 262144 | tf_op jit(solution)/shard_map/all_to_all | solution.py:439
  48.6 0.0 copy-done.3
  48.6 3.9 %collective-permute-start.1 = (f32[256,128]{1,0:T(8,128)S(1)}, f32[256,128]{1,0:T(8,128)S(1)}, u32[]{:S(2)}, u32[]{:S(2)}) collective-permute-start(f32[256,128]{1,0:T(8,128)S(1)} %copy-done.3), channel_id=1, source_target_pairs={{0,1},{1,0},{2,3},{3,2},{4,5},{5,4},{6,7},{7,6},{8,9},{9,8},{10,11... | collective-permute-start | bytes 393224 | tf_op jit(solution)/shard_map/ppermute | solution.py:352
  52.5 3.4 %tail.1 = (bf16[768,512]{1,0:T(8,128)(2,1)}, f32[256,512]{1,0:T(8,128)}) custom-call(f32[8,1,128,128]{3,2,1,0:T(8,128)} %refs_0_.5, f32[9,1,128,128]{3,2,1,0:T(8,128)} %refs_1_.5, f32[1,6,128,128]{3,2,1,0:T(8,128)} %refs_2_.7, f32[1,3,128,128]{3,2,1,0:T(8,128)} %refs_3_.3, f32[256,512]{1,0:T(8,128)} %get-tuple-element.35.refs_4_, ...), custom_call_target="tpu_custom_call" | custom-call | flops 671088640 | bytes 3801088 | tf_op jit(solution)/shard_map/tail/pallas_call | solution.py:318
  55.9 0.1 collective-permute-done.1.refs_1_
  56.0 0.0 copy-start.2
  56.0 2.0 %all-to-all-done.2.got_ref = f32[8,32,128]{2,1,0:T(8,128)S(1)} async-done(((f32[8,32,128]{2,1,0:T(8,128)}), f32[8,32,128]{2,1,0:T(8,128)S(1)}, u32[]{:S(2)}, u32[]{:S(2)}) %all-to-all-start.2) | async-done | bytes 131104 | tf_op jit(solution)/shard_map/all_to_all | solution.py:439
  58.0 0.0 copy-done.1
  58.0 0.4 third.1
  58.5 14.3 %all_to_all.20.refs_0_ = f32[8,64,128]{2,1,0:T(8,128)} all-to-all(f32[8,64,128]{2,1,0:T(8,128)S(1)} %third.1), channel_id=1, replica_groups={{0,1,2,3,4,5,6,7},{8,9,10,11,12,13,14,15},{16,17,18,19,20,21,22,23},{24..., dimensions={0} | all-to-all | bytes 524288 | tf_op jit(solution)/shard_map/all_to_all | solution.py:468
  72.8 0.0 copy-done.2
  72.8 4.1 %fall.1 = bf16[2048,256]{1,0:T(8,128)(2,1)} custom-call(f32[8,64,128]{2,1,0:T(8,128)} %all_to_all.20.refs_0_, f32[256,128]{1,0:T(8,128)} %copy-done.2, bf16[768,512]{1,0:T(8,128)(2,1)} %get-tuple-element.40.refs_2_, f32[256,512]{1,0:T(8,128)} %get-tuple-element.37.refs_3_, bf16[2048,512]{1,0:T(8,128)(2,1)} %get-tuple-element.41.refs_4_, ...), custom_call_target="tpu_custom_call" | custom-call | flops 536870912 | bytes 6946816 | tf_op jit(solution)/shard_map/fall/pallas_call | solution.py:318
Async XLA Ops:
  5.9 19.7 %all-to-all-start = ((f32[8,64,128]{2,1,0:T(8,128)}), f32[8,64,128]{2,1,0:T(8,128)S(1)}, u32[]{:S(2)}, u32[]{:S(2)}) async-start(f32[8,64,128]{2,1,0:T(8,128)} %get-tuple-element.24), calls=%async_computation | async-start | bytes 524288 | tf_op jit(solution)/shard_map/all_to_all | solution.py:391
  13.0 12.6 %collective-permute-start = (f32[128,128]{1,0:T(8,128)}, f32[128,128]{1,0:T(8,128)S(1)}, u32[]{:S(2)}, u32[]{:S(2)}) collective-permute-start(f32[128,128]{1,0:T(8,128)} %get-tuple-element.28), channel_id=1, source_target_pairs={{0,7},{1,6},{2,5},{3,4},{4,3},{5,2},{6,1},{7,0},{8,15},{9,14},{10,... | collective-permute-start | bytes 196616 | tf_op jit(solution)/shard_map/ppermute | solution.py:352
  18.1 7.5 %copy-start = (f32[8,1,128,128]{3,2,1,0:T(8,128)S(1)}, f32[8,1,128,128]{3,2,1,0:T(8,128)}, u32[]{:S(2)}) copy-start(f32[8,1,128,128]{3,2,1,0:T(8,128)} %refs_0_.5) | copy-start | bytes 1572868
  26.8 10.6 %all-to-all-start.1 = ((f32[8,64,128]{2,1,0:T(8,128)}), f32[8,64,128]{2,1,0:T(8,128)S(1)}, u32[]{:S(2)}, u32[]{:S(2)}) async-start(f32[8,64,128]{2,1,0:T(8,128)} %get-tuple-element.29), calls=%async_computation.1 | async-start | bytes 524288 | tf_op jit(solution)/shard_map/all_to_all | solution.py:418
  31.7 17.0 %copy-start.3 = (f32[256,128]{1,0:T(8,128)S(1)}, f32[256,128]{1,0:T(8,128)}, u32[]{:S(2)}) copy-start(f32[256,128]{1,0:T(8,128)} %get-tuple-element.33) | copy-start | bytes 393220
  36.5 21.6 %copy-start.1 = (f32[8,128,128]{2,1,0:T(8,128)S(1)}, f32[8,128,128]{2,1,0:T(8,128)}, u32[]{:S(2)}) copy-start(f32[8,128,128]{2,1,0:T(8,128)} %get-tuple-element.26.down_ref) | copy-start | bytes 1572868
  38.3 19.7 %all-to-all-start.2 = ((f32[8,32,128]{2,1,0:T(8,128)}), f32[8,32,128]{2,1,0:T(8,128)S(1)}, u32[]{:S(2)}, u32[]{:S(2)}) async-start(f32[8,32,128]{2,1,0:T(8,128)} %second.1), calls=%async_computation.2 | async-start | bytes 262144 | tf_op jit(solution)/shard_map/all_to_all | solution.py:439
  48.6 7.4 %collective-permute-start.1 = (f32[256,128]{1,0:T(8,128)S(1)}, f32[256,128]{1,0:T(8,128)S(1)}, u32[]{:S(2)}, u32[]{:S(2)}) collective-permute-start(f32[256,128]{1,0:T(8,128)S(1)} %copy-done.3), channel_id=1, source_target_pairs={{0,1},{1,0},{2,3},{3,2},{4,5},{5,4},{6,7},{7,6},{8,9},{9,8},{10,11... | collective-permute-start | bytes 393224 | tf_op jit(solution)/shard_map/ppermute | solution.py:352
  56.0 16.7 %copy-start.2 = (f32[256,128]{1,0:T(8,128)}, f32[256,128]{1,0:T(8,128)S(1)}, u32[]{:S(2)}) copy-start(f32[256,128]{1,0:T(8,128)S(1)} %collective-permute-done.1.refs_1_) | copy-start | bytes 393220
